TPU v7x, 256 devices: a whole 4x4x8 slice. The times are simulated.
256 devices in a mesh: seq: 32 (over y, z), head: 4 (over x_hi, core), rep: 2 (over x_lo).
Axes of the slice: x: 4 (x_hi: 2, x_lo: 2; x = x_hi * 2 + x_lo), y: 4, z: 8, core: 2. Of those that a mesh axis runs over, the one named last changes fastest.
Arguments:
- queries: bfloat16 [32768, 512], P(('rep', 'seq'), 'head'), parts along dimension 0, may hold values from -6 to 6
- keys: bfloat16 [32768, 512], P(('rep', 'seq'), 'head'), parts along dimension 0, may hold values from -6 to 6
- values: bfloat16 [32768, 512], P(('rep', 'seq'), 'head'), parts along dimension 0, may hold values from -6 to 6
- out_grad: bfloat16 [32768, 512], P(('rep', 'seq'), 'head'), parts along dimension 0, may hold values from -6 to 6
- block_mask: int32 [128, 128], replicated, may hold values 0 or 1
- block_order: int32 [128], replicated, may hold values from 0 to 127, each once
Outputs:
- query_grad: float32 [32768, 512], P(('rep', 'seq'), 'head'), parts along dimension 0
- key_grad: float32 [32768, 512], P(('rep', 'seq'), 'head'), parts along dimension 0
- value_grad: float32 [32768, 512], P(('rep', 'seq'), 'head'), parts along dimension 0
There are 2 independent parts, one for each index of `rep`. A program takes and returns all parts, laid end to end along the dimension named above; an argument that names none is the same for every part. Nothing has to cross between parts.
Inputs may be any that keep to these rules, and one draw needn't show every extreme that they name: `block_order`: a permutation of the 128 blocks.
All inputs are finite; a program needn't handle non-finite values.
Results may differ from a plain program's by a relative error of at most 0.0029.
Values may be sent and summed in bfloat16 or wider, within the bound.
No kernel may reach another device: no remote copies, remote signals or barrier semaphores. Data moves between devices by JAX's collectives and lax.ppermute only.
A program may use at most 64 MiB of HBM per device.

v0:
```python
import jax
import jax.numpy as jnp
from jax import lax
from jax.sharding import PartitionSpec as P

BLK = 128


def shifted(block, axis, distance):
    devices = range(lax.axis_size(axis))
    route = [((i - distance) % len(devices), i) for i in devices]
    return lax.ppermute(block, axis, route)


def block_positions(block_order, first_block, nblk):
    blocks = lax.dynamic_slice_in_dim(block_order, first_block, nblk, 0)
    offsets = jnp.arange(nblk * BLK, dtype=jnp.int32) % BLK
    return (blocks, jnp.repeat(blocks, BLK) * BLK + offsets)


def local_rates(block_mask, blocks, pos):
    total = block_mask.shape[0]
    ids = jnp.arange(total, dtype=jnp.int32)
    below = jnp.sum(block_mask * (ids[None, :] < ids[:, None]).astype(jnp.int32), axis=1)
    diag = jnp.sum(block_mask * (ids[None, :] == ids[:, None]).astype(jnp.int32), axis=1)
    row_block = jnp.repeat(blocks, BLK)
    count = BLK * below[row_block] + diag[row_block] * (pos % BLK + 1)
    return 1.0 / jnp.sqrt(jnp.maximum(count, 1).astype(jnp.float32))


def pair_grads(
    queries, out_grad, rates, q_blocks, q_pos, key_piece, value_piece, k_blocks, k_pos, block_mask
):
    scale = queries.shape[1] ** (-0.5)
    small = block_mask[q_blocks][:, k_blocks]
    live = (jnp.repeat(jnp.repeat(small, BLK, 0), BLK, 1) > 0) & (k_pos[None, :] <= q_pos[:, None])
    scores = jnp.dot(queries, key_piece.T, preferred_element_type=jnp.float32) * scale
    sig = jax.nn.sigmoid(scores)
    d_weights = jnp.dot(out_grad, value_piece.T, preferred_element_type=jnp.float32)
    d_scores = jnp.where(
        live, d_weights * rates[:, None] * (sig * (1.0 + scores * (1.0 - sig))), 0.0
    ).astype(jnp.bfloat16)
    result = []
    result.append(jnp.dot(d_scores, key_piece, preferred_element_type=jnp.float32) * scale)
    weights = jnp.where(live, scores * sig * rates[:, None], 0.0).astype(jnp.bfloat16)
    k_part = (
        lax.dot_general(
            d_scores, queries, (((0,), (0,)), ((), ())), preferred_element_type=jnp.float32
        )
        * scale
    )
    v_part = lax.dot_general(
        weights, out_grad, (((0,), (0,)), ((), ())), preferred_element_type=jnp.float32
    )
    result.append(jnp.stack((k_part, v_part)))
    return tuple(result)


def on_device(queries, keys, values, out_grad, block_mask, block_order):
    rows, width = queries.shape
    nblk = rows // BLK
    devices = lax.axis_size("seq")
    me = lax.axis_index("seq")
    q_blocks, q_pos = block_positions(block_order, me * nblk, nblk)
    rates = local_rates(block_mask, q_blocks, q_pos)
    paired = jnp.stack((keys, values))

    def step(turn, carry):
        key_vals, q_acc, kv_acc = carry
        source = (me - turn) % devices
        k_blocks, k_pos = block_positions(block_order, source * nblk, nblk)
        q_part, kv_part = pair_grads(
            queries,
            out_grad,
            rates,
            q_blocks,
            q_pos,
            key_vals[0],
            key_vals[1],
            k_blocks,
            k_pos,
            block_mask,
        )
        kv_acc = kv_acc + kv_part
        key_vals = shifted(key_vals, "seq", 1)
        kv_acc = shifted(kv_acc, "seq", 1)
        return (key_vals, q_acc + q_part, kv_acc)

    start_carry = (
        paired,
        jnp.zeros((rows, width), jnp.float32),
        jnp.zeros((2, rows, width), jnp.float32),
    )
    _, query_grad, grads = lax.fori_loop(0, devices, step, start_carry)
    return (query_grad, grads[0], grads[1])


def solution(mesh):
    placed = (
        P(("rep", "seq"), "head"),
        P(("rep", "seq"), "head"),
        P(("rep", "seq"), "head"),
        P(("rep", "seq"), "head"),
        P(),
        P(),
    )
    return jax.shard_map(
        on_device,
        mesh=mesh,
        in_specs=placed,
        out_specs=(P(("rep", "seq"), "head"), P(("rep", "seq"), "head"), P(("rep", "seq"), "head")),
        check_vma=False,
    )
```

profile of v0, /device:TPU:2, one launch (start us, length us, event | category | flops | bytes accessed | tf_op | source)
XLA Modules:
  0.0 765.0 jit_solution(3649399453531097410)
XLA Ops:
  2.4 3.3 gather_fusion.2
  5.8 3.3 gather_fusion.3
  11.8 752.3 %while.22 = (s32[]{:T(128)}, bf16[2,512,128]{2,1,0:T(8,128)(2,1)S(1)}, f32[512,128]{1,0:T(8,128)S(1)}, f32[2,512,128]{2,1,0:T(8,128)S(1)}, s32[]{:T(128)}, /*ind...) while((s32[]{:T(128)}, ...), condition=%wide.region_3.4_spmd.clone, body=%wide.region_2.3_spmd.clone.sunk | while | flops 342106144 | bytes 12739346 | solution.py:94
  13.1 1.6 broadcast_in_dim.122
  16.5 2.0 collective-permute-start.1
  18.5 1.9 collective-permute-start
  20.7 21.7 %collective-permute-done = bf16[2,512,128]{2,1,0:T(8,128)(2,1)S(1)} collective-permute-done((bf16[2,512,128]{2,1,0:T(8,128)(2,1)S(1)}, bf16[2,512,128]{2,1,0:T(8,128)(2,1)S(1)}, u32[]{:S(2)}, u32[]{:S(2)}) %collective-permute-start) | collective-permute-done | bytes 262176 | tf_op jit(solution)/shard_map/while/body/eval_jaxpr/ppermute | solution.py:12
  43.7 1.6 broadcast_in_dim.122
  47.6 21.6 %collective-permute-done = bf16[2,512,128]{2,1,0:T(8,128)(2,1)S(1)} collective-permute-done((bf16[2,512,128]{2,1,0:T(8,128)(2,1)S(1)}, bf16[2,512,128]{2,1,0:T(8,128)(2,1)S(1)}, u32[]{:S(2)}, u32[]{:S(2)}) %collective-permute-start) | collective-permute-done | bytes 262176 | tf_op jit(solution)/shard_map/while/body/eval_jaxpr/ppermute | solution.py:12
  70.5 1.6 broadcast_in_dim.122
  74.4 20.7 %collective-permute-done = bf16[2,512,128]{2,1,0:T(8,128)(2,1)S(1)} collective-permute-done((bf16[2,512,128]{2,1,0:T(8,128)(2,1)S(1)}, bf16[2,512,128]{2,1,0:T(8,128)(2,1)S(1)}, u32[]{:S(2)}, u32[]{:S(2)}) %collective-permute-start) | collective-permute-done | bytes 262176 | tf_op jit(solution)/shard_map/while/body/eval_jaxpr/ppermute | solution.py:12
  96.4 1.6 broadcast_in_dim.122
  100.3 19.8 %collective-permute-done = bf16[2,512,128]{2,1,0:T(8,128)(2,1)S(1)} collective-permute-done((bf16[2,512,128]{2,1,0:T(8,128)(2,1)S(1)}, bf16[2,512,128]{2,1,0:T(8,128)(2,1)S(1)}, u32[]{:S(2)}, u32[]{:S(2)}) %collective-permute-start) | collective-permute-done | bytes 262176 | tf_op jit(solution)/shard_map/while/body/eval_jaxpr/ppermute | solution.py:12
  121.3 1.6 broadcast_in_dim.122
  125.3 18.8 %collective-permute-done = bf16[2,512,128]{2,1,0:T(8,128)(2,1)S(1)} collective-permute-done((bf16[2,512,128]{2,1,0:T(8,128)(2,1)S(1)}, bf16[2,512,128]{2,1,0:T(8,128)(2,1)S(1)}, u32[]{:S(2)}, u32[]{:S(2)}) %collective-permute-start) | collective-permute-done | bytes 262176 | tf_op jit(solution)/shard_map/while/body/eval_jaxpr/ppermute | solution.py:12
  145.4 1.6 broadcast_in_dim.122
  149.3 17.9 %collective-permute-done = bf16[2,512,128]{2,1,0:T(8,128)(2,1)S(1)} collective-permute-done((bf16[2,512,128]{2,1,0:T(8,128)(2,1)S(1)}, bf16[2,512,128]{2,1,0:T(8,128)(2,1)S(1)}, u32[]{:S(2)}, u32[]{:S(2)}) %collective-permute-start) | collective-permute-done | bytes 262176 | tf_op jit(solution)/shard_map/while/body/eval_jaxpr/ppermute | solution.py:12
  168.5 1.6 broadcast_in_dim.122
  172.4 17.0 %collective-permute-done = bf16[2,512,128]{2,1,0:T(8,128)(2,1)S(1)} collective-permute-done((bf16[2,512,128]{2,1,0:T(8,128)(2,1)S(1)}, bf16[2,512,128]{2,1,0:T(8,128)(2,1)S(1)}, u32[]{:S(2)}, u32[]{:S(2)}) %collective-permute-start) | collective-permute-done | bytes 262176 | tf_op jit(solution)/shard_map/while/body/eval_jaxpr/ppermute | solution.py:12
  190.7 1.6 broadcast_in_dim.122
  194.6 16.1 %collective-permute-done = bf16[2,512,128]{2,1,0:T(8,128)(2,1)S(1)} collective-permute-done((bf16[2,512,128]{2,1,0:T(8,128)(2,1)S(1)}, bf16[2,512,128]{2,1,0:T(8,128)(2,1)S(1)}, u32[]{:S(2)}, u32[]{:S(2)}) %collective-permute-start) | collective-permute-done | bytes 262176 | tf_op jit(solution)/shard_map/while/body/eval_jaxpr/ppermute | solution.py:12
  212.0 1.6 broadcast_in_dim.122
  215.9 15.1 %collective-permute-done = bf16[2,512,128]{2,1,0:T(8,128)(2,1)S(1)} collective-permute-done((bf16[2,512,128]{2,1,0:T(8,128)(2,1)S(1)}, bf16[2,512,128]{2,1,0:T(8,128)(2,1)S(1)}, u32[]{:S(2)}, u32[]{:S(2)}) %collective-permute-start) | collective-permute-done | bytes 262176 | tf_op jit(solution)/shard_map/while/body/eval_jaxpr/ppermute | solution.py:12
  232.3 1.6 broadcast_in_dim.122
  236.3 14.9 %collective-permute-done = bf16[2,512,128]{2,1,0:T(8,128)(2,1)S(1)} collective-permute-done((bf16[2,512,128]{2,1,0:T(8,128)(2,1)S(1)}, bf16[2,512,128]{2,1,0:T(8,128)(2,1)S(1)}, u32[]{:S(2)}, u32[]{:S(2)}) %collective-permute-start) | collective-permute-done | bytes 262176 | tf_op jit(solution)/shard_map/while/body/eval_jaxpr/ppermute | solution.py:12
  252.4 1.6 broadcast_in_dim.122
  256.3 14.9 %collective-permute-done = bf16[2,512,128]{2,1,0:T(8,128)(2,1)S(1)} collective-permute-done((bf16[2,512,128]{2,1,0:T(8,128)(2,1)S(1)}, bf16[2,512,128]{2,1,0:T(8,128)(2,1)S(1)}, u32[]{:S(2)}, u32[]{:S(2)}) %collective-permute-start) | collective-permute-done | bytes 262176 | tf_op jit(solution)/shard_map/while/body/eval_jaxpr/ppermute | solution.py:12
  272.4 1.6 broadcast_in_dim.122
  276.4 15.7 %collective-permute-done = bf16[2,512,128]{2,1,0:T(8,128)(2,1)S(1)} collective-permute-done((bf16[2,512,128]{2,1,0:T(8,128)(2,1)S(1)}, bf16[2,512,128]{2,1,0:T(8,128)(2,1)S(1)}, u32[]{:S(2)}, u32[]{:S(2)}) %collective-permute-start) | collective-permute-done | bytes 262176 | tf_op jit(solution)/shard_map/while/body/eval_jaxpr/ppermute | solution.py:12
  293.3 1.6 broadcast_in_dim.122
  297.3 16.7 %collective-permute-done = bf16[2,512,128]{2,1,0:T(8,128)(2,1)S(1)} collective-permute-done((bf16[2,512,128]{2,1,0:T(8,128)(2,1)S(1)}, bf16[2,512,128]{2,1,0:T(8,128)(2,1)S(1)}, u32[]{:S(2)}, u32[]{:S(2)}) %collective-permute-start) | collective-permute-done | bytes 262176 | tf_op jit(solution)/shard_map/while/body/eval_jaxpr/ppermute | solution.py:12
  315.3 1.6 broadcast_in_dim.122
  319.2 17.8 %collective-permute-done = bf16[2,512,128]{2,1,0:T(8,128)(2,1)S(1)} collective-permute-done((bf16[2,512,128]{2,1,0:T(8,128)(2,1)S(1)}, bf16[2,512,128]{2,1,0:T(8,128)(2,1)S(1)}, u32[]{:S(2)}, u32[]{:S(2)}) %collective-permute-start) | collective-permute-done | bytes 262176 | tf_op jit(solution)/shard_map/while/body/eval_jaxpr/ppermute | solution.py:12
  338.3 1.6 broadcast_in_dim.122
  342.3 18.9 %collective-permute-done = bf16[2,512,128]{2,1,0:T(8,128)(2,1)S(1)} collective-permute-done((bf16[2,512,128]{2,1,0:T(8,128)(2,1)S(1)}, bf16[2,512,128]{2,1,0:T(8,128)(2,1)S(1)}, u32[]{:S(2)}, u32[]{:S(2)}) %collective-permute-start) | collective-permute-done | bytes 262176 | tf_op jit(solution)/shard_map/while/body/eval_jaxpr/ppermute | solution.py:12
  362.4 1.6 broadcast_in_dim.122
  366.4 20.0 %collective-permute-done = bf16[2,512,128]{2,1,0:T(8,128)(2,1)S(1)} collective-permute-done((bf16[2,512,128]{2,1,0:T(8,128)(2,1)S(1)}, bf16[2,512,128]{2,1,0:T(8,128)(2,1)S(1)}, u32[]{:S(2)}, u32[]{:S(2)}) %collective-permute-start) | collective-permute-done | bytes 262176 | tf_op jit(solution)/shard_map/while/body/eval_jaxpr/ppermute | solution.py:12
  387.6 1.6 broadcast_in_dim.122
  391.6 21.1 %collective-permute-done = bf16[2,512,128]{2,1,0:T(8,128)(2,1)S(1)} collective-permute-done((bf16[2,512,128]{2,1,0:T(8,128)(2,1)S(1)}, bf16[2,512,128]{2,1,0:T(8,128)(2,1)S(1)}, u32[]{:S(2)}, u32[]{:S(2)}) %collective-permute-start) | collective-permute-done | bytes 262176 | tf_op jit(solution)/shard_map/while/body/eval_jaxpr/ppermute | solution.py:12
  413.9 1.6 broadcast_in_dim.122
  417.9 22.2 %collective-permute-done = bf16[2,512,128]{2,1,0:T(8,128)(2,1)S(1)} collective-permute-done((bf16[2,512,128]{2,1,0:T(8,128)(2,1)S(1)}, bf16[2,512,128]{2,1,0:T(8,128)(2,1)S(1)}, u32[]{:S(2)}, u32[]{:S(2)}) %collective-permute-start) | collective-permute-done | bytes 262176 | tf_op jit(solution)/shard_map/while/body/eval_jaxpr/ppermute | solution.py:12
  441.4 1.6 broadcast_in_dim.122
  445.3 23.2 %collective-permute-done = bf16[2,512,128]{2,1,0:T(8,128)(2,1)S(1)} collective-permute-done((bf16[2,512,128]{2,1,0:T(8,128)(2,1)S(1)}, bf16[2,512,128]{2,1,0:T(8,128)(2,1)S(1)}, u32[]{:S(2)}, u32[]{:S(2)}) %collective-permute-start) | collective-permute-done | bytes 262176 | tf_op jit(solution)/shard_map/while/body/eval_jaxpr/ppermute | solution.py:12
  469.8 1.6 broadcast_in_dim.122
  473.7 22.3 %collective-permute-done = bf16[2,512,128]{2,1,0:T(8,128)(2,1)S(1)} collective-permute-done((bf16[2,512,128]{2,1,0:T(8,128)(2,1)S(1)}, bf16[2,512,128]{2,1,0:T(8,128)(2,1)S(1)}, u32[]{:S(2)}, u32[]{:S(2)}) %collective-permute-start) | collective-permute-done | bytes 262176 | tf_op jit(solution)/shard_map/while/body/eval_jaxpr/ppermute | solution.py:12
  497.3 1.6 broadcast_in_dim.122
  501.3 21.5 %collective-permute-done = bf16[2,512,128]{2,1,0:T(8,128)(2,1)S(1)} collective-permute-done((bf16[2,512,128]{2,1,0:T(8,128)(2,1)S(1)}, bf16[2,512,128]{2,1,0:T(8,128)(2,1)S(1)}, u32[]{:S(2)}, u32[]{:S(2)}) %collective-permute-start) | collective-permute-done | bytes 262176 | tf_op jit(solution)/shard_map/while/body/eval_jaxpr/ppermute | solution.py:12
  524.0 1.6 broadcast_in_dim.122
  528.0 20.6 %collective-permute-done = bf16[2,512,128]{2,1,0:T(8,128)(2,1)S(1)} collective-permute-done((bf16[2,512,128]{2,1,0:T(8,128)(2,1)S(1)}, bf16[2,512,128]{2,1,0:T(8,128)(2,1)S(1)}, u32[]{:S(2)}, u32[]{:S(2)}) %collective-permute-start) | collective-permute-done | bytes 262176 | tf_op jit(solution)/shard_map/while/body/eval_jaxpr/ppermute | solution.py:12
  549.8 1.6 broadcast_in_dim.122
  553.8 19.7 %collective-permute-done = bf16[2,512,128]{2,1,0:T(8,128)(2,1)S(1)} collective-permute-done((bf16[2,512,128]{2,1,0:T(8,128)(2,1)S(1)}, bf16[2,512,128]{2,1,0:T(8,128)(2,1)S(1)}, u32[]{:S(2)}, u32[]{:S(2)}) %collective-permute-start) | collective-permute-done | bytes 262176 | tf_op jit(solution)/shard_map/while/body/eval_jaxpr/ppermute | solution.py:12
  574.7 1.6 broadcast_in_dim.122
  578.6 18.7 %collective-permute-done = bf16[2,512,128]{2,1,0:T(8,128)(2,1)S(1)} collective-permute-done((bf16[2,512,128]{2,1,0:T(8,128)(2,1)S(1)}, bf16[2,512,128]{2,1,0:T(8,128)(2,1)S(1)}, u32[]{:S(2)}, u32[]{:S(2)}) %collective-permute-start) | collective-permute-done | bytes 262176 | tf_op jit(solution)/shard_map/while/body/eval_jaxpr/ppermute | solution.py:12
  602.6 17.8 %collective-permute-done = bf16[2,512,128]{2,1,0:T(8,128)(2,1)S(1)} collective-permute-done((bf16[2,512,128]{2,1,0:T(8,128)(2,1)S(1)}, bf16[2,512,128]{2,1,0:T(8,128)(2,1)S(1)}, u32[]{:S(2)}, u32[]{:S(2)}) %collective-permute-start) | collective-permute-done | bytes 262176 | tf_op jit(solution)/shard_map/while/body/eval_jaxpr/ppermute | solution.py:12
  621.6 1.6 broadcast_in_dim.122
  625.6 16.9 %collective-permute-done = bf16[2,512,128]{2,1,0:T(8,128)(2,1)S(1)} collective-permute-done((bf16[2,512,128]{2,1,0:T(8,128)(2,1)S(1)}, bf16[2,512,128]{2,1,0:T(8,128)(2,1)S(1)}, u32[]{:S(2)}, u32[]{:S(2)}) %collective-permute-start) | collective-permute-done | bytes 262176 | tf_op jit(solution)/shard_map/while/body/eval_jaxpr/ppermute | solution.py:12
  647.7 16.0 %collective-permute-done = bf16[2,512,128]{2,1,0:T(8,128)(2,1)S(1)} collective-permute-done((bf16[2,512,128]{2,1,0:T(8,128)(2,1)S(1)}, bf16[2,512,128]{2,1,0:T(8,128)(2,1)S(1)}, u32[]{:S(2)}, u32[]{:S(2)}) %collective-permute-start) | collective-permute-done | bytes 262176 | tf_op jit(solution)/shard_map/while/body/eval_jaxpr/ppermute | solution.py:12
  668.8 15.0 %collective-permute-done = bf16[2,512,128]{2,1,0:T(8,128)(2,1)S(1)} collective-permute-done((bf16[2,512,128]{2,1,0:T(8,128)(2,1)S(1)}, bf16[2,512,128]{2,1,0:T(8,128)(2,1)S(1)}, u32[]{:S(2)}, u32[]{:S(2)}) %collective-permute-start) | collective-permute-done | bytes 262176 | tf_op jit(solution)/shard_map/while/body/eval_jaxpr/ppermute | solution.py:12
  685.1 1.6 broadcast_in_dim.122
  689.1 14.9 %collective-permute-done = bf16[2,512,128]{2,1,0:T(8,128)(2,1)S(1)} collective-permute-done((bf16[2,512,128]{2,1,0:T(8,128)(2,1)S(1)}, bf16[2,512,128]{2,1,0:T(8,128)(2,1)S(1)}, u32[]{:S(2)}, u32[]{:S(2)}) %collective-permute-start) | collective-permute-done | bytes 262176 | tf_op jit(solution)/shard_map/while/body/eval_jaxpr/ppermute | solution.py:12
  709.1 14.9 %collective-permute-done = bf16[2,512,128]{2,1,0:T(8,128)(2,1)S(1)} collective-permute-done((bf16[2,512,128]{2,1,0:T(8,128)(2,1)S(1)}, bf16[2,512,128]{2,1,0:T(8,128)(2,1)S(1)}, u32[]{:S(2)}, u32[]{:S(2)}) %collective-permute-start) | collective-permute-done | bytes 262176 | tf_op jit(solution)/shard_map/while/body/eval_jaxpr/ppermute | solution.py:12
  725.3 1.6 broadcast_in_dim.122
  729.2 14.9 %collective-permute-done = bf16[2,512,128]{2,1,0:T(8,128)(2,1)S(1)} collective-permute-done((bf16[2,512,128]{2,1,0:T(8,128)(2,1)S(1)}, bf16[2,512,128]{2,1,0:T(8,128)(2,1)S(1)}, u32[]{:S(2)}, u32[]{:S(2)}) %collective-permute-start) | collective-permute-done | bytes 262176 | tf_op jit(solution)/shard_map/while/body/eval_jaxpr/ppermute | solution.py:12
  749.3 14.9 %collective-permute-done = bf16[2,512,128]{2,1,0:T(8,128)(2,1)S(1)} collective-permute-done((bf16[2,512,128]{2,1,0:T(8,128)(2,1)S(1)}, bf16[2,512,128]{2,1,0:T(8,128)(2,1)S(1)}, u32[]{:S(2)}, u32[]{:S(2)}) %collective-permute-start) | collective-permute-done | bytes 262176 | tf_op jit(solution)/shard_map/while/body/eval_jaxpr/ppermute | solution.py:12
  (605 shorter events, 125.8 us)
Async XLA Ops:
  16.5 25.9 %collective-permute-start.1 = (f32[2,512,128]{2,1,0:T(8,128)S(1)}, f32[2,512,128]{2,1,0:T(8,128)S(1)}, u32[]{:S(2)}, u32[]{:S(2)}) collective-permute-start(f32[2,512,128]{2,1,0:T(8,128)S(1)} %maximum_add_fusion.2), channel_id=1, source_target_pairs={{248,0},{0,8},{8,16},{16,24},{24,32},{32,40},{40,48},{48,56},{56,6... | collective-permute-start | bytes 1572872 | tf_op jit(solution)/shard_map/while/body/eval_jaxpr/ppermute | solution.py:12
  18.5 23.9 %collective-permute-start = (bf16[2,512,128]{2,1,0:T(8,128)(2,1)S(1)}, bf16[2,512,128]{2,1,0:T(8,128)(2,1)S(1)}, u32[]{:S(2)}, u32[]{:S(2)}) collective-permute-start(bf16[2,512,128]{2,1,0:T(8,128)(2,1)S(1)} %copy.31), channel_id=1, source_target_pairs={{248,0},{0,8},{8,16},{16,24},{24,32},{32,40},{40,48},{48,56},{56,6... | collective-permute-start | bytes 786440 | tf_op jit(solution)/shard_map/while/body/eval_jaxpr/ppermute | solution.py:12
  47.1 22.1 %collective-permute-start.1 = (f32[2,512,128]{2,1,0:T(8,128)S(1)}, f32[2,512,128]{2,1,0:T(8,128)S(1)}, u32[]{:S(2)}, u32[]{:S(2)}) collective-permute-start(f32[2,512,128]{2,1,0:T(8,128)S(1)} %maximum_add_fusion.2), channel_id=1, source_target_pairs={{248,0},{0,8},{8,16},{16,24},{24,32},{32,40},{40,48},{48,56},{56,6... | collective-permute-start | bytes 1572872 | tf_op jit(solution)/shard_map/while/body/eval_jaxpr/ppermute | solution.py:12
  47.2 22.0 %collective-permute-start = (bf16[2,512,128]{2,1,0:T(8,128)(2,1)S(1)}, bf16[2,512,128]{2,1,0:T(8,128)(2,1)S(1)}, u32[]{:S(2)}, u32[]{:S(2)}) collective-permute-start(bf16[2,512,128]{2,1,0:T(8,128)(2,1)S(1)} %copy.31), channel_id=1, source_target_pairs={{248,0},{0,8},{8,16},{16,24},{24,32},{32,40},{40,48},{48,56},{56,6... | collective-permute-start | bytes 786440 | tf_op jit(solution)/shard_map/while/body/eval_jaxpr/ppermute | solution.py:12
  73.9 21.2 %collective-permute-start.1 = (f32[2,512,128]{2,1,0:T(8,128)S(1)}, f32[2,512,128]{2,1,0:T(8,128)S(1)}, u32[]{:S(2)}, u32[]{:S(2)}) collective-permute-start(f32[2,512,128]{2,1,0:T(8,128)S(1)} %maximum_add_fusion.2), channel_id=1, source_target_pairs={{248,0},{0,8},{8,16},{16,24},{24,32},{32,40},{40,48},{48,56},{56,6... | collective-permute-start | bytes 1572872 | tf_op jit(solution)/shard_map/while/body/eval_jaxpr/ppermute | solution.py:12
  74.0 21.1 %collective-permute-start = (bf16[2,512,128]{2,1,0:T(8,128)(2,1)S(1)}, bf16[2,512,128]{2,1,0:T(8,128)(2,1)S(1)}, u32[]{:S(2)}, u32[]{:S(2)}) collective-permute-start(bf16[2,512,128]{2,1,0:T(8,128)(2,1)S(1)} %copy.31), channel_id=1, source_target_pairs={{248,0},{0,8},{8,16},{16,24},{24,32},{32,40},{40,48},{48,56},{56,6... | collective-permute-start | bytes 786440 | tf_op jit(solution)/shard_map/while/body/eval_jaxpr/ppermute | solution.py:12
  99.8 20.3 %collective-permute-start.1 = (f32[2,512,128]{2,1,0:T(8,128)S(1)}, f32[2,512,128]{2,1,0:T(8,128)S(1)}, u32[]{:S(2)}, u32[]{:S(2)}) collective-permute-start(f32[2,512,128]{2,1,0:T(8,128)S(1)} %maximum_add_fusion.2), channel_id=1, source_target_pairs={{248,0},{0,8},{8,16},{16,24},{24,32},{32,40},{40,48},{48,56},{56,6... | collective-permute-start | bytes 1572872 | tf_op jit(solution)/shard_map/while/body/eval_jaxpr/ppermute | solution.py:12
  99.9 20.2 %collective-permute-start = (bf16[2,512,128]{2,1,0:T(8,128)(2,1)S(1)}, bf16[2,512,128]{2,1,0:T(8,128)(2,1)S(1)}, u32[]{:S(2)}, u32[]{:S(2)}) collective-permute-start(bf16[2,512,128]{2,1,0:T(8,128)(2,1)S(1)} %copy.31), channel_id=1, source_target_pairs={{248,0},{0,8},{8,16},{16,24},{24,32},{32,40},{40,48},{48,56},{56,6... | collective-permute-start | bytes 786440 | tf_op jit(solution)/shard_map/while/body/eval_jaxpr/ppermute | solution.py:12
  124.7 19.4 %collective-permute-start.1 = (f32[2,512,128]{2,1,0:T(8,128)S(1)}, f32[2,512,128]{2,1,0:T(8,128)S(1)}, u32[]{:S(2)}, u32[]{:S(2)}) collective-permute-start(f32[2,512,128]{2,1,0:T(8,128)S(1)} %maximum_add_fusion.2), channel_id=1, source_target_pairs={{248,0},{0,8},{8,16},{16,24},{24,32},{32,40},{40,48},{48,56},{56,6... | collective-permute-start | bytes 1572872 | tf_op jit(solution)/shard_map/while/body/eval_jaxpr/ppermute | solution.py:12
  124.8 19.3 %collective-permute-start = (bf16[2,512,128]{2,1,0:T(8,128)(2,1)S(1)}, bf16[2,512,128]{2,1,0:T(8,128)(2,1)S(1)}, u32[]{:S(2)}, u32[]{:S(2)}) collective-permute-start(bf16[2,512,128]{2,1,0:T(8,128)(2,1)S(1)} %copy.31), channel_id=1, source_target_pairs={{248,0},{0,8},{8,16},{16,24},{24,32},{32,40},{40,48},{48,56},{56,6... | collective-permute-start | bytes 786440 | tf_op jit(solution)/shard_map/while/body/eval_jaxpr/ppermute | solution.py:12
  148.8 18.4 %collective-permute-start.1 = (f32[2,512,128]{2,1,0:T(8,128)S(1)}, f32[2,512,128]{2,1,0:T(8,128)S(1)}, u32[]{:S(2)}, u32[]{:S(2)}) collective-permute-start(f32[2,512,128]{2,1,0:T(8,128)S(1)} %maximum_add_fusion.2), channel_id=1, source_target_pairs={{248,0},{0,8},{8,16},{16,24},{24,32},{32,40},{40,48},{48,56},{56,6... | collective-permute-start | bytes 1572872 | tf_op jit(solution)/shard_map/while/body/eval_jaxpr/ppermute | solution.py:12
  148.9 18.3 %collective-permute-start = (bf16[2,512,128]{2,1,0:T(8,128)(2,1)S(1)}, bf16[2,512,128]{2,1,0:T(8,128)(2,1)S(1)}, u32[]{:S(2)}, u32[]{:S(2)}) collective-permute-start(bf16[2,512,128]{2,1,0:T(8,128)(2,1)S(1)} %copy.31), channel_id=1, source_target_pairs={{248,0},{0,8},{8,16},{16,24},{24,32},{32,40},{40,48},{48,56},{56,6... | collective-permute-start | bytes 786440 | tf_op jit(solution)/shard_map/while/body/eval_jaxpr/ppermute | solution.py:12
  171.9 17.5 %collective-permute-start.1 = (f32[2,512,128]{2,1,0:T(8,128)S(1)}, f32[2,512,128]{2,1,0:T(8,128)S(1)}, u32[]{:S(2)}, u32[]{:S(2)}) collective-permute-start(f32[2,512,128]{2,1,0:T(8,128)S(1)} %maximum_add_fusion.2), channel_id=1, source_target_pairs={{248,0},{0,8},{8,16},{16,24},{24,32},{32,40},{40,48},{48,56},{56,6... | collective-permute-start | bytes 1572872 | tf_op jit(solution)/shard_map/while/body/eval_jaxpr/ppermute | solution.py:12
  172.0 17.4 %collective-permute-start = (bf16[2,512,128]{2,1,0:T(8,128)(2,1)S(1)}, bf16[2,512,128]{2,1,0:T(8,128)(2,1)S(1)}, u32[]{:S(2)}, u32[]{:S(2)}) collective-permute-start(bf16[2,512,128]{2,1,0:T(8,128)(2,1)S(1)} %copy.31), channel_id=1, source_target_pairs={{248,0},{0,8},{8,16},{16,24},{24,32},{32,40},{40,48},{48,56},{56,6... | collective-permute-start | bytes 786440 | tf_op jit(solution)/shard_map/while/body/eval_jaxpr/ppermute | solution.py:12
  194.1 16.6 %collective-permute-start.1 = (f32[2,512,128]{2,1,0:T(8,128)S(1)}, f32[2,512,128]{2,1,0:T(8,128)S(1)}, u32[]{:S(2)}, u32[]{:S(2)}) collective-permute-start(f32[2,512,128]{2,1,0:T(8,128)S(1)} %maximum_add_fusion.2), channel_id=1, source_target_pairs={{248,0},{0,8},{8,16},{16,24},{24,32},{32,40},{40,48},{48,56},{56,6... | collective-permute-start | bytes 1572872 | tf_op jit(solution)/shard_map/while/body/eval_jaxpr/ppermute | solution.py:12
  194.2 16.5 %collective-permute-start = (bf16[2,512,128]{2,1,0:T(8,128)(2,1)S(1)}, bf16[2,512,128]{2,1,0:T(8,128)(2,1)S(1)}, u32[]{:S(2)}, u32[]{:S(2)}) collective-permute-start(bf16[2,512,128]{2,1,0:T(8,128)(2,1)S(1)} %copy.31), channel_id=1, source_target_pairs={{248,0},{0,8},{8,16},{16,24},{24,32},{32,40},{40,48},{48,56},{56,6... | collective-permute-start | bytes 786440 | tf_op jit(solution)/shard_map/while/body/eval_jaxpr/ppermute | solution.py:12
  215.4 15.7 %collective-permute-start.1 = (f32[2,512,128]{2,1,0:T(8,128)S(1)}, f32[2,512,128]{2,1,0:T(8,128)S(1)}, u32[]{:S(2)}, u32[]{:S(2)}) collective-permute-start(f32[2,512,128]{2,1,0:T(8,128)S(1)} %maximum_add_fusion.2), channel_id=1, source_target_pairs={{248,0},{0,8},{8,16},{16,24},{24,32},{32,40},{40,48},{48,56},{56,6... | collective-permute-start | bytes 1572872 | tf_op jit(solution)/shard_map/while/body/eval_jaxpr/ppermute | solution.py:12
  215.5 15.6 %collective-permute-start = (bf16[2,512,128]{2,1,0:T(8,128)(2,1)S(1)}, bf16[2,512,128]{2,1,0:T(8,128)(2,1)S(1)}, u32[]{:S(2)}, u32[]{:S(2)}) collective-permute-start(bf16[2,512,128]{2,1,0:T(8,128)(2,1)S(1)} %copy.31), channel_id=1, source_target_pairs={{248,0},{0,8},{8,16},{16,24},{24,32},{32,40},{40,48},{48,56},{56,6... | collective-permute-start | bytes 786440 | tf_op jit(solution)/shard_map/while/body/eval_jaxpr/ppermute | solution.py:12
  235.7 15.4 %collective-permute-start.1 = (f32[2,512,128]{2,1,0:T(8,128)S(1)}, f32[2,512,128]{2,1,0:T(8,128)S(1)}, u32[]{:S(2)}, u32[]{:S(2)}) collective-permute-start(f32[2,512,128]{2,1,0:T(8,128)S(1)} %maximum_add_fusion.2), channel_id=1, source_target_pairs={{248,0},{0,8},{8,16},{16,24},{24,32},{32,40},{40,48},{48,56},{56,6... | collective-permute-start | bytes 1572872 | tf_op jit(solution)/shard_map/while/body/eval_jaxpr/ppermute | solution.py:12
  235.8 15.3 %collective-permute-start = (bf16[2,512,128]{2,1,0:T(8,128)(2,1)S(1)}, bf16[2,512,128]{2,1,0:T(8,128)(2,1)S(1)}, u32[]{:S(2)}, u32[]{:S(2)}) collective-permute-start(bf16[2,512,128]{2,1,0:T(8,128)(2,1)S(1)} %copy.31), channel_id=1, source_target_pairs={{248,0},{0,8},{8,16},{16,24},{24,32},{32,40},{40,48},{48,56},{56,6... | collective-permute-start | bytes 786440 | tf_op jit(solution)/shard_map/while/body/eval_jaxpr/ppermute | solution.py:12
  255.8 15.4 %collective-permute-start.1 = (f32[2,512,128]{2,1,0:T(8,128)S(1)}, f32[2,512,128]{2,1,0:T(8,128)S(1)}, u32[]{:S(2)}, u32[]{:S(2)}) collective-permute-start(f32[2,512,128]{2,1,0:T(8,128)S(1)} %maximum_add_fusion.2), channel_id=1, source_target_pairs={{248,0},{0,8},{8,16},{16,24},{24,32},{32,40},{40,48},{48,56},{56,6... | collective-permute-start | bytes 1572872 | tf_op jit(solution)/shard_map/while/body/eval_jaxpr/ppermute | solution.py:12
  255.9 15.3 %collective-permute-start = (bf16[2,512,128]{2,1,0:T(8,128)(2,1)S(1)}, bf16[2,512,128]{2,1,0:T(8,128)(2,1)S(1)}, u32[]{:S(2)}, u32[]{:S(2)}) collective-permute-start(bf16[2,512,128]{2,1,0:T(8,128)(2,1)S(1)} %copy.31), channel_id=1, source_target_pairs={{248,0},{0,8},{8,16},{16,24},{24,32},{32,40},{40,48},{48,56},{56,6... | collective-permute-start | bytes 786440 | tf_op jit(solution)/shard_map/while/body/eval_jaxpr/ppermute | solution.py:12
  275.9 16.2 %collective-permute-start.1 = (f32[2,512,128]{2,1,0:T(8,128)S(1)}, f32[2,512,128]{2,1,0:T(8,128)S(1)}, u32[]{:S(2)}, u32[]{:S(2)}) collective-permute-start(f32[2,512,128]{2,1,0:T(8,128)S(1)} %maximum_add_fusion.2), channel_id=1, source_target_pairs={{248,0},{0,8},{8,16},{16,24},{24,32},{32,40},{40,48},{48,56},{56,6... | collective-permute-start | bytes 1572872 | tf_op jit(solution)/shard_map/while/body/eval_jaxpr/ppermute | solution.py:12
  276.0 16.1 %collective-permute-start = (bf16[2,512,128]{2,1,0:T(8,128)(2,1)S(1)}, bf16[2,512,128]{2,1,0:T(8,128)(2,1)S(1)}, u32[]{:S(2)}, u32[]{:S(2)}) collective-permute-start(bf16[2,512,128]{2,1,0:T(8,128)(2,1)S(1)} %copy.31), channel_id=1, source_target_pairs={{248,0},{0,8},{8,16},{16,24},{24,32},{32,40},{40,48},{48,56},{56,6... | collective-permute-start | bytes 786440 | tf_op jit(solution)/shard_map/while/body/eval_jaxpr/ppermute | solution.py:12
  296.7 17.3 %collective-permute-start.1 = (f32[2,512,128]{2,1,0:T(8,128)S(1)}, f32[2,512,128]{2,1,0:T(8,128)S(1)}, u32[]{:S(2)}, u32[]{:S(2)}) collective-permute-start(f32[2,512,128]{2,1,0:T(8,128)S(1)} %maximum_add_fusion.2), channel_id=1, source_target_pairs={{248,0},{0,8},{8,16},{16,24},{24,32},{32,40},{40,48},{48,56},{56,6... | collective-permute-start | bytes 1572872 | tf_op jit(solution)/shard_map/while/body/eval_jaxpr/ppermute | solution.py:12
  296.8 17.2 %collective-permute-start = (bf16[2,512,128]{2,1,0:T(8,128)(2,1)S(1)}, bf16[2,512,128]{2,1,0:T(8,128)(2,1)S(1)}, u32[]{:S(2)}, u32[]{:S(2)}) collective-permute-start(bf16[2,512,128]{2,1,0:T(8,128)(2,1)S(1)} %copy.31), channel_id=1, source_target_pairs={{248,0},{0,8},{8,16},{16,24},{24,32},{32,40},{40,48},{48,56},{56,6... | collective-permute-start | bytes 786440 | tf_op jit(solution)/shard_map/while/body/eval_jaxpr/ppermute | solution.py:12
  318.7 18.4 %collective-permute-start.1 = (f32[2,512,128]{2,1,0:T(8,128)S(1)}, f32[2,512,128]{2,1,0:T(8,128)S(1)}, u32[]{:S(2)}, u32[]{:S(2)}) collective-permute-start(f32[2,512,128]{2,1,0:T(8,128)S(1)} %maximum_add_fusion.2), channel_id=1, source_target_pairs={{248,0},{0,8},{8,16},{16,24},{24,32},{32,40},{40,48},{48,56},{56,6... | collective-permute-start | bytes 1572872 | tf_op jit(solution)/shard_map/while/body/eval_jaxpr/ppermute | solution.py:12
  318.8 18.3 %collective-permute-start = (bf16[2,512,128]{2,1,0:T(8,128)(2,1)S(1)}, bf16[2,512,128]{2,1,0:T(8,128)(2,1)S(1)}, u32[]{:S(2)}, u32[]{:S(2)}) collective-permute-start(bf16[2,512,128]{2,1,0:T(8,128)(2,1)S(1)} %copy.31), channel_id=1, source_target_pairs={{248,0},{0,8},{8,16},{16,24},{24,32},{32,40},{40,48},{48,56},{56,6... | collective-permute-start | bytes 786440 | tf_op jit(solution)/shard_map/while/body/eval_jaxpr/ppermute | solution.py:12
  341.7 19.4 %collective-permute-start.1 = (f32[2,512,128]{2,1,0:T(8,128)S(1)}, f32[2,512,128]{2,1,0:T(8,128)S(1)}, u32[]{:S(2)}, u32[]{:S(2)}) collective-permute-start(f32[2,512,128]{2,1,0:T(8,128)S(1)} %maximum_add_fusion.2), channel_id=1, source_target_pairs={{248,0},{0,8},{8,16},{16,24},{24,32},{32,40},{40,48},{48,56},{56,6... | collective-permute-start | bytes 1572872 | tf_op jit(solution)/shard_map/while/body/eval_jaxpr/ppermute | solution.py:12
  341.8 19.4 %collective-permute-start = (bf16[2,512,128]{2,1,0:T(8,128)(2,1)S(1)}, bf16[2,512,128]{2,1,0:T(8,128)(2,1)S(1)}, u32[]{:S(2)}, u32[]{:S(2)}) collective-permute-start(bf16[2,512,128]{2,1,0:T(8,128)(2,1)S(1)} %copy.31), channel_id=1, source_target_pairs={{248,0},{0,8},{8,16},{16,24},{24,32},{32,40},{40,48},{48,56},{56,6... | collective-permute-start | bytes 786440 | tf_op jit(solution)/shard_map/while/body/eval_jaxpr/ppermute | solution.py:12
  365.9 20.5 %collective-permute-start.1 = (f32[2,512,128]{2,1,0:T(8,128)S(1)}, f32[2,512,128]{2,1,0:T(8,128)S(1)}, u32[]{:S(2)}, u32[]{:S(2)}) collective-permute-start(f32[2,512,128]{2,1,0:T(8,128)S(1)} %maximum_add_fusion.2), channel_id=1, source_target_pairs={{248,0},{0,8},{8,16},{16,24},{24,32},{32,40},{40,48},{48,56},{56,6... | collective-permute-start | bytes 1572872 | tf_op jit(solution)/shard_map/while/body/eval_jaxpr/ppermute | solution.py:12
  366.0 20.4 %collective-permute-start = (bf16[2,512,128]{2,1,0:T(8,128)(2,1)S(1)}, bf16[2,512,128]{2,1,0:T(8,128)(2,1)S(1)}, u32[]{:S(2)}, u32[]{:S(2)}) collective-permute-start(bf16[2,512,128]{2,1,0:T(8,128)(2,1)S(1)} %copy.31), channel_id=1, source_target_pairs={{248,0},{0,8},{8,16},{16,24},{24,32},{32,40},{40,48},{48,56},{56,6... | collective-permute-start | bytes 786440 | tf_op jit(solution)/shard_map/while/body/eval_jaxpr/ppermute | solution.py:12
  391.1 21.6 %collective-permute-start.1 = (f32[2,512,128]{2,1,0:T(8,128)S(1)}, f32[2,512,128]{2,1,0:T(8,128)S(1)}, u32[]{:S(2)}, u32[]{:S(2)}) collective-permute-start(f32[2,512,128]{2,1,0:T(8,128)S(1)} %maximum_add_fusion.2), channel_id=1, source_target_pairs={{248,0},{0,8},{8,16},{16,24},{24,32},{32,40},{40,48},{48,56},{56,6... | collective-permute-start | bytes 1572872 | tf_op jit(solution)/shard_map/while/body/eval_jaxpr/ppermute | solution.py:12
  391.2 21.5 %collective-permute-start = (bf16[2,512,128]{2,1,0:T(8,128)(2,1)S(1)}, bf16[2,512,128]{2,1,0:T(8,128)(2,1)S(1)}, u32[]{:S(2)}, u32[]{:S(2)}) collective-permute-start(bf16[2,512,128]{2,1,0:T(8,128)(2,1)S(1)} %copy.31), channel_id=1, source_target_pairs={{248,0},{0,8},{8,16},{16,24},{24,32},{32,40},{40,48},{48,56},{56,6... | collective-permute-start | bytes 786440 | tf_op jit(solution)/shard_map/while/body/eval_jaxpr/ppermute | solution.py:12
  417.4 22.8 %collective-permute-start.1 = (f32[2,512,128]{2,1,0:T(8,128)S(1)}, f32[2,512,128]{2,1,0:T(8,128)S(1)}, u32[]{:S(2)}, u32[]{:S(2)}) collective-permute-start(f32[2,512,128]{2,1,0:T(8,128)S(1)} %maximum_add_fusion.2), channel_id=1, source_target_pairs={{248,0},{0,8},{8,16},{16,24},{24,32},{32,40},{40,48},{48,56},{56,6... | collective-permute-start | bytes 1572872 | tf_op jit(solution)/shard_map/while/body/eval_jaxpr/ppermute | solution.py:12
  417.5 22.7 %collective-permute-start = (bf16[2,512,128]{2,1,0:T(8,128)(2,1)S(1)}, bf16[2,512,128]{2,1,0:T(8,128)(2,1)S(1)}, u32[]{:S(2)}, u32[]{:S(2)}) collective-permute-start(bf16[2,512,128]{2,1,0:T(8,128)(2,1)S(1)} %copy.31), channel_id=1, source_target_pairs={{248,0},{0,8},{8,16},{16,24},{24,32},{32,40},{40,48},{48,56},{56,6... | collective-permute-start | bytes 786440 | tf_op jit(solution)/shard_map/while/body/eval_jaxpr/ppermute | solution.py:12
  444.8 23.7 %collective-permute-start.1 = (f32[2,512,128]{2,1,0:T(8,128)S(1)}, f32[2,512,128]{2,1,0:T(8,128)S(1)}, u32[]{:S(2)}, u32[]{:S(2)}) collective-permute-start(f32[2,512,128]{2,1,0:T(8,128)S(1)} %maximum_add_fusion.2), channel_id=1, source_target_pairs={{248,0},{0,8},{8,16},{16,24},{24,32},{32,40},{40,48},{48,56},{56,6... | collective-permute-start | bytes 1572872 | tf_op jit(solution)/shard_map/while/body/eval_jaxpr/ppermute | solution.py:12
  444.9 23.6 %collective-permute-start = (bf16[2,512,128]{2,1,0:T(8,128)(2,1)S(1)}, bf16[2,512,128]{2,1,0:T(8,128)(2,1)S(1)}, u32[]{:S(2)}, u32[]{:S(2)}) collective-permute-start(bf16[2,512,128]{2,1,0:T(8,128)(2,1)S(1)} %copy.31), channel_id=1, source_target_pairs={{248,0},{0,8},{8,16},{16,24},{24,32},{32,40},{40,48},{48,56},{56,6... | collective-permute-start | bytes 786440 | tf_op jit(solution)/shard_map/while/body/eval_jaxpr/ppermute | solution.py:12
  473.2 22.9 %collective-permute-start.1 = (f32[2,512,128]{2,1,0:T(8,128)S(1)}, f32[2,512,128]{2,1,0:T(8,128)S(1)}, u32[]{:S(2)}, u32[]{:S(2)}) collective-permute-start(f32[2,512,128]{2,1,0:T(8,128)S(1)} %maximum_add_fusion.2), channel_id=1, source_target_pairs={{248,0},{0,8},{8,16},{16,24},{24,32},{32,40},{40,48},{48,56},{56,6... | collective-permute-start | bytes 1572872 | tf_op jit(solution)/shard_map/while/body/eval_jaxpr/ppermute | solution.py:12
  473.3 22.8 %collective-permute-start = (bf16[2,512,128]{2,1,0:T(8,128)(2,1)S(1)}, bf16[2,512,128]{2,1,0:T(8,128)(2,1)S(1)}, u32[]{:S(2)}, u32[]{:S(2)}) collective-permute-start(bf16[2,512,128]{2,1,0:T(8,128)(2,1)S(1)} %copy.31), channel_id=1, source_target_pairs={{248,0},{0,8},{8,16},{16,24},{24,32},{32,40},{40,48},{48,56},{56,6... | collective-permute-start | bytes 786440 | tf_op jit(solution)/shard_map/while/body/eval_jaxpr/ppermute | solution.py:12
  500.8 22.0 %collective-permute-start.1 = (f32[2,512,128]{2,1,0:T(8,128)S(1)}, f32[2,512,128]{2,1,0:T(8,128)S(1)}, u32[]{:S(2)}, u32[]{:S(2)}) collective-permute-start(f32[2,512,128]{2,1,0:T(8,128)S(1)} %maximum_add_fusion.2), channel_id=1, source_target_pairs={{248,0},{0,8},{8,16},{16,24},{24,32},{32,40},{40,48},{48,56},{56,6... | collective-permute-start | bytes 1572872 | tf_op jit(solution)/shard_map/while/body/eval_jaxpr/ppermute | solution.py:12
  500.8 21.9 %collective-permute-start = (bf16[2,512,128]{2,1,0:T(8,128)(2,1)S(1)}, bf16[2,512,128]{2,1,0:T(8,128)(2,1)S(1)}, u32[]{:S(2)}, u32[]{:S(2)}) collective-permute-start(bf16[2,512,128]{2,1,0:T(8,128)(2,1)S(1)} %copy.31), channel_id=1, source_target_pairs={{248,0},{0,8},{8,16},{16,24},{24,32},{32,40},{40,48},{48,56},{56,6... | collective-permute-start | bytes 786440 | tf_op jit(solution)/shard_map/while/body/eval_jaxpr/ppermute | solution.py:12
  527.5 21.1 %collective-permute-start.1 = (f32[2,512,128]{2,1,0:T(8,128)S(1)}, f32[2,512,128]{2,1,0:T(8,128)S(1)}, u32[]{:S(2)}, u32[]{:S(2)}) collective-permute-start(f32[2,512,128]{2,1,0:T(8,128)S(1)} %maximum_add_fusion.2), channel_id=1, source_target_pairs={{248,0},{0,8},{8,16},{16,24},{24,32},{32,40},{40,48},{48,56},{56,6... | collective-permute-start | bytes 1572872 | tf_op jit(solution)/shard_map/while/body/eval_jaxpr/ppermute | solution.py:12
  527.6 21.0 %collective-permute-start = (bf16[2,512,128]{2,1,0:T(8,128)(2,1)S(1)}, bf16[2,512,128]{2,1,0:T(8,128)(2,1)S(1)}, u32[]{:S(2)}, u32[]{:S(2)}) collective-permute-start(bf16[2,512,128]{2,1,0:T(8,128)(2,1)S(1)} %copy.31), channel_id=1, source_target_pairs={{248,0},{0,8},{8,16},{16,24},{24,32},{32,40},{40,48},{48,56},{56,6... | collective-permute-start | bytes 786440 | tf_op jit(solution)/shard_map/while/body/eval_jaxpr/ppermute | solution.py:12
  553.3 20.2 %collective-permute-start.1 = (f32[2,512,128]{2,1,0:T(8,128)S(1)}, f32[2,512,128]{2,1,0:T(8,128)S(1)}, u32[]{:S(2)}, u32[]{:S(2)}) collective-permute-start(f32[2,512,128]{2,1,0:T(8,128)S(1)} %maximum_add_fusion.2), channel_id=1, source_target_pairs={{248,0},{0,8},{8,16},{16,24},{24,32},{32,40},{40,48},{48,56},{56,6... | collective-permute-start | bytes 1572872 | tf_op jit(solution)/shard_map/while/body/eval_jaxpr/ppermute | solution.py:12
  553.3 20.1 %collective-permute-start = (bf16[2,512,128]{2,1,0:T(8,128)(2,1)S(1)}, bf16[2,512,128]{2,1,0:T(8,128)(2,1)S(1)}, u32[]{:S(2)}, u32[]{:S(2)}) collective-permute-start(bf16[2,512,128]{2,1,0:T(8,128)(2,1)S(1)} %copy.31), channel_id=1, source_target_pairs={{248,0},{0,8},{8,16},{16,24},{24,32},{32,40},{40,48},{48,56},{56,6... | collective-permute-start | bytes 786440 | tf_op jit(solution)/shard_map/while/body/eval_jaxpr/ppermute | solution.py:12
  578.1 19.2 %collective-permute-start.1 = (f32[2,512,128]{2,1,0:T(8,128)S(1)}, f32[2,512,128]{2,1,0:T(8,128)S(1)}, u32[]{:S(2)}, u32[]{:S(2)}) collective-permute-start(f32[2,512,128]{2,1,0:T(8,128)S(1)} %maximum_add_fusion.2), channel_id=1, source_target_pairs={{248,0},{0,8},{8,16},{16,24},{24,32},{32,40},{40,48},{48,56},{56,6... | collective-permute-start | bytes 1572872 | tf_op jit(solution)/shard_map/while/body/eval_jaxpr/ppermute | solution.py:12
  578.2 19.2 %collective-permute-start = (bf16[2,512,128]{2,1,0:T(8,128)(2,1)S(1)}, bf16[2,512,128]{2,1,0:T(8,128)(2,1)S(1)}, u32[]{:S(2)}, u32[]{:S(2)}) collective-permute-start(bf16[2,512,128]{2,1,0:T(8,128)(2,1)S(1)} %copy.31), channel_id=1, source_target_pairs={{248,0},{0,8},{8,16},{16,24},{24,32},{32,40},{40,48},{48,56},{56,6... | collective-permute-start | bytes 786440 | tf_op jit(solution)/shard_map/while/body/eval_jaxpr/ppermute | solution.py:12
  602.0 18.3 %collective-permute-start.1 = (f32[2,512,128]{2,1,0:T(8,128)S(1)}, f32[2,512,128]{2,1,0:T(8,128)S(1)}, u32[]{:S(2)}, u32[]{:S(2)}) collective-permute-start(f32[2,512,128]{2,1,0:T(8,128)S(1)} %maximum_add_fusion.2), channel_id=1, source_target_pairs={{248,0},{0,8},{8,16},{16,24},{24,32},{32,40},{40,48},{48,56},{56,6... | collective-permute-start | bytes 1572872 | tf_op jit(solution)/shard_map/while/body/eval_jaxpr/ppermute | solution.py:12
  602.1 18.2 %collective-permute-start = (bf16[2,512,128]{2,1,0:T(8,128)(2,1)S(1)}, bf16[2,512,128]{2,1,0:T(8,128)(2,1)S(1)}, u32[]{:S(2)}, u32[]{:S(2)}) collective-permute-start(bf16[2,512,128]{2,1,0:T(8,128)(2,1)S(1)} %copy.31), channel_id=1, source_target_pairs={{248,0},{0,8},{8,16},{16,24},{24,32},{32,40},{40,48},{48,56},{56,6... | collective-permute-start | bytes 786440 | tf_op jit(solution)/shard_map/while/body/eval_jaxpr/ppermute | solution.py:12
  625.0 17.4 %collective-permute-start.1 = (f32[2,512,128]{2,1,0:T(8,128)S(1)}, f32[2,512,128]{2,1,0:T(8,128)S(1)}, u32[]{:S(2)}, u32[]{:S(2)}) collective-permute-start(f32[2,512,128]{2,1,0:T(8,128)S(1)} %maximum_add_fusion.2), channel_id=1, source_target_pairs={{248,0},{0,8},{8,16},{16,24},{24,32},{32,40},{40,48},{48,56},{56,6... | collective-permute-start | bytes 1572872 | tf_op jit(solution)/shard_map/while/body/eval_jaxpr/ppermute | solution.py:12
  625.1 17.3 %collective-permute-start = (bf16[2,512,128]{2,1,0:T(8,128)(2,1)S(1)}, bf16[2,512,128]{2,1,0:T(8,128)(2,1)S(1)}, u32[]{:S(2)}, u32[]{:S(2)}) collective-permute-start(bf16[2,512,128]{2,1,0:T(8,128)(2,1)S(1)} %copy.31), channel_id=1, source_target_pairs={{248,0},{0,8},{8,16},{16,24},{24,32},{32,40},{40,48},{48,56},{56,6... | collective-permute-start | bytes 786440 | tf_op jit(solution)/shard_map/while/body/eval_jaxpr/ppermute | solution.py:12
  647.1 16.5 %collective-permute-start.1 = (f32[2,512,128]{2,1,0:T(8,128)S(1)}, f32[2,512,128]{2,1,0:T(8,128)S(1)}, u32[]{:S(2)}, u32[]{:S(2)}) collective-permute-start(f32[2,512,128]{2,1,0:T(8,128)S(1)} %maximum_add_fusion.2), channel_id=1, source_target_pairs={{248,0},{0,8},{8,16},{16,24},{24,32},{32,40},{40,48},{48,56},{56,6... | collective-permute-start | bytes 1572872 | tf_op jit(solution)/shard_map/while/body/eval_jaxpr/ppermute | solution.py:12
  647.2 16.4 %collective-permute-start = (bf16[2,512,128]{2,1,0:T(8,128)(2,1)S(1)}, bf16[2,512,128]{2,1,0:T(8,128)(2,1)S(1)}, u32[]{:S(2)}, u32[]{:S(2)}) collective-permute-start(bf16[2,512,128]{2,1,0:T(8,128)(2,1)S(1)} %copy.31), channel_id=1, source_target_pairs={{248,0},{0,8},{8,16},{16,24},{24,32},{32,40},{40,48},{48,56},{56,6... | collective-permute-start | bytes 786440 | tf_op jit(solution)/shard_map/while/body/eval_jaxpr/ppermute | solution.py:12
  668.3 15.6 %collective-permute-start.1 = (f32[2,512,128]{2,1,0:T(8,128)S(1)}, f32[2,512,128]{2,1,0:T(8,128)S(1)}, u32[]{:S(2)}, u32[]{:S(2)}) collective-permute-start(f32[2,512,128]{2,1,0:T(8,128)S(1)} %maximum_add_fusion.2), channel_id=1, source_target_pairs={{248,0},{0,8},{8,16},{16,24},{24,32},{32,40},{40,48},{48,56},{56,6... | collective-permute-start | bytes 1572872 | tf_op jit(solution)/shard_map/while/body/eval_jaxpr/ppermute | solution.py:12
  668.4 15.5 %collective-permute-start = (bf16[2,512,128]{2,1,0:T(8,128)(2,1)S(1)}, bf16[2,512,128]{2,1,0:T(8,128)(2,1)S(1)}, u32[]{:S(2)}, u32[]{:S(2)}) collective-permute-start(bf16[2,512,128]{2,1,0:T(8,128)(2,1)S(1)} %copy.31), channel_id=1, source_target_pairs={{248,0},{0,8},{8,16},{16,24},{24,32},{32,40},{40,48},{48,56},{56,6... | collective-permute-start | bytes 786440 | tf_op jit(solution)/shard_map/while/body/eval_jaxpr/ppermute | solution.py:12
  688.5 15.4 %collective-permute-start.1 = (f32[2,512,128]{2,1,0:T(8,128)S(1)}, f32[2,512,128]{2,1,0:T(8,128)S(1)}, u32[]{:S(2)}, u32[]{:S(2)}) collective-permute-start(f32[2,512,128]{2,1,0:T(8,128)S(1)} %maximum_add_fusion.2), channel_id=1, source_target_pairs={{248,0},{0,8},{8,16},{16,24},{24,32},{32,40},{40,48},{48,56},{56,6... | collective-permute-start | bytes 1572872 | tf_op jit(solution)/shard_map/while/body/eval_jaxpr/ppermute | solution.py:12
  688.6 15.3 %collective-permute-start = (bf16[2,512,128]{2,1,0:T(8,128)(2,1)S(1)}, bf16[2,512,128]{2,1,0:T(8,128)(2,1)S(1)}, u32[]{:S(2)}, u32[]{:S(2)}) collective-permute-start(bf16[2,512,128]{2,1,0:T(8,128)(2,1)S(1)} %copy.31), channel_id=1, source_target_pairs={{248,0},{0,8},{8,16},{16,24},{24,32},{32,40},{40,48},{48,56},{56,6... | collective-permute-start | bytes 786440 | tf_op jit(solution)/shard_map/while/body/eval_jaxpr/ppermute | solution.py:12
  708.6 15.4 %collective-permute-start.1 = (f32[2,512,128]{2,1,0:T(8,128)S(1)}, f32[2,512,128]{2,1,0:T(8,128)S(1)}, u32[]{:S(2)}, u32[]{:S(2)}) collective-permute-start(f32[2,512,128]{2,1,0:T(8,128)S(1)} %maximum_add_fusion.2), channel_id=1, source_target_pairs={{248,0},{0,8},{8,16},{16,24},{24,32},{32,40},{40,48},{48,56},{56,6... | collective-permute-start | bytes 1572872 | tf_op jit(solution)/shard_map/while/body/eval_jaxpr/ppermute | solution.py:12
  708.7 15.3 %collective-permute-start = (bf16[2,512,128]{2,1,0:T(8,128)(2,1)S(1)}, bf16[2,512,128]{2,1,0:T(8,128)(2,1)S(1)}, u32[]{:S(2)}, u32[]{:S(2)}) collective-permute-start(bf16[2,512,128]{2,1,0:T(8,128)(2,1)S(1)} %copy.31), channel_id=1, source_target_pairs={{248,0},{0,8},{8,16},{16,24},{24,32},{32,40},{40,48},{48,56},{56,6... | collective-permute-start | bytes 786440 | tf_op jit(solution)/shard_map/while/body/eval_jaxpr/ppermute | solution.py:12
  728.7 15.4 %collective-permute-start.1 = (f32[2,512,128]{2,1,0:T(8,128)S(1)}, f32[2,512,128]{2,1,0:T(8,128)S(1)}, u32[]{:S(2)}, u32[]{:S(2)}) collective-permute-start(f32[2,512,128]{2,1,0:T(8,128)S(1)} %maximum_add_fusion.2), channel_id=1, source_target_pairs={{248,0},{0,8},{8,16},{16,24},{24,32},{32,40},{40,48},{48,56},{56,6... | collective-permute-start | bytes 1572872 | tf_op jit(solution)/shard_map/while/body/eval_jaxpr/ppermute | solution.py:12
  728.8 15.3 %collective-permute-start = (bf16[2,512,128]{2,1,0:T(8,128)(2,1)S(1)}, bf16[2,512,128]{2,1,0:T(8,128)(2,1)S(1)}, u32[]{:S(2)}, u32[]{:S(2)}) collective-permute-start(bf16[2,512,128]{2,1,0:T(8,128)(2,1)S(1)} %copy.31), channel_id=1, source_target_pairs={{248,0},{0,8},{8,16},{16,24},{24,32},{32,40},{40,48},{48,56},{56,6... | collective-permute-start | bytes 786440 | tf_op jit(solution)/shard_map/while/body/eval_jaxpr/ppermute | solution.py:12
  748.7 15.4 %collective-permute-start.1 = (f32[2,512,128]{2,1,0:T(8,128)S(1)}, f32[2,512,128]{2,1,0:T(8,128)S(1)}, u32[]{:S(2)}, u32[]{:S(2)}) collective-permute-start(f32[2,512,128]{2,1,0:T(8,128)S(1)} %maximum_add_fusion.2), channel_id=1, source_target_pairs={{248,0},{0,8},{8,16},{16,24},{24,32},{32,40},{40,48},{48,56},{56,6... | collective-permute-start | bytes 1572872 | tf_op jit(solution)/shard_map/while/body/eval_jaxpr/ppermute | solution.py:12
  748.8 15.3 %collective-permute-start = (bf16[2,512,128]{2,1,0:T(8,128)(2,1)S(1)}, bf16[2,512,128]{2,1,0:T(8,128)(2,1)S(1)}, u32[]{:S(2)}, u32[]{:S(2)}) collective-permute-start(bf16[2,512,128]{2,1,0:T(8,128)(2,1)S(1)} %copy.31), channel_id=1, source_target_pairs={{248,0},{0,8},{8,16},{16,24},{24,32},{32,40},{40,48},{48,56},{56,6... | collective-permute-start | bytes 786440 | tf_op jit(solution)/shard_map/while/body/eval_jaxpr/ppermute | solution.py:12
  (6 other events, 13.4 us)
where the time goes:
time: 765 us
  waiting for transfers between devices  582 us (76%)
  local copies, waits for them, and re-layouts  84.5 us (11%)
  matrix products  75.5 us (10%)
  other arithmetic  10.4 us (1%)
  starting transfers between devices  9.1 us (1%)
    ppermute x64, waiting for transfers between devices, shifted(): return lax.ppermute(block, axis, route)  582 us
    broadcast_in_dim x32, local copies, waits for them, and re-layouts, pair_grads(): jnp.repeat(jnp.repeat(small, BLK, 0), BLK, 1) > 0  51.1 us
    dot_general x32, matrix products, pair_grads(): lax.dot_general(weights, out_grad, (((0,), (0,)), ((), ())), preferred_el...  22.5 us
    dot_general x32, matrix products, pair_grads(): jnp.dot(out_grad, value_piece.T, preferred_element_type=jnp.float32)  22.1 us
    gather x33, local copies, waits for them, and re-layouts, pair_grads(): small = block_mask[q_blocks][:, k_blocks]  19.3 us
  transfers between devices with their start and end apart: 64, of which 32 were waited for; matrix products, arithmetic and copies ran while one was open for 1% of the time, Pallas kernels for 0%

commit v1 on v0

v1 whole, which is shorter than its diff:
```python
import functools

import jax
import jax.numpy as jnp
from jax import lax
from jax.experimental import pallas as pl
from jax.experimental.pallas import tpu as pltpu
from jax.sharding import PartitionSpec as P

BLK = 128
NZ = 8
NY = 4
OWN = 4
NK = NY * OWN
UNROLL = 4
SPARE = 8
GROUPS = ((0, 1, 2, 3, 4, 5, 6, 7),)
bf16, f32, i32 = jnp.bfloat16, jnp.float32, jnp.int32


def list_sizes():
    return [len(g) * OWN * NK + SPARE for g in GROUPS]


def z_shift(a, d):
    route = [(y * NZ + z, y * NZ + (z + d) % NZ) for y in range(NY) for z in range(NZ)]
    return lax.ppermute(a, "seq", route)


def y_shift(a, d):
    route = [(y * NZ + z, (y + d) % NY * NZ + z) for y in range(NY) for z in range(NZ)]
    return lax.ppermute(a, "seq", route)


def plan_kernel(me_ref, order_ref, smask_ref, vmask_ref, rate_ref, count_ref, *list_refs):
    me = me_ref[0]
    y, z = me // NZ, me % NZ
    for g, (group, out) in enumerate(zip(GROUPS, list_refs)):
        n = jnp.int32(0)
        for place, slot in enumerate(group):
            first = (y * NZ + (z - slot + NZ) % NZ) * OWN

            def row(i, n, place=place, first=first, out=out):
                bq = order_ref[first + i]
                for t in range(NY):
                    kfirst = ((y - t + NY) % NY * NZ + z) * OWN
                    for j in range(OWN):
                        bk = order_ref[kfirst + j]
                        live = jnp.where((smask_ref[bq, bk] > 0) & (bk <= bq), 1, 0)
                        diag = jnp.where(bk == bq, 1, 0)
                        out[n] = (place * OWN + i) + (t * OWN + j) * 64 + bq * 1024 + diag * 262144
                        n = n + live
                return n

            n = lax.fori_loop(0, OWN, row, n)
        for s in range(UNROLL):
            out[n + s] = jnp.int32(BLK * 1024)
        count_ref[g] = n
    ids_r = lax.broadcasted_iota(i32, (BLK, BLK), 0)
    ids_c = lax.broadcasted_iota(i32, (BLK, BLK), 1)
    mask = vmask_ref[...].astype(f32)
    below = jnp.sum(jnp.where(ids_c < ids_r, mask, 0.0), axis=1, keepdims=True)
    diag = jnp.sum(jnp.where(ids_c == ids_r, mask, 0.0), axis=1, keepdims=True)
    count = below * float(BLK) + diag * (ids_c + 1).astype(f32)
    rate_ref[pl.ds(0, BLK), :] = 1.0 / jnp.sqrt(jnp.maximum(count, 1.0))
    rate_ref[pl.ds(BLK, 8), :] = jnp.zeros((8, BLK), f32)


def make_plan(me, block_order, block_mask):
    smem = pl.BlockSpec(memory_space=pltpu.SMEM)
    vmem = pl.BlockSpec(memory_space=pltpu.VMEM)
    return pl.pallas_call(
        plan_kernel,
        out_shape=[
            jax.ShapeDtypeStruct((BLK + 8, BLK), f32),
            jax.ShapeDtypeStruct((len(GROUPS),), i32),
        ]
        + [jax.ShapeDtypeStruct((n,), i32) for n in list_sizes()],
        in_specs=[smem, smem, smem, vmem],
        out_specs=[vmem, smem] + [smem] * len(GROUPS),
        cost_estimate=pl.CostEstimate(flops=10_000, bytes_accessed=200_000, transcendentals=0),
    )(me, block_order, block_mask, block_mask)


def pairs_kernel(g, first, last, n_slots, *refs):
    refs = list(refs)
    take = lambda n: [refs.pop(0) for _ in range(n)]
    count_ref, list_ref, rate_ref = take(3)
    q_in, g_in = take(n_slots), take(n_slots)
    k_in, v_in = take(NY), take(NY)
    acc_in = [] if first else take(2)
    dq_out = take(n_slots)
    kv_out = take(NY + 1) if last else take(2)
    q_s, g_s, k_s, v_s, dq_s = take(5)
    dk_s, dv_s = take(2) if last else kv_out
    sem = take(1)[0]
    rows = OWN * BLK
    copies = []
    for ins, dst in ((q_in, q_s), (g_in, g_s), (k_in, k_s), (v_in, v_s)):
        for i, src in enumerate(ins):
            copies.append(
                pltpu.make_async_copy(src, dst.at[pl.ds(i * rows, rows), :], sem.at[len(copies)])
            )
    if not first:
        for src, dst in zip(acc_in, (dk_s, dv_s)):
            copies.append(pltpu.make_async_copy(src, dst, sem.at[len(copies)]))
    for c in copies:
        c.start()
    dq_s[...] = jnp.zeros_like(dq_s)
    if first:
        dk_s[...] = jnp.zeros_like(dk_s)
        dv_s[...] = jnp.zeros_like(dv_s)
    for c in copies:
        c.wait()
    scale = BLK ** (-0.5)
    masked = 0 in GROUPS[g]
    ahead = lax.broadcasted_iota(i32, (BLK, BLK), 1) - lax.broadcasted_iota(i32, (BLK, BLK), 0)
    across = (((1,), (1,)), ((), ()))
    down = (((0,), (0,)), ((), ()))

    def step(t, carry):
        entries = [list_ref[t * UNROLL + u] for u in range(UNROLL)]
        qs = [pl.ds(pl.multiple_of((e % 64) * BLK, BLK), BLK) for e in entries]
        ks = [pl.ds(pl.multiple_of((e // 64 % 16) * BLK, BLK), BLK) for e in entries]
        parts = []
        for e, q, k in zip(entries, qs, ks):
            rate = rate_ref[pl.ds(e // 1024 % 256, 1), :]
            s = lax.dot_general(k_s[k, :], q_s[q, :], across, preferred_element_type=f32) * scale
            sig = jax.nn.sigmoid(s)
            w = sig * rate
            if masked:
                w = jnp.where(ahead >= jnp.where(e >= 262144, 0, -BLK), w, 0.0)
            a = s * w
            da = lax.dot_general(v_s[k, :], g_s[q, :], across, preferred_element_type=f32)
            ds = (da * (w + a * (1.0 - sig))).astype(bf16)
            parts.append((a.astype(bf16), ds))
        sums = []
        for q, k, (a, ds) in zip(qs, ks, parts):
            dv = jnp.dot(a, g_s[q, :], preferred_element_type=f32)
            dk = jnp.dot(ds, q_s[q, :], preferred_element_type=f32)
            dq = lax.dot_general(ds, k_s[k, :], down, preferred_element_type=f32)
            sums.append((dq, dk, dv))
        for q, k, (dq, dk, dv) in zip(qs, ks, sums):
            dv_s[k, :] += dv
            dk_s[k, :] += dk
            dq_s[q, :] += dq
        return carry

    lax.fori_loop(0, (count_ref[g] + UNROLL - 1) // UNROLL, step, 0)
    for i, out in enumerate(dq_out):
        out[...] = dq_s[pl.ds(i * rows, rows), :].astype(out.dtype)
    if last:
        kv_out[0][pl.ds(0, rows), :] = dk_s[pl.ds(0, rows), :] * scale
        kv_out[1][pl.ds(0, rows), :] = dv_s[pl.ds(0, rows), :]
        for t in range(1, NY):
            kv_out[t + 1][pl.ds(0, rows), :] = dk_s[pl.ds(t * rows, rows), :].astype(bf16)
            kv_out[t + 1][pl.ds(rows, rows), :] = dv_s[pl.ds(t * rows, rows), :].astype(bf16)


def run_pairs(g, plan, q, gr, k, v, acc):
    rate, count, lists = plan[0], plan[1], plan[2:]
    first, last = g == 0, g == len(GROUPS) - 1
    n = len(GROUPS[g])
    rows = OWN * BLK
    smem = pl.BlockSpec(memory_space=pltpu.SMEM)
    vmem = pl.BlockSpec(memory_space=pltpu.VMEM)
    hbm = pl.BlockSpec(memory_space=pl.ANY)
    sds = jax.ShapeDtypeStruct
    outs = [sds((rows, BLK), f32 if s == 0 else bf16) for s in GROUPS[g]]
    if last:
        outs += [sds((rows, BLK), f32)] * 2 + [sds((2 * rows, BLK), bf16)] * (NY - 1)
    else:
        outs += [sds((NY * rows, BLK), f32)] * 2
    scratch = [
        pltpu.VMEM((n * rows, BLK), bf16),
        pltpu.VMEM((n * rows, BLK), bf16),
        pltpu.VMEM((NY * rows, BLK), bf16),
        pltpu.VMEM((NY * rows, BLK), bf16),
        pltpu.VMEM((n * rows, BLK), f32),
    ]
    if last:
        scratch += [pltpu.VMEM((NY * rows, BLK), f32)] * 2
    scratch.append(pltpu.SemaphoreType.DMA((2 * n + 2 * NY + 2,)))
    tiles = 4 * n
    return pl.pallas_call(
        functools.partial(pairs_kernel, g, first, last, n),
        out_shape=outs,
        in_specs=[smem, smem, vmem] + [hbm] * (2 * n + 2 * NY + len(acc)),
        out_specs=[vmem] * len(outs),
        scratch_shapes=scratch,
        compiler_params=pltpu.CompilerParams(vmem_limit_bytes=32 * 1024 * 1024),
        cost_estimate=pl.CostEstimate(
            flops=tiles * 10 * BLK**3, bytes_accessed=4_000_000, transcendentals=tiles * BLK * BLK
        ),
    )(count, lists[g], rate, *q, *gr, *k, *v, *acc)


def on_device(queries, keys, values, out_grad, block_mask, block_order):
    scale = BLK ** (-0.5)
    me = lax.axis_index("seq").astype(i32).reshape(1)
    plan = make_plan(me, block_order, block_mask)
    k = [keys] + [y_shift(keys, t) for t in range(1, NY)]
    v = [values] + [y_shift(values, t) for t in range(1, NY)]
    q, gr = {0: queries}, {0: out_grad}
    for s in range(1, NZ // 2):
        for part in (q, gr):
            part[s] = z_shift(part[s - 1], 1)
            part[NZ - s] = z_shift(part[(NZ - s + 1) % NZ], -1)
    half = NZ // 2
    q[half] = z_shift(q[half - 1], 1)
    gr[half] = z_shift(gr[half + 1], -1)

    back, acc = {}, ()
    for g, group in enumerate(GROUPS):
        out = run_pairs(g, plan, [q[s] for s in group], [gr[s] for s in group], k, v, acc)
        for s, dq in zip(group, out):
            back[s] = dq if s == 0 else z_shift(dq, -s)
        acc = tuple(out[len(group) :])
    own_k, own_v = acc[0], acc[1]
    kv_back = [y_shift(acc[t + 1], -t) for t in range(1, NY)]
    query_grad = sum(back[s].astype(f32) for s in range(NZ)) * scale
    rows = queries.shape[0]
    key_grad = own_k + sum(p[:rows].astype(f32) for p in kv_back) * scale
    value_grad = own_v + sum(p[rows:].astype(f32) for p in kv_back)
    return query_grad, key_grad, value_grad


def solution(mesh):
    whole = P(("rep", "seq"), "head")
    return jax.shard_map(
        on_device,
        mesh=mesh,
        in_specs=(whole, whole, whole, whole, P(), P()),
        out_specs=(whole, whole, whole),
        check_vma=False,
    )
```

time: 765 us -> 92.9 us (0.12)
  the two profiles are of different devices: /device:TPU:2 before, /device:TPU:32 now
where the time goes in v1:
time: 92.9 us; the launch traced here: 92.3 us
  starting transfers between devices  54.3 us (58%)
  waiting for transfers between devices  15.8 us (17%)
  Pallas kernels  15.4 us (17%)
  local copies, waits for them, and re-layouts  4.22 us (5%)
  other arithmetic  1.74 us (2%)
    ppermute x21, starting transfers between devices, z_shift(): return lax.ppermute(a, 'seq', route)  37.8 us
    ppermute x9, starting transfers between devices, y_shift(): return lax.ppermute(a, 'seq', route)  16.6 us
    pallas_call x1, Pallas kernels, run_pairs(): pl.pallas_call(functools.partial(pairs_kernel, g, first, last, n), out_sh...  9.52 us
    ppermute x21, waiting for transfers between devices, z_shift(): return lax.ppermute(a, 'seq', route)  8.89 us
    ppermute x9, waiting for transfers between devices, y_shift(): return lax.ppermute(a, 'seq', route)  6.91 us
    pallas_call x1, Pallas kernels, make_plan(): pl.pallas_call(plan_kernel, out_shape=[jax.ShapeDtypeStruct((BLK + 8, BLK...  5.9 us
    unnamed x12, local copies, waits for them, and re-layouts  4.22 us
  transfers between devices with their start and end apart: 30, of which 6 were waited for; matrix products, arithmetic and copies ran while one was open for 1% of the time, Pallas kernels for 6%

profile of v1, /device:TPU:32, one launch (start us, length us, event | category | flops | bytes accessed | tf_op | source)
XLA Modules:
  0.0 92.3 jit_solution(18221017465670552051)
XLA Ops:
  0.6 2.0 %collective-permute-start = (bf16[512,128]{1,0:T(8,128)(2,1)}, bf16[512,128]{1,0:T(8,128)(2,1)S(1)}, u32[]{:S(2)}, u32[]{:S(2)}) collective-permute-start(bf16[512,128]{1,0:T(8,128)(2,1)} %refs_3_.1), channel_id=1, source_target_pairs={{0,8},{8,16},{16,24},{24,32},{32,40},{40,48},{48,56},{56,0},{64,72... | collective-permute-start | bytes 393224 | tf_op jit(solution)/shard_map/ppermute | solution.py:27
  2.6 0.1 collective-permute-start.4
  2.7 1.9 %collective-permute-start.7 = (bf16[512,128]{1,0:T(8,128)(2,1)}, bf16[512,128]{1,0:T(8,128)(2,1)S(1)}, u32[]{:S(2)}, u32[]{:S(2)}) collective-permute-start(bf16[512,128]{1,0:T(8,128)(2,1)} %refs_11_.1), channel_id=1, source_target_pairs={{0,8},{8,16},{16,24},{24,32},{32,40},{40,48},{48,56},{56,0},{64,72... | collective-permute-start | bytes 393224 | tf_op jit(solution)/shard_map/ppermute | solution.py:27
  4.7 2.1 %collective-permute-start.10 = (bf16[512,128]{1,0:T(8,128)(2,1)}, bf16[512,128]{1,0:T(8,128)(2,1)S(1)}, u32[]{:S(2)}, u32[]{:S(2)}) collective-permute-start(bf16[512,128]{1,0:T(8,128)(2,1)} %refs_11_.1), channel_id=1, source_target_pairs={{0,56},{8,0},{16,8},{24,16},{32,24},{40,32},{48,40},{56,48},{64,12... | collective-permute-start | bytes 393224 | tf_op jit(solution)/shard_map/ppermute | solution.py:27
  6.8 3.2 %collective-permute-start.15 = (bf16[512,128]{1,0:T(8,128)(2,1)}, bf16[512,128]{1,0:T(8,128)(2,1)S(1)}, u32[]{:S(2)}, u32[]{:S(2)}) collective-permute-start(bf16[512,128]{1,0:T(8,128)(2,1)} %refs_19_.1), channel_id=1, source_target_pairs={{0,128},{8,136},{16,144},{24,152},{32,160},{40,168},{48,176},{56,1... | collective-permute-start | bytes 393224 | tf_op jit(solution)/shard_map/ppermute | solution.py:32
  10.0 0.0 collective-permute-done.refs_4_
  10.0 0.7 collective-permute-start.14
  10.7 0.0 collective-permute-done.4.refs_10_
  10.7 2.6 %collective-permute-start.16 = (bf16[512,128]{1,0:T(8,128)(2,1)}, bf16[512,128]{1,0:T(8,128)(2,1)S(1)}, u32[]{:S(2)}, u32[]{:S(2)}) collective-permute-start(bf16[512,128]{1,0:T(8,128)(2,1)} %refs_19_.1), channel_id=1, source_target_pairs={{0,192},{8,200},{16,208},{24,216},{32,224},{40,232},{48,240},{56,2... | collective-permute-start | bytes 393224 | tf_op jit(solution)/shard_map/ppermute | solution.py:32
  13.2 0.0 collective-permute-done.7.refs_12_
  13.2 0.2 collective-permute-start.18
  13.4 0.0 collective-permute-done.10.refs_18_
  13.4 1.5 %collective-permute-start.1 = (bf16[512,128]{1,0:T(8,128)(2,1)S(1)}, bf16[512,128]{1,0:T(8,128)(2,1)S(1)}, u32[]{:S(2)}, u32[]{:S(2)}) collective-permute-start(bf16[512,128]{1,0:T(8,128)(2,1)S(1)} %collective-permute-done.refs_4_), channel_id=1, source_target_pairs={{0,8},{8,16},{16,24},{24,32},{32,40},{40,48},{48,56},{56,0},{64,72... | collective-permute-start | bytes 393224 | tf_op jit(solution)/shard_map/ppermute | solution.py:27
  14.9 0.0 collective-permute-done.15.refs_21_
  14.9 3.3 %collective-permute-start.11 = (bf16[512,128]{1,0:T(8,128)(2,1)S(1)}, bf16[512,128]{1,0:T(8,128)(2,1)S(1)}, u32[]{:S(2)}, u32[]{:S(2)}) collective-permute-start(bf16[512,128]{1,0:T(8,128)(2,1)S(1)} %collective-permute-done.10.refs_18_), channel_id=1, source_target_pairs={{0,56},{8,0},{16,8},{24,16},{32,24},{40,32},{48,40},{56,48},{64,12... | collective-permute-start | bytes 393224 | tf_op jit(solution)/shard_map/ppermute | solution.py:27
  18.1 0.0 collective-permute-done.14.refs_20_
  18.1 1.6 %collective-permute-start.17 = (bf16[512,128]{1,0:T(8,128)(2,1)}, bf16[512,128]{1,0:T(8,128)(2,1)S(1)}, u32[]{:S(2)}, u32[]{:S(2)}) collective-permute-start(bf16[512,128]{1,0:T(8,128)(2,1)} %refs_23_.1), channel_id=1, source_target_pairs={{0,64},{8,72},{16,80},{24,88},{32,96},{40,104},{48,112},{56,120},{... | collective-permute-start | bytes 393224 | tf_op jit(solution)/shard_map/ppermute | solution.py:32
  19.8 0.0 collective-permute-done.16.refs_22_
  19.8 2.6 %collective-permute-start.5 = (bf16[512,128]{1,0:T(8,128)(2,1)S(1)}, bf16[512,128]{1,0:T(8,128)(2,1)S(1)}, u32[]{:S(2)}, u32[]{:S(2)}) collective-permute-start(bf16[512,128]{1,0:T(8,128)(2,1)S(1)} %collective-permute-done.4.refs_10_), channel_id=1, source_target_pairs={{0,56},{8,0},{16,8},{24,16},{32,24},{40,32},{48,40},{56,48},{64,12... | collective-permute-start | bytes 393224 | tf_op jit(solution)/shard_map/ppermute | solution.py:27
  22.4 0.0 collective-permute-done.18.refs_25_
  22.4 0.0 collective-permute-start.8
  22.4 0.0 collective-permute-done.1.refs_5_
  22.4 3.0 %collective-permute-start.2 = (bf16[512,128]{1,0:T(8,128)(2,1)S(1)}, bf16[512,128]{1,0:T(8,128)(2,1)S(1)}, u32[]{:S(2)}, u32[]{:S(2)}) collective-permute-start(bf16[512,128]{1,0:T(8,128)(2,1)S(1)} %collective-permute-done.1.refs_5_), channel_id=1, source_target_pairs={{0,8},{8,16},{16,24},{24,32},{32,40},{40,48},{48,56},{56,0},{64,72... | collective-permute-start | bytes 393224 | tf_op jit(solution)/shard_map/ppermute | solution.py:27
  25.4 0.0 collective-permute-done.11.refs_17_
  25.4 0.0 collective-permute-start.12
  25.4 0.0 collective-permute-done.17.refs_24_
  25.4 2.3 %collective-permute-start.19 = (bf16[512,128]{1,0:T(8,128)(2,1)}, bf16[512,128]{1,0:T(8,128)(2,1)S(1)}, u32[]{:S(2)}, u32[]{:S(2)}) collective-permute-start(bf16[512,128]{1,0:T(8,128)(2,1)} %refs_23_.1), channel_id=1, source_target_pairs={{0,192},{8,200},{16,208},{24,216},{32,224},{40,232},{48,240},{56,2... | collective-permute-start | bytes 393224 | tf_op jit(solution)/shard_map/ppermute | solution.py:32
  27.7 3.2 %collective-permute-start.6 = (bf16[512,128]{1,0:T(8,128)(2,1)S(1)}, bf16[512,128]{1,0:T(8,128)(2,1)S(1)}, u32[]{:S(2)}, u32[]{:S(2)}) collective-permute-start(bf16[512,128]{1,0:T(8,128)(2,1)S(1)} %collective-permute-done.5.refs_9_), channel_id=1, source_target_pairs={{0,56},{8,0},{16,8},{24,16},{32,24},{40,32},{48,40},{56,48},{64,12... | collective-permute-start | bytes 393224 | tf_op jit(solution)/shard_map/ppermute | solution.py:27
  30.9 0.0 collective-permute-done.8.refs_13_
  30.9 0.0 collective-permute-start.9
  30.9 0.0 collective-permute-done.2.refs_6_
  30.9 1.0 %collective-permute-start.3 = (bf16[512,128]{1,0:T(8,128)(2,1)S(1)}, bf16[512,128]{1,0:T(8,128)(2,1)S(1)}, u32[]{:S(2)}, u32[]{:S(2)}) collective-permute-start(bf16[512,128]{1,0:T(8,128)(2,1)S(1)} %collective-permute-done.2.refs_6_), channel_id=1, source_target_pairs={{0,8},{8,16},{16,24},{24,32},{32,40},{40,48},{48,56},{56,0},{64,72... | collective-permute-start | bytes 393224 | tf_op jit(solution)/shard_map/ppermute | solution.py:27
  31.9 0.0 collective-permute-done.12.refs_16_
  31.9 1.1 %collective-permute-start.13 = (bf16[512,128]{1,0:T(8,128)(2,1)S(1)}, bf16[512,128]{1,0:T(8,128)(2,1)S(1)}, u32[]{:S(2)}, u32[]{:S(2)}) collective-permute-start(bf16[512,128]{1,0:T(8,128)(2,1)S(1)} %collective-permute-done.12.refs_16_), channel_id=1, source_target_pairs={{0,56},{8,0},{16,8},{24,16},{32,24},{40,32},{48,40},{56,48},{64,12... | collective-permute-start | bytes 393224 | tf_op jit(solution)/shard_map/ppermute | solution.py:27
  33.0 5.9 %shard_map.85 = (f32[136,128]{1,0:T(8,128)}, s32[1]{0:T(128)}, s32[520]{0:T(1024)}) custom-call(s32[1]{0:T(128)} %bitcast.me_ref, s32[128]{0:T(128)} %order_ref.1, s32[128,128]{1,0:T(8,128)} %vmask_ref.1, s32[128,128]{1,0:T(8,128)} %vmask_ref.1), custom_call_target="tpu_custom_call" | custom-call | flops 10000 | bytes 200000 | tf_op jit(solution)/shard_map/pallas_call | solution.py:72
  38.9 0.0 copy-start.5
  38.9 0.0 collective-permute-done.9.refs_14_
  38.9 0.0 collective-permute-done.3.refs_7_
  39.0 0.6 copy-done.5
  39.6 0.9 copy-done.1
  40.5 0.9 copy-done.2
  41.4 0.9 copy-done.3
  42.3 0.9 copy-done.4
  43.2 9.5 %shard_map.86 = (f32[512,128]{1,0:T(8,128)S(1)}, bf16[512,128]{1,0:T(8,128)(2,1)S(1)}, bf16[512,128]{1,0:T(8,128)(2,1)S(1)}, bf16[512,128]{1,0:T(8,128)(2,1)S(1)...) custom-call(s32[1]{0:T(128)} %get-tuple-element.19.refs_0_, ...), custom_call_target="tpu_custom_call" | custom-call | flops 671088640 | bytes 4000000 | tf_op jit(solution)/shard_map/pallas_call | solution.py:185
  52.7 3.7 %collective-permute-start.20 = (bf16[512,128]{1,0:T(8,128)(2,1)S(1)}, bf16[512,128]{1,0:T(8,128)(2,1)S(1)}, u32[]{:S(2)}, u32[]{:S(2)}) collective-permute-start(bf16[512,128]{1,0:T(8,128)(2,1)S(1)} %get-tuple-element.23), channel_id=1, source_target_pairs={{0,56},{8,0},{16,8},{24,16},{32,24},{40,32},{48,40},{56,48},{64,12... | collective-permute-start | bytes 393224 | tf_op jit(solution)/shard_map/ppermute | solution.py:27
  56.5 0.9 collective-permute-start.21
  57.4 3.6 %collective-permute-start.22 = (bf16[512,128]{1,0:T(8,128)(2,1)S(1)}, bf16[512,128]{1,0:T(8,128)(2,1)S(1)}, u32[]{:S(2)}, u32[]{:S(2)}) collective-permute-start(bf16[512,128]{1,0:T(8,128)(2,1)S(1)} %get-tuple-element.25), channel_id=1, source_target_pairs={{0,40},{8,48},{16,56},{24,0},{32,8},{40,16},{48,24},{56,32},{64,10... | collective-permute-start | bytes 393224 | tf_op jit(solution)/shard_map/ppermute | solution.py:27
  60.9 1.6 %collective-permute-start.23 = (bf16[512,128]{1,0:T(8,128)(2,1)S(1)}, bf16[512,128]{1,0:T(8,128)(2,1)S(1)}, u32[]{:S(2)}, u32[]{:S(2)}) collective-permute-start(bf16[512,128]{1,0:T(8,128)(2,1)S(1)} %get-tuple-element.26), channel_id=1, source_target_pairs={{0,32},{8,40},{16,48},{24,56},{32,0},{40,8},{48,16},{56,24},{64,96... | collective-permute-start | bytes 393224 | tf_op jit(solution)/shard_map/ppermute | solution.py:27
  62.5 3.3 %collective-permute-start.24 = (bf16[512,128]{1,0:T(8,128)(2,1)S(1)}, bf16[512,128]{1,0:T(8,128)(2,1)S(1)}, u32[]{:S(2)}, u32[]{:S(2)}) collective-permute-start(bf16[512,128]{1,0:T(8,128)(2,1)S(1)} %get-tuple-element.27), channel_id=1, source_target_pairs={{0,24},{8,32},{16,40},{24,48},{32,56},{40,0},{48,8},{56,16},{64,88... | collective-permute-start | bytes 393224 | tf_op jit(solution)/shard_map/ppermute | solution.py:27
  65.9 2.9 %collective-permute-start.25 = (bf16[512,128]{1,0:T(8,128)(2,1)S(1)}, bf16[512,128]{1,0:T(8,128)(2,1)S(1)}, u32[]{:S(2)}, u32[]{:S(2)}) collective-permute-start(bf16[512,128]{1,0:T(8,128)(2,1)S(1)} %get-tuple-element.28), channel_id=1, source_target_pairs={{0,16},{8,24},{16,32},{24,40},{32,48},{40,56},{48,0},{56,8},{64,80... | collective-permute-start | bytes 393224 | tf_op jit(solution)/shard_map/ppermute | solution.py:27
  68.8 1.0 %collective-permute-done.21 = bf16[512,128]{1,0:T(8,128)(2,1)S(1)} collective-permute-done((bf16[512,128]{1,0:T(8,128)(2,1)S(1)}, bf16[512,128]{1,0:T(8,128)(2,1)S(1)}, u32[]{:S(2)}, u32[]{:S(2)}) %collective-permute-start.21) | collective-permute-done | bytes 131104 | tf_op jit(solution)/shard_map/ppermute | solution.py:27
  69.7 0.0 collective-permute-start.26
  69.8 4.0 %collective-permute-done.22 = bf16[512,128]{1,0:T(8,128)(2,1)S(1)} collective-permute-done((bf16[512,128]{1,0:T(8,128)(2,1)S(1)}, bf16[512,128]{1,0:T(8,128)(2,1)S(1)}, u32[]{:S(2)}, u32[]{:S(2)}) %collective-permute-start.22) | collective-permute-done | bytes 131104 | tf_op jit(solution)/shard_map/ppermute | solution.py:27
  73.8 3.4 %collective-permute-start.27 = (bf16[1024,128]{1,0:T(8,128)(2,1)S(1)}, bf16[1024,128]{1,0:T(8,128)(2,1)S(1)}, u32[]{:S(2)}, u32[]{:S(2)}) collective-permute-start(bf16[1024,128]{1,0:T(8,128)(2,1)S(1)} %get-tuple-element.31), channel_id=1, source_target_pairs={{0,192},{8,200},{16,208},{24,216},{32,224},{40,232},{48,240},{56,2... | collective-permute-start | bytes 786440 | tf_op jit(solution)/shard_map/ppermute | solution.py:32
  77.1 3.6 %collective-permute-done.23 = bf16[512,128]{1,0:T(8,128)(2,1)S(1)} collective-permute-done((bf16[512,128]{1,0:T(8,128)(2,1)S(1)}, bf16[512,128]{1,0:T(8,128)(2,1)S(1)}, u32[]{:S(2)}, u32[]{:S(2)}) %collective-permute-start.23) | collective-permute-done | bytes 131104 | tf_op jit(solution)/shard_map/ppermute | solution.py:27
  80.7 0.3 collective-permute-done.24
  81.0 2.7 %collective-permute-start.29 = (bf16[1024,128]{1,0:T(8,128)(2,1)S(1)}, bf16[1024,128]{1,0:T(8,128)(2,1)S(1)}, u32[]{:S(2)}, u32[]{:S(2)}) collective-permute-start(bf16[1024,128]{1,0:T(8,128)(2,1)S(1)} %get-tuple-element.33), channel_id=1, source_target_pairs={{0,64},{8,72},{16,80},{24,88},{32,96},{40,104},{48,112},{56,120},{... | collective-permute-start | bytes 786440 | tf_op jit(solution)/shard_map/ppermute | solution.py:32
  83.6 0.0 collective-permute-done.25
  83.6 0.0 collective-permute-done.26
  83.6 0.8 add_multiply_fusion
  84.5 0.0 collective-permute-done.27
  84.5 4.2 %collective-permute-done.28 = bf16[1024,128]{1,0:T(8,128)(2,1)S(1)} collective-permute-done((bf16[1024,128]{1,0:T(8,128)(2,1)S(1)}, bf16[1024,128]{1,0:T(8,128)(2,1)S(1)}, u32[]{:S(2)}, u32[]{:S(2)}) %collective-permute-start.28) | collective-permute-done | bytes 262176 | tf_op jit(solution)/shard_map/ppermute | solution.py:32
  88.7 2.7 %collective-permute-done.29 = bf16[1024,128]{1,0:T(8,128)(2,1)S(1)} collective-permute-done((bf16[1024,128]{1,0:T(8,128)(2,1)S(1)}, bf16[1024,128]{1,0:T(8,128)(2,1)S(1)}, u32[]{:S(2)}, u32[]{:S(2)}) %collective-permute-start.29) | collective-permute-done | bytes 262176 | tf_op jit(solution)/shard_map/ppermute | solution.py:32
  91.4 0.9 add_add_fusion
  (12 shorter events, 0.0 us)
Async XLA Ops:
  0.6 38.3 %copy-start = (bf16[512,128]{1,0:T(8,128)(2,1)S(1)}, bf16[512,128]{1,0:T(8,128)(2,1)}, u32[]{:S(2)}) copy-start(bf16[512,128]{1,0:T(8,128)(2,1)} %refs_3_.1) | copy-start | bytes 393220
  0.6 9.3 %collective-permute-start = (bf16[512,128]{1,0:T(8,128)(2,1)}, bf16[512,128]{1,0:T(8,128)(2,1)S(1)}, u32[]{:S(2)}, u32[]{:S(2)}) collective-permute-start(bf16[512,128]{1,0:T(8,128)(2,1)} %refs_3_.1), channel_id=1, source_target_pairs={{0,8},{8,16},{16,24},{24,32},{32,40},{40,48},{48,56},{56,0},{64,72... | collective-permute-start | bytes 393224 | tf_op jit(solution)/shard_map/ppermute | solution.py:27
  2.6 8.0 %collective-permute-start.4 = (bf16[512,128]{1,0:T(8,128)(2,1)}, bf16[512,128]{1,0:T(8,128)(2,1)S(1)}, u32[]{:S(2)}, u32[]{:S(2)}) collective-permute-start(bf16[512,128]{1,0:T(8,128)(2,1)} %refs_3_.1), channel_id=1, source_target_pairs={{0,56},{8,0},{16,8},{24,16},{32,24},{40,32},{48,40},{56,48},{64,12... | collective-permute-start | bytes 393224 | tf_op jit(solution)/shard_map/ppermute | solution.py:27
  2.7 10.5 %collective-permute-start.7 = (bf16[512,128]{1,0:T(8,128)(2,1)}, bf16[512,128]{1,0:T(8,128)(2,1)S(1)}, u32[]{:S(2)}, u32[]{:S(2)}) collective-permute-start(bf16[512,128]{1,0:T(8,128)(2,1)} %refs_11_.1), channel_id=1, source_target_pairs={{0,8},{8,16},{16,24},{24,32},{32,40},{40,48},{48,56},{56,0},{64,72... | collective-permute-start | bytes 393224 | tf_op jit(solution)/shard_map/ppermute | solution.py:27
  4.7 8.7 %collective-permute-start.10 = (bf16[512,128]{1,0:T(8,128)(2,1)}, bf16[512,128]{1,0:T(8,128)(2,1)S(1)}, u32[]{:S(2)}, u32[]{:S(2)}) collective-permute-start(bf16[512,128]{1,0:T(8,128)(2,1)} %refs_11_.1), channel_id=1, source_target_pairs={{0,56},{8,0},{16,8},{24,16},{32,24},{40,32},{48,40},{56,48},{64,12... | collective-permute-start | bytes 393224 | tf_op jit(solution)/shard_map/ppermute | solution.py:27
  6.8 8.1 %collective-permute-start.15 = (bf16[512,128]{1,0:T(8,128)(2,1)}, bf16[512,128]{1,0:T(8,128)(2,1)S(1)}, u32[]{:S(2)}, u32[]{:S(2)}) collective-permute-start(bf16[512,128]{1,0:T(8,128)(2,1)} %refs_19_.1), channel_id=1, source_target_pairs={{0,128},{8,136},{16,144},{24,152},{32,160},{40,168},{48,176},{56,1... | collective-permute-start | bytes 393224 | tf_op jit(solution)/shard_map/ppermute | solution.py:32
  10.0 8.2 %collective-permute-start.14 = (bf16[512,128]{1,0:T(8,128)(2,1)}, bf16[512,128]{1,0:T(8,128)(2,1)S(1)}, u32[]{:S(2)}, u32[]{:S(2)}) collective-permute-start(bf16[512,128]{1,0:T(8,128)(2,1)} %refs_19_.1), channel_id=1, source_target_pairs={{0,64},{8,72},{16,80},{24,88},{32,96},{40,104},{48,112},{56,120},{... | collective-permute-start | bytes 393224 | tf_op jit(solution)/shard_map/ppermute | solution.py:32
  10.7 9.1 %collective-permute-start.16 = (bf16[512,128]{1,0:T(8,128)(2,1)}, bf16[512,128]{1,0:T(8,128)(2,1)S(1)}, u32[]{:S(2)}, u32[]{:S(2)}) collective-permute-start(bf16[512,128]{1,0:T(8,128)(2,1)} %refs_19_.1), channel_id=1, source_target_pairs={{0,192},{8,200},{16,208},{24,216},{32,224},{40,232},{48,240},{56,2... | collective-permute-start | bytes 393224 | tf_op jit(solution)/shard_map/ppermute | solution.py:32
  13.2 9.2 %collective-permute-start.18 = (bf16[512,128]{1,0:T(8,128)(2,1)}, bf16[512,128]{1,0:T(8,128)(2,1)S(1)}, u32[]{:S(2)}, u32[]{:S(2)}) collective-permute-start(bf16[512,128]{1,0:T(8,128)(2,1)} %refs_23_.1), channel_id=1, source_target_pairs={{0,128},{8,136},{16,144},{24,152},{32,160},{40,168},{48,176},{56,1... | collective-permute-start | bytes 393224 | tf_op jit(solution)/shard_map/ppermute | solution.py:32
  13.4 9.0 %collective-permute-start.1 = (bf16[512,128]{1,0:T(8,128)(2,1)S(1)}, bf16[512,128]{1,0:T(8,128)(2,1)S(1)}, u32[]{:S(2)}, u32[]{:S(2)}) collective-permute-start(bf16[512,128]{1,0:T(8,128)(2,1)S(1)} %collective-permute-done.refs_4_), channel_id=1, source_target_pairs={{0,8},{8,16},{16,24},{24,32},{32,40},{40,48},{48,56},{56,0},{64,72... | collective-permute-start | bytes 393224 | tf_op jit(solution)/shard_map/ppermute | solution.py:27
  14.9 10.6 %collective-permute-start.11 = (bf16[512,128]{1,0:T(8,128)(2,1)S(1)}, bf16[512,128]{1,0:T(8,128)(2,1)S(1)}, u32[]{:S(2)}, u32[]{:S(2)}) collective-permute-start(bf16[512,128]{1,0:T(8,128)(2,1)S(1)} %collective-permute-done.10.refs_18_), channel_id=1, source_target_pairs={{0,56},{8,0},{16,8},{24,16},{32,24},{40,32},{48,40},{56,48},{64,12... | collective-permute-start | bytes 393224 | tf_op jit(solution)/shard_map/ppermute | solution.py:27
  18.1 7.3 %collective-permute-start.17 = (bf16[512,128]{1,0:T(8,128)(2,1)}, bf16[512,128]{1,0:T(8,128)(2,1)S(1)}, u32[]{:S(2)}, u32[]{:S(2)}) collective-permute-start(bf16[512,128]{1,0:T(8,128)(2,1)} %refs_23_.1), channel_id=1, source_target_pairs={{0,64},{8,72},{16,80},{24,88},{32,96},{40,104},{48,112},{56,120},{... | collective-permute-start | bytes 393224 | tf_op jit(solution)/shard_map/ppermute | solution.py:32
  19.8 7.9 %collective-permute-start.5 = (bf16[512,128]{1,0:T(8,128)(2,1)S(1)}, bf16[512,128]{1,0:T(8,128)(2,1)S(1)}, u32[]{:S(2)}, u32[]{:S(2)}) collective-permute-start(bf16[512,128]{1,0:T(8,128)(2,1)S(1)} %collective-permute-done.4.refs_10_), channel_id=1, source_target_pairs={{0,56},{8,0},{16,8},{24,16},{32,24},{40,32},{48,40},{56,48},{64,12... | collective-permute-start | bytes 393224 | tf_op jit(solution)/shard_map/ppermute | solution.py:27
  22.4 8.5 %collective-permute-start.8 = (bf16[512,128]{1,0:T(8,128)(2,1)S(1)}, bf16[512,128]{1,0:T(8,128)(2,1)S(1)}, u32[]{:S(2)}, u32[]{:S(2)}) collective-permute-start(bf16[512,128]{1,0:T(8,128)(2,1)S(1)} %collective-permute-done.7.refs_12_), channel_id=1, source_target_pairs={{0,8},{8,16},{16,24},{24,32},{32,40},{40,48},{48,56},{56,0},{64,72... | collective-permute-start | bytes 393224 | tf_op jit(solution)/shard_map/ppermute | solution.py:27
  22.4 8.5 %collective-permute-start.2 = (bf16[512,128]{1,0:T(8,128)(2,1)S(1)}, bf16[512,128]{1,0:T(8,128)(2,1)S(1)}, u32[]{:S(2)}, u32[]{:S(2)}) collective-permute-start(bf16[512,128]{1,0:T(8,128)(2,1)S(1)} %collective-permute-done.1.refs_5_), channel_id=1, source_target_pairs={{0,8},{8,16},{16,24},{24,32},{32,40},{40,48},{48,56},{56,0},{64,72... | collective-permute-start | bytes 393224 | tf_op jit(solution)/shard_map/ppermute | solution.py:27
  25.4 6.5 %collective-permute-start.12 = (bf16[512,128]{1,0:T(8,128)(2,1)S(1)}, bf16[512,128]{1,0:T(8,128)(2,1)S(1)}, u32[]{:S(2)}, u32[]{:S(2)}) collective-permute-start(bf16[512,128]{1,0:T(8,128)(2,1)S(1)} %collective-permute-done.11.refs_17_), channel_id=1, source_target_pairs={{0,56},{8,0},{16,8},{24,16},{32,24},{40,32},{48,40},{56,48},{64,12... | collective-permute-start | bytes 393224 | tf_op jit(solution)/shard_map/ppermute | solution.py:27
  25.4 13.5 %collective-permute-start.19 = (bf16[512,128]{1,0:T(8,128)(2,1)}, bf16[512,128]{1,0:T(8,128)(2,1)S(1)}, u32[]{:S(2)}, u32[]{:S(2)}) collective-permute-start(bf16[512,128]{1,0:T(8,128)(2,1)} %refs_23_.1), channel_id=1, source_target_pairs={{0,192},{8,200},{16,208},{24,216},{32,224},{40,232},{48,240},{56,2... | collective-permute-start | bytes 393224 | tf_op jit(solution)/shard_map/ppermute | solution.py:32
  27.7 11.2 %collective-permute-start.6 = (bf16[512,128]{1,0:T(8,128)(2,1)S(1)}, bf16[512,128]{1,0:T(8,128)(2,1)S(1)}, u32[]{:S(2)}, u32[]{:S(2)}) collective-permute-start(bf16[512,128]{1,0:T(8,128)(2,1)S(1)} %collective-permute-done.5.refs_9_), channel_id=1, source_target_pairs={{0,56},{8,0},{16,8},{24,16},{32,24},{40,32},{48,40},{56,48},{64,12... | collective-permute-start | bytes 393224 | tf_op jit(solution)/shard_map/ppermute | solution.py:27
  30.9 8.1 %collective-permute-start.9 = (bf16[512,128]{1,0:T(8,128)(2,1)S(1)}, bf16[512,128]{1,0:T(8,128)(2,1)S(1)}, u32[]{:S(2)}, u32[]{:S(2)}) collective-permute-start(bf16[512,128]{1,0:T(8,128)(2,1)S(1)} %collective-permute-done.8.refs_13_), channel_id=1, source_target_pairs={{0,8},{8,16},{16,24},{24,32},{32,40},{40,48},{48,56},{56,0},{64,72... | collective-permute-start | bytes 393224 | tf_op jit(solution)/shard_map/ppermute | solution.py:27
  30.9 8.1 %collective-permute-start.3 = (bf16[512,128]{1,0:T(8,128)(2,1)S(1)}, bf16[512,128]{1,0:T(8,128)(2,1)S(1)}, u32[]{:S(2)}, u32[]{:S(2)}) collective-permute-start(bf16[512,128]{1,0:T(8,128)(2,1)S(1)} %collective-permute-done.2.refs_6_), channel_id=1, source_target_pairs={{0,8},{8,16},{16,24},{24,32},{32,40},{40,48},{48,56},{56,0},{64,72... | collective-permute-start | bytes 393224 | tf_op jit(solution)/shard_map/ppermute | solution.py:27
  31.9 7.1 %collective-permute-start.13 = (bf16[512,128]{1,0:T(8,128)(2,1)S(1)}, bf16[512,128]{1,0:T(8,128)(2,1)S(1)}, u32[]{:S(2)}, u32[]{:S(2)}) collective-permute-start(bf16[512,128]{1,0:T(8,128)(2,1)S(1)} %collective-permute-done.12.refs_16_), channel_id=1, source_target_pairs={{0,56},{8,0},{16,8},{24,16},{32,24},{40,32},{48,40},{56,48},{64,12... | collective-permute-start | bytes 393224 | tf_op jit(solution)/shard_map/ppermute | solution.py:27
  38.9 0.7 copy-start.5
  39.6 0.9 copy-start.1
  40.5 0.9 copy-start.2
  41.4 0.9 copy-start.3
  42.3 0.9 copy-start.4
  52.7 13.1 %collective-permute-start.20 = (bf16[512,128]{1,0:T(8,128)(2,1)S(1)}, bf16[512,128]{1,0:T(8,128)(2,1)S(1)}, u32[]{:S(2)}, u32[]{:S(2)}) collective-permute-start(bf16[512,128]{1,0:T(8,128)(2,1)S(1)} %get-tuple-element.23), channel_id=1, source_target_pairs={{0,56},{8,0},{16,8},{24,16},{32,24},{40,32},{48,40},{56,48},{64,12... | collective-permute-start | bytes 393224 | tf_op jit(solution)/shard_map/ppermute | solution.py:27
  56.5 13.3 %collective-permute-start.21 = (bf16[512,128]{1,0:T(8,128)(2,1)S(1)}, bf16[512,128]{1,0:T(8,128)(2,1)S(1)}, u32[]{:S(2)}, u32[]{:S(2)}) collective-permute-start(bf16[512,128]{1,0:T(8,128)(2,1)S(1)} %get-tuple-element.24), channel_id=1, source_target_pairs={{0,48},{8,56},{16,0},{24,8},{32,16},{40,24},{48,32},{56,40},{64,11... | collective-permute-start | bytes 393224 | tf_op jit(solution)/shard_map/ppermute | solution.py:27
  57.4 16.4 %collective-permute-start.22 = (bf16[512,128]{1,0:T(8,128)(2,1)S(1)}, bf16[512,128]{1,0:T(8,128)(2,1)S(1)}, u32[]{:S(2)}, u32[]{:S(2)}) collective-permute-start(bf16[512,128]{1,0:T(8,128)(2,1)S(1)} %get-tuple-element.25), channel_id=1, source_target_pairs={{0,40},{8,48},{16,56},{24,0},{32,8},{40,16},{48,24},{56,32},{64,10... | collective-permute-start | bytes 393224 | tf_op jit(solution)/shard_map/ppermute | solution.py:27
  60.9 19.8 %collective-permute-start.23 = (bf16[512,128]{1,0:T(8,128)(2,1)S(1)}, bf16[512,128]{1,0:T(8,128)(2,1)S(1)}, u32[]{:S(2)}, u32[]{:S(2)}) collective-permute-start(bf16[512,128]{1,0:T(8,128)(2,1)S(1)} %get-tuple-element.26), channel_id=1, source_target_pairs={{0,32},{8,40},{16,48},{24,56},{32,0},{40,8},{48,16},{56,24},{64,96... | collective-permute-start | bytes 393224 | tf_op jit(solution)/shard_map/ppermute | solution.py:27
  62.5 18.5 %collective-permute-start.24 = (bf16[512,128]{1,0:T(8,128)(2,1)S(1)}, bf16[512,128]{1,0:T(8,128)(2,1)S(1)}, u32[]{:S(2)}, u32[]{:S(2)}) collective-permute-start(bf16[512,128]{1,0:T(8,128)(2,1)S(1)} %get-tuple-element.27), channel_id=1, source_target_pairs={{0,24},{8,32},{16,40},{24,48},{32,56},{40,0},{48,8},{56,16},{64,88... | collective-permute-start | bytes 393224 | tf_op jit(solution)/shard_map/ppermute | solution.py:27
  65.9 17.8 %collective-permute-start.25 = (bf16[512,128]{1,0:T(8,128)(2,1)S(1)}, bf16[512,128]{1,0:T(8,128)(2,1)S(1)}, u32[]{:S(2)}, u32[]{:S(2)}) collective-permute-start(bf16[512,128]{1,0:T(8,128)(2,1)S(1)} %get-tuple-element.28), channel_id=1, source_target_pairs={{0,16},{8,24},{16,32},{24,40},{32,48},{40,56},{48,0},{56,8},{64,80... | collective-permute-start | bytes 393224 | tf_op jit(solution)/shard_map/ppermute | solution.py:27
  69.7 13.9 %collective-permute-start.26 = (bf16[512,128]{1,0:T(8,128)(2,1)S(1)}, bf16[512,128]{1,0:T(8,128)(2,1)S(1)}, u32[]{:S(2)}, u32[]{:S(2)}) collective-permute-start(bf16[512,128]{1,0:T(8,128)(2,1)S(1)} %get-tuple-element.29), channel_id=1, source_target_pairs={{0,8},{8,16},{16,24},{24,32},{32,40},{40,48},{48,56},{56,0},{64,72... | collective-permute-start | bytes 393224 | tf_op jit(solution)/shard_map/ppermute | solution.py:27
  73.8 10.7 %collective-permute-start.27 = (bf16[1024,128]{1,0:T(8,128)(2,1)S(1)}, bf16[1024,128]{1,0:T(8,128)(2,1)S(1)}, u32[]{:S(2)}, u32[]{:S(2)}) collective-permute-start(bf16[1024,128]{1,0:T(8,128)(2,1)S(1)} %get-tuple-element.31), channel_id=1, source_target_pairs={{0,192},{8,200},{16,208},{24,216},{32,224},{40,232},{48,240},{56,2... | collective-permute-start | bytes 786440 | tf_op jit(solution)/shard_map/ppermute | solution.py:32
  80.7 8.0 %collective-permute-start.28 = (bf16[1024,128]{1,0:T(8,128)(2,1)S(1)}, bf16[1024,128]{1,0:T(8,128)(2,1)S(1)}, u32[]{:S(2)}, u32[]{:S(2)}) collective-permute-start(bf16[1024,128]{1,0:T(8,128)(2,1)S(1)} %get-tuple-element.32), channel_id=1, source_target_pairs={{0,128},{8,136},{16,144},{24,152},{32,160},{40,168},{48,176},{56,1... | collective-permute-start | bytes 786440 | tf_op jit(solution)/shard_map/ppermute | solution.py:32
  81.0 10.4 %collective-permute-start.29 = (bf16[1024,128]{1,0:T(8,128)(2,1)S(1)}, bf16[1024,128]{1,0:T(8,128)(2,1)S(1)}, u32[]{:S(2)}, u32[]{:S(2)}) collective-permute-start(bf16[1024,128]{1,0:T(8,128)(2,1)S(1)} %get-tuple-element.33), channel_id=1, source_target_pairs={{0,64},{8,72},{16,80},{24,88},{32,96},{40,104},{48,112},{56,120},{... | collective-permute-start | bytes 786440 | tf_op jit(solution)/shard_map/ppermute | solution.py:32

commit v2 on v1

--- a/solution.py
+++ b/solution.py
@@ -12,9 +12,9 @@
 NY = 4
 OWN = 4
 NK = NY * OWN
-UNROLL = 4
+UNROLL = 8
 SPARE = 8
-GROUPS = ((0, 1, 2, 3, 4, 5, 6, 7),)
+GROUPS = ((0, 1, 7, 2, 6), (3, 5, 4))
 bf16, f32, i32 = jnp.bfloat16, jnp.float32, jnp.int32
 
 
@@ -35,21 +35,23 @@
 def plan_kernel(me_ref, order_ref, smask_ref, vmask_ref, rate_ref, count_ref, *list_refs):
     me = me_ref[0]
     y, z = me // NZ, me % NZ
+    kfirsts = [((y - t + NY) % NY * NZ + z) * OWN for t in range(NY)]
+    bks = [order_ref[kfirsts[t] + j] for t in range(NY) for j in range(OWN)]
     for g, (group, out) in enumerate(zip(GROUPS, list_refs)):
         n = jnp.int32(0)
         for place, slot in enumerate(group):
             first = (y * NZ + (z - slot + NZ) % NZ) * OWN
 
-            def row(i, n, place=place, first=first, out=out):
+            def row(i, n, place=place, slot=slot, first=first, out=out):
                 bq = order_ref[first + i]
-                for t in range(NY):
-                    kfirst = ((y - t + NY) % NY * NZ + z) * OWN
-                    for j in range(OWN):
-                        bk = order_ref[kfirst + j]
-                        live = jnp.where((smask_ref[bq, bk] > 0) & (bk <= bq), 1, 0)
-                        diag = jnp.where(bk == bq, 1, 0)
-                        out[n] = (place * OWN + i) + (t * OWN + j) * 64 + bq * 1024 + diag * 262144
-                        n = n + live
+                head = place * OWN + i + bq * 1024
+                for c, bk in enumerate(bks):
+                    live = (smask_ref[bq, bk] > 0) & (bk <= bq)
+                    entry = head + c * 64
+                    if slot == 0 and c < OWN:
+                        entry = entry + jnp.where(bk == bq, 262144, 0)
+                    out[n] = entry
+                    n = n + jnp.where(live, 1, 0)
                 return n
 
             n = lax.fori_loop(0, OWN, row, n)
@@ -64,6 +66,29 @@
     count = below * float(BLK) + diag * (ids_c + 1).astype(f32)
     rate_ref[pl.ds(0, BLK), :] = 1.0 / jnp.sqrt(jnp.maximum(count, 1.0))
     rate_ref[pl.ds(BLK, 8), :] = jnp.zeros((8, BLK), f32)
+
+
+def stack_kernel(a_ref, b_ref, ab_ref, sem):
+    rows = a_ref.shape[0]
+    copies = [
+        pltpu.make_async_copy(src, ab_ref.at[pl.ds(i * rows, rows), :], sem.at[i])
+        for i, src in enumerate((a_ref, b_ref))
+    ]
+    for c in copies:
+        c.start()
+    for c in copies:
+        c.wait()
+
+
+def stack_pair(a, b):
+    return pl.pallas_call(
+        stack_kernel,
+        out_shape=jax.ShapeDtypeStruct((2 * a.shape[0], a.shape[1]), a.dtype),
+        in_specs=[pl.BlockSpec(memory_space=pltpu.HBM)] * 2,
+        out_specs=pl.BlockSpec(memory_space=pltpu.VMEM),
+        scratch_shapes=[pltpu.SemaphoreType.DMA((2,))],
+        cost_estimate=pl.CostEstimate(flops=0, bytes_accessed=500_000, transcendentals=0),
+    )(a, b)
 
 
 def make_plan(me, block_order, block_mask):
@@ -82,36 +107,34 @@
     )(me, block_order, block_mask, block_mask)
 
 
-def pairs_kernel(g, first, last, n_slots, *refs):
+def pairs_kernel(g, first, last, row_parts, *refs):
     refs = list(refs)
     take = lambda n: [refs.pop(0) for _ in range(n)]
+    n_slots = len(GROUPS[g])
     count_ref, list_ref, rate_ref = take(3)
-    q_in, g_in = take(n_slots), take(n_slots)
-    k_in, v_in = take(NY), take(NY)
+    row_in = take(len(row_parts))
+    kv_in = take(NY)
     acc_in = [] if first else take(2)
     dq_out = take(n_slots)
     kv_out = take(NY + 1) if last else take(2)
     q_s, g_s, k_s, v_s, dq_s = take(5)
     dk_s, dv_s = take(2) if last else kv_out
-    sem = take(1)[0]
     rows = OWN * BLK
-    copies = []
-    for ins, dst in ((q_in, q_s), (g_in, g_s), (k_in, k_s), (v_in, v_s)):
-        for i, src in enumerate(ins):
-            copies.append(
-                pltpu.make_async_copy(src, dst.at[pl.ds(i * rows, rows), :], sem.at[len(copies)])
-            )
-    if not first:
-        for src, dst in zip(acc_in, (dk_s, dv_s)):
-            copies.append(pltpu.make_async_copy(src, dst, sem.at[len(copies)]))
-    for c in copies:
-        c.start()
+
+    def fetch(src, at, dst, place):
+        dst[pl.ds(place * rows, rows), :] = src[pl.ds(at, rows), :]
+
+    for src, (place, kind) in zip(row_in, row_parts):
+        if kind != "g":
+            fetch(src, 0, q_s, place)
+        if kind != "q":
+            fetch(src, rows if kind == "qg" else 0, g_s, place)
+    for t, src in enumerate(kv_in):
+        fetch(src, 0, k_s, t)
+        fetch(src, rows, v_s, t)
     dq_s[...] = jnp.zeros_like(dq_s)
-    if first:
-        dk_s[...] = jnp.zeros_like(dk_s)
-        dv_s[...] = jnp.zeros_like(dv_s)
-    for c in copies:
-        c.wait()
+    dk_s[...] = jnp.zeros_like(dk_s)
+    dv_s[...] = jnp.zeros_like(dv_s)
     scale = BLK ** (-0.5)
     masked = 0 in GROUPS[g]
     ahead = lax.broadcasted_iota(i32, (BLK, BLK), 1) - lax.broadcasted_iota(i32, (BLK, BLK), 0)
@@ -150,22 +173,33 @@
     for i, out in enumerate(dq_out):
         out[...] = dq_s[pl.ds(i * rows, rows), :].astype(out.dtype)
     if last:
-        kv_out[0][pl.ds(0, rows), :] = dk_s[pl.ds(0, rows), :] * scale
-        kv_out[1][pl.ds(0, rows), :] = dv_s[pl.ds(0, rows), :]
-        for t in range(1, NY):
-            kv_out[t + 1][pl.ds(0, rows), :] = dk_s[pl.ds(t * rows, rows), :].astype(bf16)
-            kv_out[t + 1][pl.ds(rows, rows), :] = dv_s[pl.ds(t * rows, rows), :].astype(bf16)
-
-
-def run_pairs(g, plan, q, gr, k, v, acc):
+        for t in range(NY):
+            own = pl.ds(t * rows, rows)
+            dk, dv = [
+                sum((p[own, :] for p in earlier), s[own, :])
+                for s, earlier in ((dk_s, acc_in[:1]), (dv_s, acc_in[1:]))
+            ]
+            if t == 0:
+                kv_out[0][...] = dk * scale
+                kv_out[1][...] = dv
+            else:
+                kv_out[t + 1][pl.ds(0, rows), :] = dk.astype(bf16)
+                kv_out[t + 1][pl.ds(rows, rows), :] = dv.astype(bf16)
+
+
+def run_pairs(g, plan, row_shards, kv, acc):
     rate, count, lists = plan[0], plan[1], plan[2:]
     first, last = g == 0, g == len(GROUPS) - 1
     n = len(GROUPS[g])
     rows = OWN * BLK
     smem = pl.BlockSpec(memory_space=pltpu.SMEM)
     vmem = pl.BlockSpec(memory_space=pltpu.VMEM)
-    hbm = pl.BlockSpec(memory_space=pl.ANY)
     sds = jax.ShapeDtypeStruct
+    row_parts, row_arrays = [], []
+    for place, s in enumerate(GROUPS[g]):
+        for kind, array in row_shards[s].items():
+            row_parts.append((place, kind))
+            row_arrays.append(array)
     outs = [sds((rows, BLK), f32 if s == 0 else bf16) for s in GROUPS[g]]
     if last:
         outs += [sds((rows, BLK), f32)] * 2 + [sds((2 * rows, BLK), bf16)] * (NY - 1)
@@ -180,46 +214,51 @@
     ]
     if last:
         scratch += [pltpu.VMEM((NY * rows, BLK), f32)] * 2
-    scratch.append(pltpu.SemaphoreType.DMA((2 * n + 2 * NY + 2,)))
     tiles = 4 * n
     return pl.pallas_call(
-        functools.partial(pairs_kernel, g, first, last, n),
+        functools.partial(pairs_kernel, g, first, last, row_parts),
         out_shape=outs,
-        in_specs=[smem, smem, vmem] + [hbm] * (2 * n + 2 * NY + len(acc)),
+        in_specs=[smem, smem] + [vmem] * (1 + len(row_arrays) + NY + len(acc)),
         out_specs=[vmem] * len(outs),
         scratch_shapes=scratch,
         compiler_params=pltpu.CompilerParams(vmem_limit_bytes=32 * 1024 * 1024),
         cost_estimate=pl.CostEstimate(
             flops=tiles * 10 * BLK**3, bytes_accessed=4_000_000, transcendentals=tiles * BLK * BLK
         ),
-    )(count, lists[g], rate, *q, *gr, *k, *v, *acc)
+    )(count, lists[g], rate, *row_arrays, *kv, *acc)
 
 
 def on_device(queries, keys, values, out_grad, block_mask, block_order):
     scale = BLK ** (-0.5)
+    rows = queries.shape[0]
     me = lax.axis_index("seq").astype(i32).reshape(1)
     plan = make_plan(me, block_order, block_mask)
-    k = [keys] + [y_shift(keys, t) for t in range(1, NY)]
-    v = [values] + [y_shift(values, t) for t in range(1, NY)]
-    q, gr = {0: queries}, {0: out_grad}
-    for s in range(1, NZ // 2):
-        for part in (q, gr):
-            part[s] = z_shift(part[s - 1], 1)
-            part[NZ - s] = z_shift(part[(NZ - s + 1) % NZ], -1)
-    half = NZ // 2
-    q[half] = z_shift(q[half - 1], 1)
-    gr[half] = z_shift(gr[half + 1], -1)
-
+    qg, kv = stack_pair(queries, out_grad), stack_pair(keys, values)
+    ahead, behind = z_shift(qg, 1), z_shift(qg, -1)
+    kvs = [kv] + [y_shift(kv, t) for t in (1, 3, 2)]
+    kvs = [kvs[0], kvs[1], kvs[3], kvs[2]]
+    (ahead, behind), plan = lax.optimization_barrier(((ahead, behind), plan))
+    shards = {0: {"qg": qg}, 1: {"qg": ahead}, NZ - 1: {"qg": behind}}
+    split = lambda a: {"q": a[:rows], "g": a[rows:]}
+    ahead, behind = split(ahead), split(behind)
+    for s in range(2, NZ // 2):
+        ahead = {kind: z_shift(a, 1) for kind, a in ahead.items()}
+        behind = {kind: z_shift(a, -1) for kind, a in behind.items()}
+        shards[s], shards[NZ - s] = ahead, behind
     back, acc = {}, ()
     for g, group in enumerate(GROUPS):
-        out = run_pairs(g, plan, [q[s] for s in group], [gr[s] for s in group], k, v, acc)
-        for s, dq in zip(group, out):
+        out = run_pairs(g, plan, shards, kvs, acc)
+        if g == 0:
+            ahead, behind, out = lax.optimization_barrier((ahead, behind, out))
+            shards[NZ // 2 - 1], shards[NZ // 2 + 1] = ahead, behind
+            shards[NZ // 2] = {"q": z_shift(ahead["q"], 1), "g": z_shift(behind["g"], -1)}
+        acc = tuple(out[len(group) :])
+        if g == len(GROUPS) - 1:
+            kv_back = [y_shift(acc[t + 1], -t) for t in (2, 1, 3)]
+        for s, dq in reversed(list(zip(group, out))):
             back[s] = dq if s == 0 else z_shift(dq, -s)
-        acc = tuple(out[len(group) :])
     own_k, own_v = acc[0], acc[1]
-    kv_back = [y_shift(acc[t + 1], -t) for t in range(1, NY)]
     query_grad = sum(back[s].astype(f32) for s in range(NZ)) * scale
-    rows = queries.shape[0]
     key_grad = own_k + sum(p[:rows].astype(f32) for p in kv_back) * scale
     value_grad = own_v + sum(p[rows:].astype(f32) for p in kv_back)
     return query_grad, key_grad, value_grad

time: 92.9 us -> 75.9 us (0.82)
  the two profiles are of different devices: /device:TPU:32 before, /device:TPU:2 now
where the time goes in v2:
time: 75.9 us; the launch traced here: 75.1 us
  starting transfers between devices  42.1 us (55%)
  waiting for transfers between devices  17.7 us (23%)
  Pallas kernels  12.7 us (17%)
  other arithmetic  1.74 us (2%)
  between operations  0.83 us (1%)
    ppermute x19, starting transfers between devices, z_shift(): return lax.ppermute(a, 'seq', route)  34.5 us
    ppermute x19, waiting for transfers between devices, z_shift(): return lax.ppermute(a, 'seq', route)  11.5 us
    ppermute x6, starting transfers between devices, y_shift(): return lax.ppermute(a, 'seq', route)  7.62 us
    ppermute x6, waiting for transfers between devices, y_shift(): return lax.ppermute(a, 'seq', route)  6.23 us
    pallas_call x1, Pallas kernels, make_plan(): pl.pallas_call(plan_kernel, out_shape=[jax.ShapeDtypeStruct((BLK + 8, BLK...  4.99 us
    pallas_call x2, Pallas kernels, run_pairs(): pl.pallas_call(functools.partial(pairs_kernel, g, first, last, row_parts)...  4.3 us
    pallas_call x2, Pallas kernels, stack_pair(): pl.pallas_call(stack_kernel, out_shape=jax.ShapeDtypeStruct((2 * a.shape[...  3.37 us
  transfers between devices with their start and end apart: 25, of which 9 were waited for; matrix products, arithmetic and copies ran while one was open for 1% of the time, Pallas kernels for 15%

profile of v2, /device:TPU:2, one launch (start us, length us, event | category | flops | bytes accessed | tf_op | source)
XLA Modules:
  0.0 75.1 jit_solution(15060128554693126769)
XLA Ops:
  0.6 1.7 %shard_map.85.refs_3_ = bf16[1024,128]{1,0:T(8,128)(2,1)} custom-call(bf16[512,128]{1,0:T(8,128)(2,1)} %a_ref.2, bf16[512,128]{1,0:T(8,128)(2,1)} %b_ref.2), custom_call_target="tpu_custom_call" | custom-call | bytes 500000 | tf_op jit(solution)/shard_map/pallas_call | solution.py:84
  2.3 5.9 %collective-permute-start.1 = (bf16[1024,128]{1,0:T(8,128)(2,1)}, bf16[1024,128]{1,0:T(8,128)(2,1)S(1)}, u32[]{:S(2)}, u32[]{:S(2)}) collective-permute-start(bf16[1024,128]{1,0:T(8,128)(2,1)} %shard_map.85.refs_3_), channel_id=1, source_target_pairs={{0,56},{8,0},{16,8},{24,16},{32,24},{40,32},{48,40},{56,48},{64,12... | collective-permute-start | bytes 786440 | tf_op jit(solution)/shard_map/ppermute | solution.py:27
  8.3 0.0 collective-permute-start
  8.3 1.7 %shard_map.87.refs_10_.refs_9_ = bf16[1024,128]{1,0:T(8,128)(2,1)} custom-call(bf16[512,128]{1,0:T(8,128)(2,1)} %a_ref.3, bf16[512,128]{1,0:T(8,128)(2,1)} %b_ref.3), custom_call_target="tpu_custom_call" | custom-call | bytes 500000 | tf_op jit(solution)/shard_map/pallas_call | solution.py:84
  10.0 3.1 %collective-permute-start.12 = (bf16[1024,128]{1,0:T(8,128)(2,1)}, bf16[1024,128]{1,0:T(8,128)(2,1)S(1)}, u32[]{:S(2)}, u32[]{:S(2)}) collective-permute-start(bf16[1024,128]{1,0:T(8,128)(2,1)} %shard_map.87.refs_10_.refs_9_), channel_id=1, source_target_pairs={{0,192},{8,200},{16,208},{24,216},{32,224},{40,232},{48,240},{56,2... | collective-permute-start | bytes 786440 | tf_op jit(solution)/shard_map/ppermute | solution.py:32
  13.0 0.6 collective-permute-start.11
  13.7 1.0 %collective-permute-start.10 = (bf16[1024,128]{1,0:T(8,128)(2,1)}, bf16[1024,128]{1,0:T(8,128)(2,1)S(1)}, u32[]{:S(2)}, u32[]{:S(2)}) collective-permute-start(bf16[1024,128]{1,0:T(8,128)(2,1)} %shard_map.87.refs_10_.refs_9_), channel_id=1, source_target_pairs={{0,64},{8,72},{16,80},{24,88},{32,96},{40,104},{48,112},{56,120},{... | collective-permute-start | bytes 786440 | tf_op jit(solution)/shard_map/ppermute | solution.py:32
  14.6 5.0 %shard_map.86 = (f32[136,128]{1,0:T(8,128)}, s32[2]{0:T(128)}, s32[328]{0:T(512)}, s32[200]{0:T(256)}) custom-call(s32[1]{0:T(128)} %bitcast.me_ref, s32[128]{0:T(128)} %order_ref.1, s32[128,128]{1,0:T(8,128)} %vmask_ref.1, s32[128,128]{1,0:T(8,128)} %vmask_ref.1), custom_call_target="tpu_custom_call" | custom-call | flops 10000 | bytes 200000 | tf_op jit(solution)/shard_map/pallas_call | solution.py:97
  19.6 0.0 collective-permute-done.1.refs_5_
  19.7 0.0 collective-permute-done.refs_4_
  19.7 0.0 copy-start.2
  19.7 0.1 collective-permute-start.4
  19.8 0.0 copy-start
  19.8 0.0 copy-start.1
  19.8 0.1 collective-permute-start.2
  19.9 0.0 copy-start.3
  19.9 4.3 %collective-permute-done.12.refs_13_.refs_12_ = bf16[1024,128]{1,0:T(8,128)(2,1)S(1)} collective-permute-done((bf16[1024,128]{1,0:T(8,128)(2,1)}, bf16[1024,128]{1,0:T(8,128)(2,1)S(1)}, u32[]{:S(2)}, u32[]{:S(2)}) %collective-permute-start.12) | collective-permute-done | bytes 262176 | tf_op jit(solution)/shard_map/ppermute | solution.py:32
  24.3 3.0 %collective-permute-start.8 = (bf16[512,128]{1,0:T(8,128)(2,1)S(1)}, bf16[512,128]{1,0:T(8,128)(2,1)S(1)}, u32[]{:S(2)}, u32[]{:S(2)}) collective-permute-start(bf16[512,128]{1,0:T(8,128)(2,1)S(1)} %get-tuple-element.77), channel_id=1, source_target_pairs={{0,56},{8,0},{16,8},{24,16},{32,24},{40,32},{48,40},{56,48},{64,12... | collective-permute-start | bytes 393224 | tf_op jit(solution)/shard_map/ppermute | solution.py:27
  27.2 0.0 collective-permute-done.11.refs_12_.refs_11_
  27.2 0.1 collective-permute-start.6
  27.3 0.0 collective-permute-done.4.refs_6_
  27.3 2.0 %collective-permute-start.5 = (bf16[512,128]{1,0:T(8,128)(2,1)S(1)}, bf16[512,128]{1,0:T(8,128)(2,1)S(1)}, u32[]{:S(2)}, u32[]{:S(2)}) collective-permute-start(bf16[512,128]{1,0:T(8,128)(2,1)S(1)} %collective-permute-done.4.refs_6_), channel_id=1, source_target_pairs={{0,8},{8,16},{16,24},{24,32},{32,40},{40,48},{48,56},{56,0},{64,72... | collective-permute-start | bytes 393224 | tf_op jit(solution)/shard_map/ppermute | solution.py:27
  29.3 0.0 collective-permute-done.2.refs_7_
  29.3 0.1 collective-permute-start.3
  29.3 1.4 %collective-permute-done.8.refs_8_ = bf16[512,128]{1,0:T(8,128)(2,1)S(1)} collective-permute-done((bf16[512,128]{1,0:T(8,128)(2,1)S(1)}, bf16[512,128]{1,0:T(8,128)(2,1)S(1)}, u32[]{:S(2)}, u32[]{:S(2)}) %collective-permute-start.8) | collective-permute-done | bytes 131104 | tf_op jit(solution)/shard_map/ppermute | solution.py:27
  30.7 3.7 %collective-permute-start.9 = (bf16[512,128]{1,0:T(8,128)(2,1)S(1)}, bf16[512,128]{1,0:T(8,128)(2,1)S(1)}, u32[]{:S(2)}, u32[]{:S(2)}) collective-permute-start(bf16[512,128]{1,0:T(8,128)(2,1)S(1)} %collective-permute-done.8.refs_8_), channel_id=1, source_target_pairs={{0,56},{8,0},{16,8},{24,16},{32,24},{40,32},{48,40},{56,48},{64,12... | collective-permute-start | bytes 393224 | tf_op jit(solution)/shard_map/ppermute | solution.py:27
  34.4 0.0 collective-permute-done.6.refs_9_
  34.4 2.8 %collective-permute-start.7 = (bf16[512,128]{1,0:T(8,128)(2,1)S(1)}, bf16[512,128]{1,0:T(8,128)(2,1)S(1)}, u32[]{:S(2)}, u32[]{:S(2)}) collective-permute-start(bf16[512,128]{1,0:T(8,128)(2,1)S(1)} %collective-permute-done.6.refs_9_), channel_id=1, source_target_pairs={{0,56},{8,0},{16,8},{24,16},{32,24},{40,32},{48,40},{56,48},{64,12... | collective-permute-start | bytes 393224 | tf_op jit(solution)/shard_map/ppermute | solution.py:27
  37.2 0.0 collective-permute-done.10.refs_11_.refs_10_
  37.2 0.0 copy-done.2
  37.2 0.0 copy-done
  37.2 0.0 copy-done.1
  37.2 2.5 %shard_map.88 = (f32[512,128]{1,0:T(8,128)S(1)}, bf16[512,128]{1,0:T(8,128)(2,1)S(1)}, bf16[512,128]{1,0:T(8,128)(2,1)S(1)}, bf16[512,128]{1,0:T(8,128)(2,1)S(1)...) custom-call(s32[2]{0:T(128)S(1)} %copy-done.4, s32[328]{0:T(512)S(1)} %copy-done.3, ...), custom_call_target="tpu_custom_call" | custom-call | flops 419430400 | bytes 4000000 | tf_op jit(solution)/shard_map/pallas_call | solution.py:218
  39.7 0.0 collective-permute-done.5.refs_4_
  39.8 0.0 collective-permute-done.3.refs_3_
  39.8 0.0 collective-permute-done.9.refs_6_
  39.8 2.5 %collective-permute-done.7.refs_5_ = bf16[512,128]{1,0:T(8,128)(2,1)S(1)} collective-permute-done((bf16[512,128]{1,0:T(8,128)(2,1)S(1)}, bf16[512,128]{1,0:T(8,128)(2,1)S(1)}, u32[]{:S(2)}, u32[]{:S(2)}) %collective-permute-start.7) | collective-permute-done | bytes 131104 | tf_op jit(solution)/shard_map/ppermute | solution.py:27
  42.3 0.0 collective-permute-start.15
  42.3 3.8 %collective-permute-start.16 = (bf16[512,128]{1,0:T(8,128)(2,1)S(1)}, bf16[512,128]{1,0:T(8,128)(2,1)S(1)}, u32[]{:S(2)}, u32[]{:S(2)}) collective-permute-start(bf16[512,128]{1,0:T(8,128)(2,1)S(1)} %collective-permute-done.7.refs_5_), channel_id=1, source_target_pairs={{0,56},{8,0},{16,8},{24,16},{32,24},{40,32},{48,40},{56,48},{64,12... | collective-permute-start | bytes 393224 | tf_op jit(solution)/shard_map/ppermute | solution.py:27
  46.2 2.0 %collective-permute-start.13 = (bf16[512,128]{1,0:T(8,128)(2,1)S(1)}, bf16[512,128]{1,0:T(8,128)(2,1)S(1)}, u32[]{:S(2)}, u32[]{:S(2)}) collective-permute-start(bf16[512,128]{1,0:T(8,128)(2,1)S(1)} %get-tuple-element.56), channel_id=1, source_target_pairs={{0,56},{8,0},{16,8},{24,16},{32,24},{40,32},{48,40},{56,48},{64,12... | collective-permute-start | bytes 393224 | tf_op jit(solution)/shard_map/ppermute | solution.py:27
  48.2 0.0 collective-permute-start.14
  48.2 2.9 %collective-permute-start.20 = (bf16[512,128]{1,0:T(8,128)(2,1)S(1)}, bf16[512,128]{1,0:T(8,128)(2,1)S(1)}, u32[]{:S(2)}, u32[]{:S(2)}) collective-permute-start(bf16[512,128]{1,0:T(8,128)(2,1)S(1)} %get-tuple-element.68), channel_id=1, source_target_pairs={{0,16},{8,24},{16,32},{24,40},{32,48},{40,56},{48,0},{56,8},{64,80... | collective-permute-start | bytes 393224 | tf_op jit(solution)/shard_map/ppermute | solution.py:27
  51.1 0.0 collective-permute-done.15.refs_7_
  51.1 0.0 collective-permute-start.21
  51.1 2.3 %collective-permute-done.16.refs_8_ = bf16[512,128]{1,0:T(8,128)(2,1)S(1)} collective-permute-done((bf16[512,128]{1,0:T(8,128)(2,1)S(1)}, bf16[512,128]{1,0:T(8,128)(2,1)S(1)}, u32[]{:S(2)}, u32[]{:S(2)}) %collective-permute-start.16) | collective-permute-done | bytes 131104 | tf_op jit(solution)/shard_map/ppermute | solution.py:27
  53.4 1.8 %shard_map.89 = (bf16[512,128]{1,0:T(8,128)(2,1)S(1)}, bf16[512,128]{1,0:T(8,128)(2,1)S(1)}, bf16[512,128]{1,0:T(8,128)(2,1)S(1)}, f32[512,128]{1,0:T(8,128)S(1)...) custom-call(s32[2]{0:T(128)S(1)} %copy-done.4, ...), custom_call_target="tpu_custom_call" | custom-call | flops 251658240 | bytes 4000000 | tf_op jit(solution)/shard_map/pallas_call | solution.py:218
  55.2 3.0 %collective-permute-start.17 = (bf16[512,128]{1,0:T(8,128)(2,1)S(1)}, bf16[512,128]{1,0:T(8,128)(2,1)S(1)}, u32[]{:S(2)}, u32[]{:S(2)}) collective-permute-start(bf16[512,128]{1,0:T(8,128)(2,1)S(1)} %get-tuple-element.65), channel_id=1, source_target_pairs={{0,40},{8,48},{16,56},{24,0},{32,8},{40,16},{48,24},{56,32},{64,10... | collective-permute-start | bytes 393224 | tf_op jit(solution)/shard_map/ppermute | solution.py:27
  58.2 0.0 collective-permute-done.13
  58.2 0.6 collective-permute-start.18
  58.8 0.3 collective-permute-done.14
  59.1 4.5 %collective-permute-start.19 = (bf16[512,128]{1,0:T(8,128)(2,1)S(1)}, bf16[512,128]{1,0:T(8,128)(2,1)S(1)}, u32[]{:S(2)}, u32[]{:S(2)}) collective-permute-start(bf16[512,128]{1,0:T(8,128)(2,1)S(1)} %get-tuple-element.67), channel_id=1, source_target_pairs={{0,24},{8,32},{16,40},{24,48},{32,56},{40,0},{48,8},{56,16},{64,88... | collective-permute-start | bytes 393224 | tf_op jit(solution)/shard_map/ppermute | solution.py:27
  63.5 0.0 collective-permute-done.20
  63.5 0.0 collective-permute-start.22
  63.5 0.0 collective-permute-done.21
  63.5 2.4 %collective-permute-start.23 = (bf16[1024,128]{1,0:T(8,128)(2,1)S(1)}, bf16[1024,128]{1,0:T(8,128)(2,1)S(1)}, u32[]{:S(2)}, u32[]{:S(2)}) collective-permute-start(bf16[1024,128]{1,0:T(8,128)(2,1)S(1)} %get-tuple-element.72), channel_id=1, source_target_pairs={{0,192},{8,200},{16,208},{24,216},{32,224},{40,232},{48,240},{56,2... | collective-permute-start | bytes 786440 | tf_op jit(solution)/shard_map/ppermute | solution.py:32
  66.0 0.0 collective-permute-done.17
  66.0 0.5 collective-permute-start.24
  66.5 1.6 %collective-permute-done.18 = bf16[512,128]{1,0:T(8,128)(2,1)S(1)} collective-permute-done((bf16[512,128]{1,0:T(8,128)(2,1)S(1)}, bf16[512,128]{1,0:T(8,128)(2,1)S(1)}, u32[]{:S(2)}, u32[]{:S(2)}) %collective-permute-start.18) | collective-permute-done | bytes 131104 | tf_op jit(solution)/shard_map/ppermute | solution.py:27
  68.0 3.4 %collective-permute-done.19 = bf16[512,128]{1,0:T(8,128)(2,1)S(1)} collective-permute-done((bf16[512,128]{1,0:T(8,128)(2,1)S(1)}, bf16[512,128]{1,0:T(8,128)(2,1)S(1)}, u32[]{:S(2)}, u32[]{:S(2)}) %collective-permute-start.19) | collective-permute-done | bytes 131104 | tf_op jit(solution)/shard_map/ppermute | solution.py:27
  71.5 0.8 %add_multiply_fusion = f32[512,128]{1,0:T(8,128)} fusion(bf16[512,128]{1,0:T(8,128)(2,1)S(1)} %collective-permute-done.21, bf16[512,128]{1,0:T(8,128)(2,1)S(1)} %collective-permute-done.20, bf16[512,128]{1,0:T(8,128)(2,1)S(1)} %collective-permute-done.19, bf16[512,128]{1,0:T(8,128)(2,1)S(1)} %collective-permute-done.18, ...), kind=kLoop, calls=%fused_computation.2 | loop fusion | flops 983040 | bytes 1441792 | tf_op jit(solution)/shard_map/mul | solution.py:261
  72.3 0.0 collective-permute-done.22
  72.3 1.3 %collective-permute-done.23 = bf16[1024,128]{1,0:T(8,128)(2,1)S(1)} collective-permute-done((bf16[1024,128]{1,0:T(8,128)(2,1)S(1)}, bf16[1024,128]{1,0:T(8,128)(2,1)S(1)}, u32[]{:S(2)}, u32[]{:S(2)}) %collective-permute-start.23) | collective-permute-done | bytes 262176 | tf_op jit(solution)/shard_map/ppermute | solution.py:32
  73.6 0.6 collective-permute-done.24
  74.2 0.9 %add_add_fusion = (f32[512,128]{1,0:T(8,128)}, f32[512,128]{1,0:T(8,128)}) fusion(f32[512,128]{1,0:T(8,128)S(1)} %get-tuple-element.74, bf16[1024,128]{1,0:T(8,128)(2,1)S(1)} %collective-permute-done.24, bf16[1024,128]{1,0:T(8,128)(2,1)S(1)} %collective-permute-done.23, bf16[1024,128]{1,0:T(8,128)(2,1)S(1)} %collective-permute-done.22, ...), kind=kLoop, calls=%fused_computation | loop fusion | flops 851968 | bytes 1835008 | tf_op jit(solution)/shard_map/add | solution.py:263
  (7 shorter events, 0.0 us)
Async XLA Ops:
  2.3 17.3 %collective-permute-start.1 = (bf16[1024,128]{1,0:T(8,128)(2,1)}, bf16[1024,128]{1,0:T(8,128)(2,1)S(1)}, u32[]{:S(2)}, u32[]{:S(2)}) collective-permute-start(bf16[1024,128]{1,0:T(8,128)(2,1)} %shard_map.85.refs_3_), channel_id=1, source_target_pairs={{0,56},{8,0},{16,8},{24,16},{32,24},{40,32},{48,40},{56,48},{64,12... | collective-permute-start | bytes 786440 | tf_op jit(solution)/shard_map/ppermute | solution.py:27
  8.3 11.4 %collective-permute-start = (bf16[1024,128]{1,0:T(8,128)(2,1)}, bf16[1024,128]{1,0:T(8,128)(2,1)S(1)}, u32[]{:S(2)}, u32[]{:S(2)}) collective-permute-start(bf16[1024,128]{1,0:T(8,128)(2,1)} %shard_map.85.refs_3_), channel_id=1, source_target_pairs={{0,8},{8,16},{16,24},{24,32},{32,40},{40,48},{48,56},{56,0},{64,72... | collective-permute-start | bytes 786440 | tf_op jit(solution)/shard_map/ppermute | solution.py:27
  10.0 14.3 %collective-permute-start.12 = (bf16[1024,128]{1,0:T(8,128)(2,1)}, bf16[1024,128]{1,0:T(8,128)(2,1)S(1)}, u32[]{:S(2)}, u32[]{:S(2)}) collective-permute-start(bf16[1024,128]{1,0:T(8,128)(2,1)} %shard_map.87.refs_10_.refs_9_), channel_id=1, source_target_pairs={{0,192},{8,200},{16,208},{24,216},{32,224},{40,232},{48,240},{56,2... | collective-permute-start | bytes 786440 | tf_op jit(solution)/shard_map/ppermute | solution.py:32
  13.0 14.2 %collective-permute-start.11 = (bf16[1024,128]{1,0:T(8,128)(2,1)}, bf16[1024,128]{1,0:T(8,128)(2,1)S(1)}, u32[]{:S(2)}, u32[]{:S(2)}) collective-permute-start(bf16[1024,128]{1,0:T(8,128)(2,1)} %shard_map.87.refs_10_.refs_9_), channel_id=1, source_target_pairs={{0,128},{8,136},{16,144},{24,152},{32,160},{40,168},{48,176},{56,1... | collective-permute-start | bytes 786440 | tf_op jit(solution)/shard_map/ppermute | solution.py:32
  13.7 23.5 %collective-permute-start.10 = (bf16[1024,128]{1,0:T(8,128)(2,1)}, bf16[1024,128]{1,0:T(8,128)(2,1)S(1)}, u32[]{:S(2)}, u32[]{:S(2)}) collective-permute-start(bf16[1024,128]{1,0:T(8,128)(2,1)} %shard_map.87.refs_10_.refs_9_), channel_id=1, source_target_pairs={{0,64},{8,72},{16,80},{24,88},{32,96},{40,104},{48,112},{56,120},{... | collective-permute-start | bytes 786440 | tf_op jit(solution)/shard_map/ppermute | solution.py:32
  19.7 17.5 %copy-start.2 = (f32[136,128]{1,0:T(8,128)S(1)}, f32[136,128]{1,0:T(8,128)}, u32[]{:S(2)}) copy-start(f32[136,128]{1,0:T(8,128)} %get-tuple-element.47.refs_2_) | copy-start | bytes 208900
  19.7 7.6 %collective-permute-start.4 = (bf16[512,128]{1,0:T(8,128)(2,1)S(1)}, bf16[512,128]{1,0:T(8,128)(2,1)S(1)}, u32[]{:S(2)}, u32[]{:S(2)}) collective-permute-start(bf16[512,128]{1,0:T(8,128)(2,1)S(1)} %get-tuple-element.79), channel_id=1, source_target_pairs={{0,8},{8,16},{16,24},{24,32},{32,40},{40,48},{48,56},{56,0},{64,72... | collective-permute-start | bytes 393224 | tf_op jit(solution)/shard_map/ppermute | solution.py:27
  19.8 17.4 %copy-start = (bf16[1024,128]{1,0:T(8,128)(2,1)S(1)}, bf16[1024,128]{1,0:T(8,128)(2,1)}, u32[]{:S(2)}) copy-start(bf16[1024,128]{1,0:T(8,128)(2,1)} %shard_map.87.refs_10_.refs_9_) | copy-start | bytes 786436
  19.8 17.4 %copy-start.1 = (bf16[1024,128]{1,0:T(8,128)(2,1)S(1)}, bf16[1024,128]{1,0:T(8,128)(2,1)}, u32[]{:S(2)}) copy-start(bf16[1024,128]{1,0:T(8,128)(2,1)} %shard_map.85.refs_3_) | copy-start | bytes 786436
  19.8 9.4 %collective-permute-start.2 = (bf16[512,128]{1,0:T(8,128)(2,1)S(1)}, bf16[512,128]{1,0:T(8,128)(2,1)S(1)}, u32[]{:S(2)}, u32[]{:S(2)}) collective-permute-start(bf16[512,128]{1,0:T(8,128)(2,1)S(1)} %get-tuple-element.80), channel_id=1, source_target_pairs={{0,8},{8,16},{16,24},{24,32},{32,40},{40,48},{48,56},{56,0},{64,72... | collective-permute-start | bytes 393224 | tf_op jit(solution)/shard_map/ppermute | solution.py:27
  19.9 17.3 %copy-start.3 = (s32[328]{0:T(512)S(1)}, s32[328]{0:T(512)}, u32[]{:S(2)}) copy-start(s32[328]{0:T(512)} %get-tuple-element.46.refs_1_) | copy-start | bytes 3940
  24.3 13.0 %copy-start.4 = (s32[2]{0:T(128)S(1)}, s32[2]{0:T(128)}, u32[]{:S(2)}) copy-start(s32[2]{0:T(128)} %get-tuple-element.45.refs_0_) | copy-start | bytes 28
  24.3 6.4 %collective-permute-start.8 = (bf16[512,128]{1,0:T(8,128)(2,1)S(1)}, bf16[512,128]{1,0:T(8,128)(2,1)S(1)}, u32[]{:S(2)}, u32[]{:S(2)}) collective-permute-start(bf16[512,128]{1,0:T(8,128)(2,1)S(1)} %get-tuple-element.77), channel_id=1, source_target_pairs={{0,56},{8,0},{16,8},{24,16},{32,24},{40,32},{48,40},{56,48},{64,12... | collective-permute-start | bytes 393224 | tf_op jit(solution)/shard_map/ppermute | solution.py:27
  27.2 7.2 %collective-permute-start.6 = (bf16[512,128]{1,0:T(8,128)(2,1)S(1)}, bf16[512,128]{1,0:T(8,128)(2,1)S(1)}, u32[]{:S(2)}, u32[]{:S(2)}) collective-permute-start(bf16[512,128]{1,0:T(8,128)(2,1)S(1)} %get-tuple-element.78), channel_id=1, source_target_pairs={{0,56},{8,0},{16,8},{24,16},{32,24},{40,32},{48,40},{56,48},{64,12... | collective-permute-start | bytes 393224 | tf_op jit(solution)/shard_map/ppermute | solution.py:27
  27.3 12.4 %collective-permute-start.5 = (bf16[512,128]{1,0:T(8,128)(2,1)S(1)}, bf16[512,128]{1,0:T(8,128)(2,1)S(1)}, u32[]{:S(2)}, u32[]{:S(2)}) collective-permute-start(bf16[512,128]{1,0:T(8,128)(2,1)S(1)} %collective-permute-done.4.refs_6_), channel_id=1, source_target_pairs={{0,8},{8,16},{16,24},{24,32},{32,40},{40,48},{48,56},{56,0},{64,72... | collective-permute-start | bytes 393224 | tf_op jit(solution)/shard_map/ppermute | solution.py:27
  29.3 10.5 %collective-permute-start.3 = (bf16[512,128]{1,0:T(8,128)(2,1)S(1)}, bf16[512,128]{1,0:T(8,128)(2,1)S(1)}, u32[]{:S(2)}, u32[]{:S(2)}) collective-permute-start(bf16[512,128]{1,0:T(8,128)(2,1)S(1)} %collective-permute-done.2.refs_7_), channel_id=1, source_target_pairs={{0,8},{8,16},{16,24},{24,32},{32,40},{40,48},{48,56},{56,0},{64,72... | collective-permute-start | bytes 393224 | tf_op jit(solution)/shard_map/ppermute | solution.py:27
  30.7 9.1 %collective-permute-start.9 = (bf16[512,128]{1,0:T(8,128)(2,1)S(1)}, bf16[512,128]{1,0:T(8,128)(2,1)S(1)}, u32[]{:S(2)}, u32[]{:S(2)}) collective-permute-start(bf16[512,128]{1,0:T(8,128)(2,1)S(1)} %collective-permute-done.8.refs_8_), channel_id=1, source_target_pairs={{0,56},{8,0},{16,8},{24,16},{32,24},{40,32},{48,40},{56,48},{64,12... | collective-permute-start | bytes 393224 | tf_op jit(solution)/shard_map/ppermute | solution.py:27
  34.4 7.9 %collective-permute-start.7 = (bf16[512,128]{1,0:T(8,128)(2,1)S(1)}, bf16[512,128]{1,0:T(8,128)(2,1)S(1)}, u32[]{:S(2)}, u32[]{:S(2)}) collective-permute-start(bf16[512,128]{1,0:T(8,128)(2,1)S(1)} %collective-permute-done.6.refs_9_), channel_id=1, source_target_pairs={{0,56},{8,0},{16,8},{24,16},{32,24},{40,32},{48,40},{56,48},{64,12... | collective-permute-start | bytes 393224 | tf_op jit(solution)/shard_map/ppermute | solution.py:27
  42.3 11.1 %copy-start.5 = (s32[200]{0:T(256)S(1)}, s32[200]{0:T(256)}, u32[]{:S(2)}) copy-start(s32[200]{0:T(256)} %get-tuple-element.58.refs_1_) | copy-start | bytes 2404
  42.3 8.8 %collective-permute-start.15 = (bf16[512,128]{1,0:T(8,128)(2,1)S(1)}, bf16[512,128]{1,0:T(8,128)(2,1)S(1)}, u32[]{:S(2)}, u32[]{:S(2)}) collective-permute-start(bf16[512,128]{1,0:T(8,128)(2,1)S(1)} %collective-permute-done.5.refs_4_), channel_id=1, source_target_pairs={{0,8},{8,16},{16,24},{24,32},{32,40},{40,48},{48,56},{56,0},{64,72... | collective-permute-start | bytes 393224 | tf_op jit(solution)/shard_map/ppermute | solution.py:27
  42.3 11.1 %collective-permute-start.16 = (bf16[512,128]{1,0:T(8,128)(2,1)S(1)}, bf16[512,128]{1,0:T(8,128)(2,1)S(1)}, u32[]{:S(2)}, u32[]{:S(2)}) collective-permute-start(bf16[512,128]{1,0:T(8,128)(2,1)S(1)} %collective-permute-done.7.refs_5_), channel_id=1, source_target_pairs={{0,56},{8,0},{16,8},{24,16},{32,24},{40,32},{48,40},{56,48},{64,12... | collective-permute-start | bytes 393224 | tf_op jit(solution)/shard_map/ppermute | solution.py:27
  46.2 12.0 %collective-permute-start.13 = (bf16[512,128]{1,0:T(8,128)(2,1)S(1)}, bf16[512,128]{1,0:T(8,128)(2,1)S(1)}, u32[]{:S(2)}, u32[]{:S(2)}) collective-permute-start(bf16[512,128]{1,0:T(8,128)(2,1)S(1)} %get-tuple-element.56), channel_id=1, source_target_pairs={{0,56},{8,0},{16,8},{24,16},{32,24},{40,32},{48,40},{56,48},{64,12... | collective-permute-start | bytes 393224 | tf_op jit(solution)/shard_map/ppermute | solution.py:27
  48.2 10.9 %collective-permute-start.14 = (bf16[512,128]{1,0:T(8,128)(2,1)S(1)}, bf16[512,128]{1,0:T(8,128)(2,1)S(1)}, u32[]{:S(2)}, u32[]{:S(2)}) collective-permute-start(bf16[512,128]{1,0:T(8,128)(2,1)S(1)} %get-tuple-element.57), channel_id=1, source_target_pairs={{0,48},{8,56},{16,0},{24,8},{32,16},{40,24},{48,32},{56,40},{64,11... | collective-permute-start | bytes 393224 | tf_op jit(solution)/shard_map/ppermute | solution.py:27
  48.2 15.4 %collective-permute-start.20 = (bf16[512,128]{1,0:T(8,128)(2,1)S(1)}, bf16[512,128]{1,0:T(8,128)(2,1)S(1)}, u32[]{:S(2)}, u32[]{:S(2)}) collective-permute-start(bf16[512,128]{1,0:T(8,128)(2,1)S(1)} %get-tuple-element.68), channel_id=1, source_target_pairs={{0,16},{8,24},{16,32},{24,40},{32,48},{40,56},{48,0},{56,8},{64,80... | collective-permute-start | bytes 393224 | tf_op jit(solution)/shard_map/ppermute | solution.py:27
  51.1 12.4 %collective-permute-start.21 = (bf16[512,128]{1,0:T(8,128)(2,1)S(1)}, bf16[512,128]{1,0:T(8,128)(2,1)S(1)}, u32[]{:S(2)}, u32[]{:S(2)}) collective-permute-start(bf16[512,128]{1,0:T(8,128)(2,1)S(1)} %get-tuple-element.69), channel_id=1, source_target_pairs={{0,8},{8,16},{16,24},{24,32},{32,40},{40,48},{48,56},{56,0},{64,72... | collective-permute-start | bytes 393224 | tf_op jit(solution)/shard_map/ppermute | solution.py:27
  55.2 10.8 %collective-permute-start.17 = (bf16[512,128]{1,0:T(8,128)(2,1)S(1)}, bf16[512,128]{1,0:T(8,128)(2,1)S(1)}, u32[]{:S(2)}, u32[]{:S(2)}) collective-permute-start(bf16[512,128]{1,0:T(8,128)(2,1)S(1)} %get-tuple-element.65), channel_id=1, source_target_pairs={{0,40},{8,48},{16,56},{24,0},{32,8},{40,16},{48,24},{56,32},{64,10... | collective-permute-start | bytes 393224 | tf_op jit(solution)/shard_map/ppermute | solution.py:27
  58.2 9.9 %collective-permute-start.18 = (bf16[512,128]{1,0:T(8,128)(2,1)S(1)}, bf16[512,128]{1,0:T(8,128)(2,1)S(1)}, u32[]{:S(2)}, u32[]{:S(2)}) collective-permute-start(bf16[512,128]{1,0:T(8,128)(2,1)S(1)} %get-tuple-element.66), channel_id=1, source_target_pairs={{0,32},{8,40},{16,48},{24,56},{32,0},{40,8},{48,16},{56,24},{64,96... | collective-permute-start | bytes 393224 | tf_op jit(solution)/shard_map/ppermute | solution.py:27
  59.1 12.4 %collective-permute-start.19 = (bf16[512,128]{1,0:T(8,128)(2,1)S(1)}, bf16[512,128]{1,0:T(8,128)(2,1)S(1)}, u32[]{:S(2)}, u32[]{:S(2)}) collective-permute-start(bf16[512,128]{1,0:T(8,128)(2,1)S(1)} %get-tuple-element.67), channel_id=1, source_target_pairs={{0,24},{8,32},{16,40},{24,48},{32,56},{40,0},{48,8},{56,16},{64,88... | collective-permute-start | bytes 393224 | tf_op jit(solution)/shard_map/ppermute | solution.py:27
  63.5 8.8 %collective-permute-start.22 = (bf16[1024,128]{1,0:T(8,128)(2,1)S(1)}, bf16[1024,128]{1,0:T(8,128)(2,1)S(1)}, u32[]{:S(2)}, u32[]{:S(2)}) collective-permute-start(bf16[1024,128]{1,0:T(8,128)(2,1)S(1)} %get-tuple-element.71), channel_id=1, source_target_pairs={{0,128},{8,136},{16,144},{24,152},{32,160},{40,168},{48,176},{56,1... | collective-permute-start | bytes 786440 | tf_op jit(solution)/shard_map/ppermute | solution.py:32
  63.5 10.0 %collective-permute-start.23 = (bf16[1024,128]{1,0:T(8,128)(2,1)S(1)}, bf16[1024,128]{1,0:T(8,128)(2,1)S(1)}, u32[]{:S(2)}, u32[]{:S(2)}) collective-permute-start(bf16[1024,128]{1,0:T(8,128)(2,1)S(1)} %get-tuple-element.72), channel_id=1, source_target_pairs={{0,192},{8,200},{16,208},{24,216},{32,224},{40,232},{48,240},{56,2... | collective-permute-start | bytes 786440 | tf_op jit(solution)/shard_map/ppermute | solution.py:32
  66.0 8.2 %collective-permute-start.24 = (bf16[1024,128]{1,0:T(8,128)(2,1)S(1)}, bf16[1024,128]{1,0:T(8,128)(2,1)S(1)}, u32[]{:S(2)}, u32[]{:S(2)}) collective-permute-start(bf16[1024,128]{1,0:T(8,128)(2,1)S(1)} %get-tuple-element.73), channel_id=1, source_target_pairs={{0,64},{8,72},{16,80},{24,88},{32,96},{40,104},{48,112},{56,120},{... | collective-permute-start | bytes 786440 | tf_op jit(solution)/shard_map/ppermute | solution.py:32

commit v3 on v2

--- a/solution.py
+++ b/solution.py
@@ -68,11 +68,13 @@
     rate_ref[pl.ds(BLK, 8), :] = jnp.zeros((8, BLK), f32)
 
 
-def stack_kernel(a_ref, b_ref, ab_ref, sem):
+def stack_kernel(a_ref, b_ref, c_ref, d_ref, ab_ref, cd_ref, sem):
     rows = a_ref.shape[0]
     copies = [
-        pltpu.make_async_copy(src, ab_ref.at[pl.ds(i * rows, rows), :], sem.at[i])
-        for i, src in enumerate((a_ref, b_ref))
+        pltpu.make_async_copy(src, dst.at[pl.ds(at, rows), :], sem.at[i])
+        for i, (src, dst, at) in enumerate(
+            ((a_ref, ab_ref, 0), (b_ref, ab_ref, rows), (c_ref, cd_ref, 0), (d_ref, cd_ref, rows))
+        )
     ]
     for c in copies:
         c.start()
@@ -80,15 +82,16 @@
         c.wait()
 
 
-def stack_pair(a, b):
+def stack_pairs(a, b, c, d):
+    out = jax.ShapeDtypeStruct((2 * a.shape[0], a.shape[1]), a.dtype)
     return pl.pallas_call(
         stack_kernel,
-        out_shape=jax.ShapeDtypeStruct((2 * a.shape[0], a.shape[1]), a.dtype),
-        in_specs=[pl.BlockSpec(memory_space=pltpu.HBM)] * 2,
-        out_specs=pl.BlockSpec(memory_space=pltpu.VMEM),
-        scratch_shapes=[pltpu.SemaphoreType.DMA((2,))],
-        cost_estimate=pl.CostEstimate(flops=0, bytes_accessed=500_000, transcendentals=0),
-    )(a, b)
+        out_shape=[out, out],
+        in_specs=[pl.BlockSpec(memory_space=pltpu.HBM)] * 4,
+        out_specs=[pl.BlockSpec(memory_space=pltpu.VMEM)] * 2,
+        scratch_shapes=[pltpu.SemaphoreType.DMA((4,))],
+        cost_estimate=pl.CostEstimate(flops=0, bytes_accessed=1_000_000, transcendentals=0),
+    )(a, b, c, d)
 
 
 def make_plan(me, block_order, block_mask):
@@ -233,11 +236,11 @@
     rows = queries.shape[0]
     me = lax.axis_index("seq").astype(i32).reshape(1)
     plan = make_plan(me, block_order, block_mask)
-    qg, kv = stack_pair(queries, out_grad), stack_pair(keys, values)
+    qg, kv = stack_pairs(queries, out_grad, keys, values)
     ahead, behind = z_shift(qg, 1), z_shift(qg, -1)
-    kvs = [kv] + [y_shift(kv, t) for t in (1, 3, 2)]
-    kvs = [kvs[0], kvs[1], kvs[3], kvs[2]]
-    (ahead, behind), plan = lax.optimization_barrier(((ahead, behind), plan))
+    kvs = [kv, y_shift(kv, 1), None, y_shift(kv, 3)]
+    (ahead, behind), plan, kv = lax.optimization_barrier(((ahead, behind), plan, kv))
+    kvs[2] = y_shift(kv, 2)
     shards = {0: {"qg": qg}, 1: {"qg": ahead}, NZ - 1: {"qg": behind}}
     split = lambda a: {"q": a[:rows], "g": a[rows:]}
     ahead, behind = split(ahead), split(behind)

time: 75.9 us -> 71.3 us (0.939); the launches traced: 75.1 us -> 71.5 us
  starting transfers between devices: 42.1 us -> 38.3 us
  Pallas kernels: 12.7 us -> 11.3 us
  waiting for transfers between devices: 17.7 us -> 18.6 us
    ppermute x19, starting transfers between devices: 34.5 us -> 29.7 us  [z_shift(): return lax.ppermute(a, 'seq', route)]
    ppermute x19, waiting for transfers between devices: 11.5 us -> 14.3 us  [z_shift(): return lax.ppermute(a, 'seq', route)]
    ppermute x6, waiting for transfers between devices: 6.23 us -> 4.29 us  [y_shift(): return lax.ppermute(a, 'seq', route)]
    pallas_call x2 -> x1, Pallas kernels: 3.37 us -> 1.92 us  [stack_pairs(): pl.pallas_call(stack_kernel, out_shape=[out, out], in_specs=[pl.BlockSpec...]
    ppermute x6, starting transfers between devices: 7.62 us -> 8.6 us  [y_shift(): return lax.ppermute(a, 'seq', route)]
  transfers between devices with their start and end apart: 25 -> 25, of which waited for: 9 -> 10; matrix products, arithmetic and copies ran while one was open for 1% -> 1% of each run, Pallas kernels for 15% -> 13%
where the time goes in v3:
time: 71.3 us; the launch traced here: 71.5 us
  starting transfers between devices  38.3 us (54%)
  waiting for transfers between devices  18.6 us (26%)
  Pallas kernels  11.3 us (16%)
  other arithmetic  1.76 us (2%)
  between operations  0.8 us (1%)
  local copies, waits for them, and re-layouts  0.78 us (1%)
    ppermute x19, starting transfers between devices, z_shift(): return lax.ppermute(a, 'seq', route)  29.7 us
    ppermute x19, waiting for transfers between devices, z_shift(): return lax.ppermute(a, 'seq', route)  14.3 us
    ppermute x6, starting transfers between devices, y_shift(): return lax.ppermute(a, 'seq', route)  8.6 us
    pallas_call x1, Pallas kernels, make_plan(): pl.pallas_call(plan_kernel, out_shape=[jax.ShapeDtypeStruct((BLK + 8, BLK...  4.99 us
    pallas_call x2, Pallas kernels, run_pairs(): pl.pallas_call(functools.partial(pairs_kernel, g, first, last, row_parts)...  4.35 us
    ppermute x6, waiting for transfers between devices, y_shift(): return lax.ppermute(a, 'seq', route)  4.29 us
    pallas_call x1, Pallas kernels, stack_pairs(): pl.pallas_call(stack_kernel, out_shape=[out, out], in_specs=[pl.BlockSpec...  1.92 us
  transfers between devices with their start and end apart: 25, of which 10 were waited for; matrix products, arithmetic and copies ran while one was open for 1% of the time, Pallas kernels for 13%

profile of v3, /device:TPU:2, one launch (start us, length us, event | category | flops | bytes accessed | tf_op | source)
XLA Modules:
  0.0 71.5 jit_solution(12840897002939276050)
XLA Ops:
  0.6 1.9 %shard_map.85 = (bf16[1024,128]{1,0:T(8,128)(2,1)}, bf16[1024,128]{1,0:T(8,128)(2,1)}) custom-call(bf16[512,128]{1,0:T(8,128)(2,1)} %a_ref.1, bf16[512,128]{1,0:T(8,128)(2,1)} %b_ref.1, bf16[512,128]{1,0:T(8,128)(2,1)} %c_ref.1, bf16[512,128]{1,0:T(8,128)(2,1)} %d_ref.1), custom_call_target="tpu_custom_call" | custom-call | bytes 1000000 | tf_op jit(solution)/shard_map/pallas_call | solution.py:87
  2.6 5.9 %collective-permute-start.1 = (bf16[1024,128]{1,0:T(8,128)(2,1)}, bf16[1024,128]{1,0:T(8,128)(2,1)S(1)}, u32[]{:S(2)}, u32[]{:S(2)}) collective-permute-start(bf16[1024,128]{1,0:T(8,128)(2,1)} %get-tuple-element.42.refs_3_), channel_id=1, source_target_pairs={{0,56},{8,0},{16,8},{24,16},{32,24},{40,32},{48,40},{56,48},{64,12... | collective-permute-start | bytes 786440 | tf_op jit(solution)/shard_map/ppermute | solution.py:27
  8.5 0.0 collective-permute-start
  8.5 3.0 %collective-permute-start.12 = (bf16[1024,128]{1,0:T(8,128)(2,1)}, bf16[1024,128]{1,0:T(8,128)(2,1)S(1)}, u32[]{:S(2)}, u32[]{:S(2)}) collective-permute-start(bf16[1024,128]{1,0:T(8,128)(2,1)} %get-tuple-element.53.refs_10_.refs_9_), channel_id=1, source_target_pairs={{0,192},{8,200},{16,208},{24,216},{32,224},{40,232},{48,240},{56,2... | collective-permute-start | bytes 786440 | tf_op jit(solution)/shard_map/ppermute | solution.py:32
  11.5 0.0 collective-permute-start.10
  11.5 5.0 %shard_map.86 = (f32[136,128]{1,0:T(8,128)}, s32[2]{0:T(128)}, s32[328]{0:T(512)}, s32[200]{0:T(256)}) custom-call(s32[1]{0:T(128)} %bitcast.me_ref, s32[128]{0:T(128)} %order_ref.1, s32[128,128]{1,0:T(8,128)} %vmask_ref.1, s32[128,128]{1,0:T(8,128)} %vmask_ref.1), custom_call_target="tpu_custom_call" | custom-call | flops 10000 | bytes 200000 | tf_op jit(solution)/shard_map/pallas_call | solution.py:100
  16.5 0.0 collective-permute-done.1.refs_5_
  16.5 1.2 %collective-permute-done.refs_4_ = bf16[1024,128]{1,0:T(8,128)(2,1)S(1)} collective-permute-done((bf16[1024,128]{1,0:T(8,128)(2,1)}, bf16[1024,128]{1,0:T(8,128)(2,1)S(1)}, u32[]{:S(2)}, u32[]{:S(2)}) %collective-permute-start) | collective-permute-done | bytes 262176 | tf_op jit(solution)/shard_map/ppermute | solution.py:27
  17.7 0.1 collective-permute-start.4
  17.8 0.0 copy-start.1
  17.8 0.0 copy-start.2
  17.8 0.1 collective-permute-start.2
  17.9 0.7 %copy-done = bf16[1024,128]{1,0:T(8,128)(2,1)S(1)} copy-done((bf16[1024,128]{1,0:T(8,128)(2,1)S(1)}, bf16[1024,128]{1,0:T(8,128)(2,1)}, u32[]{:S(2)}) %copy-start) | copy-done | bytes 262168
  18.6 3.2 %collective-permute-start.11 = (bf16[1024,128]{1,0:T(8,128)(2,1)S(1)}, bf16[1024,128]{1,0:T(8,128)(2,1)S(1)}, u32[]{:S(2)}, u32[]{:S(2)}) collective-permute-start(bf16[1024,128]{1,0:T(8,128)(2,1)S(1)} %copy-done), channel_id=1, source_target_pairs={{0,128},{8,136},{16,144},{24,152},{32,160},{40,168},{48,176},{56,1... | collective-permute-start | bytes 786440 | tf_op jit(solution)/shard_map/ppermute | solution.py:32
  21.8 0.0 copy-start.3
  21.9 0.0 collective-permute-done.12.refs_13_.refs_12_
  21.9 0.0 copy-start.4
  21.9 2.6 %collective-permute-start.8 = (bf16[512,128]{1,0:T(8,128)(2,1)S(1)}, bf16[512,128]{1,0:T(8,128)(2,1)S(1)}, u32[]{:S(2)}, u32[]{:S(2)}) collective-permute-start(bf16[512,128]{1,0:T(8,128)(2,1)S(1)} %get-tuple-element.83), channel_id=1, source_target_pairs={{0,56},{8,0},{16,8},{24,16},{32,24},{40,32},{48,40},{56,48},{64,12... | collective-permute-start | bytes 393224 | tf_op jit(solution)/shard_map/ppermute | solution.py:27
  24.5 0.0 collective-permute-done.10.refs_11_.refs_10_
  24.5 1.9 %collective-permute-start.6 = (bf16[512,128]{1,0:T(8,128)(2,1)S(1)}, bf16[512,128]{1,0:T(8,128)(2,1)S(1)}, u32[]{:S(2)}, u32[]{:S(2)}) collective-permute-start(bf16[512,128]{1,0:T(8,128)(2,1)S(1)} %get-tuple-element.84), channel_id=1, source_target_pairs={{0,56},{8,0},{16,8},{24,16},{32,24},{40,32},{48,40},{56,48},{64,12... | collective-permute-start | bytes 393224 | tf_op jit(solution)/shard_map/ppermute | solution.py:27
  26.4 0.0 collective-permute-done.4.refs_6_
  26.4 0.1 collective-permute-start.5
  26.5 0.0 collective-permute-done.2.refs_7_
  26.5 0.1 collective-permute-start.3
  26.6 1.7 %collective-permute-done.8.refs_8_ = bf16[512,128]{1,0:T(8,128)(2,1)S(1)} collective-permute-done((bf16[512,128]{1,0:T(8,128)(2,1)S(1)}, bf16[512,128]{1,0:T(8,128)(2,1)S(1)}, u32[]{:S(2)}, u32[]{:S(2)}) %collective-permute-start.8) | collective-permute-done | bytes 131104 | tf_op jit(solution)/shard_map/ppermute | solution.py:27
  28.3 2.4 %collective-permute-start.9 = (bf16[512,128]{1,0:T(8,128)(2,1)S(1)}, bf16[512,128]{1,0:T(8,128)(2,1)S(1)}, u32[]{:S(2)}, u32[]{:S(2)}) collective-permute-start(bf16[512,128]{1,0:T(8,128)(2,1)S(1)} %collective-permute-done.8.refs_8_), channel_id=1, source_target_pairs={{0,56},{8,0},{16,8},{24,16},{32,24},{40,32},{48,40},{56,48},{64,12... | collective-permute-start | bytes 393224 | tf_op jit(solution)/shard_map/ppermute | solution.py:27
  30.6 0.1 collective-permute-done.6.refs_9_
  30.7 2.8 %collective-permute-start.7 = (bf16[512,128]{1,0:T(8,128)(2,1)S(1)}, bf16[512,128]{1,0:T(8,128)(2,1)S(1)}, u32[]{:S(2)}, u32[]{:S(2)}) collective-permute-start(bf16[512,128]{1,0:T(8,128)(2,1)S(1)} %collective-permute-done.6.refs_9_), channel_id=1, source_target_pairs={{0,56},{8,0},{16,8},{24,16},{32,24},{40,32},{48,40},{56,48},{64,12... | collective-permute-start | bytes 393224 | tf_op jit(solution)/shard_map/ppermute | solution.py:27
  33.5 0.0 collective-permute-done.11.refs_12_.refs_11_
  33.5 0.0 copy-done.1
  33.5 0.0 copy-done.2
  33.5 2.5 %shard_map.87 = (f32[512,128]{1,0:T(8,128)S(1)}, bf16[512,128]{1,0:T(8,128)(2,1)S(1)}, bf16[512,128]{1,0:T(8,128)(2,1)S(1)}, bf16[512,128]{1,0:T(8,128)(2,1)S(1)...) custom-call(s32[2]{0:T(128)S(1)} %copy-done.4, s32[328]{0:T(512)S(1)} %copy-done.3, ...), custom_call_target="tpu_custom_call" | custom-call | flops 419430400 | bytes 4000000 | tf_op jit(solution)/shard_map/pallas_call | solution.py:221
  36.1 0.0 collective-permute-done.5.refs_4_
  36.1 0.0 collective-permute-done.3.refs_3_
  36.1 0.0 collective-permute-done.9.refs_6_
  36.1 0.6 collective-permute-done.7.refs_5_
  36.7 0.0 collective-permute-start.15
  36.7 3.7 %collective-permute-start.16 = (bf16[512,128]{1,0:T(8,128)(2,1)S(1)}, bf16[512,128]{1,0:T(8,128)(2,1)S(1)}, u32[]{:S(2)}, u32[]{:S(2)}) collective-permute-start(bf16[512,128]{1,0:T(8,128)(2,1)S(1)} %collective-permute-done.7.refs_5_), channel_id=1, source_target_pairs={{0,56},{8,0},{16,8},{24,16},{32,24},{40,32},{48,40},{56,48},{64,12... | collective-permute-start | bytes 393224 | tf_op jit(solution)/shard_map/ppermute | solution.py:27
  40.4 2.0 %collective-permute-start.13 = (bf16[512,128]{1,0:T(8,128)(2,1)S(1)}, bf16[512,128]{1,0:T(8,128)(2,1)S(1)}, u32[]{:S(2)}, u32[]{:S(2)}) collective-permute-start(bf16[512,128]{1,0:T(8,128)(2,1)S(1)} %get-tuple-element.62), channel_id=1, source_target_pairs={{0,56},{8,0},{16,8},{24,16},{32,24},{40,32},{48,40},{56,48},{64,12... | collective-permute-start | bytes 393224 | tf_op jit(solution)/shard_map/ppermute | solution.py:27
  42.5 0.0 collective-permute-start.14
  42.5 2.9 %collective-permute-start.20 = (bf16[512,128]{1,0:T(8,128)(2,1)S(1)}, bf16[512,128]{1,0:T(8,128)(2,1)S(1)}, u32[]{:S(2)}, u32[]{:S(2)}) collective-permute-start(bf16[512,128]{1,0:T(8,128)(2,1)S(1)} %get-tuple-element.74), channel_id=1, source_target_pairs={{0,16},{8,24},{16,32},{24,40},{32,48},{40,56},{48,0},{56,8},{64,80... | collective-permute-start | bytes 393224 | tf_op jit(solution)/shard_map/ppermute | solution.py:27
  45.4 0.4 collective-permute-done.15.refs_7_
  45.8 0.0 collective-permute-start.21
  45.8 0.0 collective-permute-done.16.refs_8_
  45.8 0.0 copy-done.5
  45.8 1.8 %shard_map.88 = (bf16[512,128]{1,0:T(8,128)(2,1)S(1)}, bf16[512,128]{1,0:T(8,128)(2,1)S(1)}, bf16[512,128]{1,0:T(8,128)(2,1)S(1)}, f32[512,128]{1,0:T(8,128)S(1)...) custom-call(s32[2]{0:T(128)S(1)} %copy-done.4, ...), custom_call_target="tpu_custom_call" | custom-call | flops 251658240 | bytes 4000000 | tf_op jit(solution)/shard_map/pallas_call | solution.py:221
  47.6 3.1 %collective-permute-start.17 = (bf16[512,128]{1,0:T(8,128)(2,1)S(1)}, bf16[512,128]{1,0:T(8,128)(2,1)S(1)}, u32[]{:S(2)}, u32[]{:S(2)}) collective-permute-start(bf16[512,128]{1,0:T(8,128)(2,1)S(1)} %get-tuple-element.71), channel_id=1, source_target_pairs={{0,40},{8,48},{16,56},{24,0},{32,8},{40,16},{48,24},{56,32},{64,10... | collective-permute-start | bytes 393224 | tf_op jit(solution)/shard_map/ppermute | solution.py:27
  50.7 0.0 collective-permute-done.13
  50.7 1.6 %collective-permute-start.18 = (bf16[512,128]{1,0:T(8,128)(2,1)S(1)}, bf16[512,128]{1,0:T(8,128)(2,1)S(1)}, u32[]{:S(2)}, u32[]{:S(2)}) collective-permute-start(bf16[512,128]{1,0:T(8,128)(2,1)S(1)} %get-tuple-element.72), channel_id=1, source_target_pairs={{0,32},{8,40},{16,48},{24,56},{32,0},{40,8},{48,16},{56,24},{64,96... | collective-permute-start | bytes 393224 | tf_op jit(solution)/shard_map/ppermute | solution.py:27
  52.3 2.4 %collective-permute-done.14 = bf16[512,128]{1,0:T(8,128)(2,1)S(1)} collective-permute-done((bf16[512,128]{1,0:T(8,128)(2,1)S(1)}, bf16[512,128]{1,0:T(8,128)(2,1)S(1)}, u32[]{:S(2)}, u32[]{:S(2)}) %collective-permute-start.14) | collective-permute-done | bytes 131104 | tf_op jit(solution)/shard_map/ppermute | solution.py:27
  54.7 0.4 collective-permute-start.19
  55.1 0.0 collective-permute-done.20
  55.1 0.4 collective-permute-start.22
  55.4 7.5 %collective-permute-done.21 = bf16[512,128]{1,0:T(8,128)(2,1)S(1)} collective-permute-done((bf16[512,128]{1,0:T(8,128)(2,1)S(1)}, bf16[512,128]{1,0:T(8,128)(2,1)S(1)}, u32[]{:S(2)}, u32[]{:S(2)}) %collective-permute-start.21) | collective-permute-done | bytes 131104 | tf_op jit(solution)/shard_map/ppermute | solution.py:27
  63.0 0.0 collective-permute-start.23
  63.0 0.0 collective-permute-done.17
  63.0 2.0 %collective-permute-start.24 = (bf16[1024,128]{1,0:T(8,128)(2,1)S(1)}, bf16[1024,128]{1,0:T(8,128)(2,1)S(1)}, u32[]{:S(2)}, u32[]{:S(2)}) collective-permute-start(bf16[1024,128]{1,0:T(8,128)(2,1)S(1)} %get-tuple-element.79), channel_id=1, source_target_pairs={{0,64},{8,72},{16,80},{24,88},{32,96},{40,104},{48,112},{56,120},{... | collective-permute-start | bytes 786440 | tf_op jit(solution)/shard_map/ppermute | solution.py:32
  65.0 0.0 collective-permute-done.18
  65.0 0.4 collective-permute-done.19
  65.4 0.9 %add_multiply_fusion = f32[512,128]{1,0:T(8,128)} fusion(bf16[512,128]{1,0:T(8,128)(2,1)S(1)} %collective-permute-done.21, bf16[512,128]{1,0:T(8,128)(2,1)S(1)} %collective-permute-done.20, bf16[512,128]{1,0:T(8,128)(2,1)S(1)} %collective-permute-done.19, bf16[512,128]{1,0:T(8,128)(2,1)S(1)} %collective-permute-done.18, ...), kind=kLoop, calls=%fused_computation.2 | loop fusion | flops 983040 | bytes 1441792 | tf_op jit(solution)/shard_map/mul | solution.py:264
  66.3 0.0 collective-permute-done.22
  66.3 3.1 %collective-permute-done.23 = bf16[1024,128]{1,0:T(8,128)(2,1)S(1)} collective-permute-done((bf16[1024,128]{1,0:T(8,128)(2,1)S(1)}, bf16[1024,128]{1,0:T(8,128)(2,1)S(1)}, u32[]{:S(2)}, u32[]{:S(2)}) %collective-permute-start.23) | collective-permute-done | bytes 262176 | tf_op jit(solution)/shard_map/ppermute | solution.py:32
  69.3 1.2 %collective-permute-done.24 = bf16[1024,128]{1,0:T(8,128)(2,1)S(1)} collective-permute-done((bf16[1024,128]{1,0:T(8,128)(2,1)S(1)}, bf16[1024,128]{1,0:T(8,128)(2,1)S(1)}, u32[]{:S(2)}, u32[]{:S(2)}) %collective-permute-start.24) | collective-permute-done | bytes 262176 | tf_op jit(solution)/shard_map/ppermute | solution.py:32
  70.6 0.9 %add_add_fusion = (f32[512,128]{1,0:T(8,128)}, f32[512,128]{1,0:T(8,128)}) fusion(f32[512,128]{1,0:T(8,128)S(1)} %get-tuple-element.80, bf16[1024,128]{1,0:T(8,128)(2,1)S(1)} %collective-permute-done.24, bf16[1024,128]{1,0:T(8,128)(2,1)S(1)} %collective-permute-done.23, bf16[1024,128]{1,0:T(8,128)(2,1)S(1)} %collective-permute-done.22, ...), kind=kLoop, calls=%fused_computation | loop fusion | flops 851968 | bytes 1835008 | tf_op jit(solution)/shard_map/add | solution.py:266
  (6 shorter events, 0.0 us)
Async XLA Ops:
  2.6 14.0 %collective-permute-start.1 = (bf16[1024,128]{1,0:T(8,128)(2,1)}, bf16[1024,128]{1,0:T(8,128)(2,1)S(1)}, u32[]{:S(2)}, u32[]{:S(2)}) collective-permute-start(bf16[1024,128]{1,0:T(8,128)(2,1)} %get-tuple-element.42.refs_3_), channel_id=1, source_target_pairs={{0,56},{8,0},{16,8},{24,16},{32,24},{40,32},{48,40},{56,48},{64,12... | collective-permute-start | bytes 786440 | tf_op jit(solution)/shard_map/ppermute | solution.py:27
  8.5 9.2 %collective-permute-start = (bf16[1024,128]{1,0:T(8,128)(2,1)}, bf16[1024,128]{1,0:T(8,128)(2,1)S(1)}, u32[]{:S(2)}, u32[]{:S(2)}) collective-permute-start(bf16[1024,128]{1,0:T(8,128)(2,1)} %get-tuple-element.42.refs_3_), channel_id=1, source_target_pairs={{0,8},{8,16},{16,24},{24,32},{32,40},{40,48},{48,56},{56,0},{64,72... | collective-permute-start | bytes 786440 | tf_op jit(solution)/shard_map/ppermute | solution.py:27
  8.5 13.4 %collective-permute-start.12 = (bf16[1024,128]{1,0:T(8,128)(2,1)}, bf16[1024,128]{1,0:T(8,128)(2,1)S(1)}, u32[]{:S(2)}, u32[]{:S(2)}) collective-permute-start(bf16[1024,128]{1,0:T(8,128)(2,1)} %get-tuple-element.53.refs_10_.refs_9_), channel_id=1, source_target_pairs={{0,192},{8,200},{16,208},{24,216},{32,224},{40,232},{48,240},{56,2... | collective-permute-start | bytes 786440 | tf_op jit(solution)/shard_map/ppermute | solution.py:32
  11.5 13.0 %collective-permute-start.10 = (bf16[1024,128]{1,0:T(8,128)(2,1)}, bf16[1024,128]{1,0:T(8,128)(2,1)S(1)}, u32[]{:S(2)}, u32[]{:S(2)}) collective-permute-start(bf16[1024,128]{1,0:T(8,128)(2,1)} %get-tuple-element.53.refs_10_.refs_9_), channel_id=1, source_target_pairs={{0,64},{8,72},{16,80},{24,88},{32,96},{40,104},{48,112},{56,120},{... | collective-permute-start | bytes 786440 | tf_op jit(solution)/shard_map/ppermute | solution.py:32
  17.7 1.0 %copy-start = (bf16[1024,128]{1,0:T(8,128)(2,1)S(1)}, bf16[1024,128]{1,0:T(8,128)(2,1)}, u32[]{:S(2)}) copy-start(bf16[1024,128]{1,0:T(8,128)(2,1)} %get-tuple-element.53.refs_10_.refs_9_) | copy-start | bytes 786436
  17.7 8.7 %collective-permute-start.4 = (bf16[512,128]{1,0:T(8,128)(2,1)S(1)}, bf16[512,128]{1,0:T(8,128)(2,1)S(1)}, u32[]{:S(2)}, u32[]{:S(2)}) collective-permute-start(bf16[512,128]{1,0:T(8,128)(2,1)S(1)} %get-tuple-element.85), channel_id=1, source_target_pairs={{0,8},{8,16},{16,24},{24,32},{32,40},{40,48},{48,56},{56,0},{64,72... | collective-permute-start | bytes 393224 | tf_op jit(solution)/shard_map/ppermute | solution.py:27
  17.8 15.7 %copy-start.1 = (f32[136,128]{1,0:T(8,128)S(1)}, f32[136,128]{1,0:T(8,128)}, u32[]{:S(2)}) copy-start(f32[136,128]{1,0:T(8,128)} %get-tuple-element.52.refs_2_) | copy-start | bytes 208900
  17.8 15.7 %copy-start.2 = (bf16[1024,128]{1,0:T(8,128)(2,1)S(1)}, bf16[1024,128]{1,0:T(8,128)(2,1)}, u32[]{:S(2)}) copy-start(bf16[1024,128]{1,0:T(8,128)(2,1)} %get-tuple-element.42.refs_3_) | copy-start | bytes 786436
  17.8 8.7 %collective-permute-start.2 = (bf16[512,128]{1,0:T(8,128)(2,1)S(1)}, bf16[512,128]{1,0:T(8,128)(2,1)S(1)}, u32[]{:S(2)}, u32[]{:S(2)}) collective-permute-start(bf16[512,128]{1,0:T(8,128)(2,1)S(1)} %get-tuple-element.86), channel_id=1, source_target_pairs={{0,8},{8,16},{16,24},{24,32},{32,40},{40,48},{48,56},{56,0},{64,72... | collective-permute-start | bytes 393224 | tf_op jit(solution)/shard_map/ppermute | solution.py:27
  18.6 14.9 %collective-permute-start.11 = (bf16[1024,128]{1,0:T(8,128)(2,1)S(1)}, bf16[1024,128]{1,0:T(8,128)(2,1)S(1)}, u32[]{:S(2)}, u32[]{:S(2)}) collective-permute-start(bf16[1024,128]{1,0:T(8,128)(2,1)S(1)} %copy-done), channel_id=1, source_target_pairs={{0,128},{8,136},{16,144},{24,152},{32,160},{40,168},{48,176},{56,1... | collective-permute-start | bytes 786440 | tf_op jit(solution)/shard_map/ppermute | solution.py:32
  21.8 11.7 %copy-start.3 = (s32[328]{0:T(512)S(1)}, s32[328]{0:T(512)}, u32[]{:S(2)}) copy-start(s32[328]{0:T(512)} %get-tuple-element.51.refs_1_) | copy-start | bytes 3940
  21.9 11.7 %copy-start.4 = (s32[2]{0:T(128)S(1)}, s32[2]{0:T(128)}, u32[]{:S(2)}) copy-start(s32[2]{0:T(128)} %get-tuple-element.50.refs_0_) | copy-start | bytes 28
  21.9 6.4 %collective-permute-start.8 = (bf16[512,128]{1,0:T(8,128)(2,1)S(1)}, bf16[512,128]{1,0:T(8,128)(2,1)S(1)}, u32[]{:S(2)}, u32[]{:S(2)}) collective-permute-start(bf16[512,128]{1,0:T(8,128)(2,1)S(1)} %get-tuple-element.83), channel_id=1, source_target_pairs={{0,56},{8,0},{16,8},{24,16},{32,24},{40,32},{48,40},{56,48},{64,12... | collective-permute-start | bytes 393224 | tf_op jit(solution)/shard_map/ppermute | solution.py:27
  24.5 6.2 %collective-permute-start.6 = (bf16[512,128]{1,0:T(8,128)(2,1)S(1)}, bf16[512,128]{1,0:T(8,128)(2,1)S(1)}, u32[]{:S(2)}, u32[]{:S(2)}) collective-permute-start(bf16[512,128]{1,0:T(8,128)(2,1)S(1)} %get-tuple-element.84), channel_id=1, source_target_pairs={{0,56},{8,0},{16,8},{24,16},{32,24},{40,32},{48,40},{56,48},{64,12... | collective-permute-start | bytes 393224 | tf_op jit(solution)/shard_map/ppermute | solution.py:27
  26.4 9.7 %collective-permute-start.5 = (bf16[512,128]{1,0:T(8,128)(2,1)S(1)}, bf16[512,128]{1,0:T(8,128)(2,1)S(1)}, u32[]{:S(2)}, u32[]{:S(2)}) collective-permute-start(bf16[512,128]{1,0:T(8,128)(2,1)S(1)} %collective-permute-done.4.refs_6_), channel_id=1, source_target_pairs={{0,8},{8,16},{16,24},{24,32},{32,40},{40,48},{48,56},{56,0},{64,72... | collective-permute-start | bytes 393224 | tf_op jit(solution)/shard_map/ppermute | solution.py:27
  26.5 9.6 %collective-permute-start.3 = (bf16[512,128]{1,0:T(8,128)(2,1)S(1)}, bf16[512,128]{1,0:T(8,128)(2,1)S(1)}, u32[]{:S(2)}, u32[]{:S(2)}) collective-permute-start(bf16[512,128]{1,0:T(8,128)(2,1)S(1)} %collective-permute-done.2.refs_7_), channel_id=1, source_target_pairs={{0,8},{8,16},{16,24},{24,32},{32,40},{40,48},{48,56},{56,0},{64,72... | collective-permute-start | bytes 393224 | tf_op jit(solution)/shard_map/ppermute | solution.py:27
  28.3 7.8 %collective-permute-start.9 = (bf16[512,128]{1,0:T(8,128)(2,1)S(1)}, bf16[512,128]{1,0:T(8,128)(2,1)S(1)}, u32[]{:S(2)}, u32[]{:S(2)}) collective-permute-start(bf16[512,128]{1,0:T(8,128)(2,1)S(1)} %collective-permute-done.8.refs_8_), channel_id=1, source_target_pairs={{0,56},{8,0},{16,8},{24,16},{32,24},{40,32},{48,40},{56,48},{64,12... | collective-permute-start | bytes 393224 | tf_op jit(solution)/shard_map/ppermute | solution.py:27
  30.7 6.0 %collective-permute-start.7 = (bf16[512,128]{1,0:T(8,128)(2,1)S(1)}, bf16[512,128]{1,0:T(8,128)(2,1)S(1)}, u32[]{:S(2)}, u32[]{:S(2)}) collective-permute-start(bf16[512,128]{1,0:T(8,128)(2,1)S(1)} %collective-permute-done.6.refs_9_), channel_id=1, source_target_pairs={{0,56},{8,0},{16,8},{24,16},{32,24},{40,32},{48,40},{56,48},{64,12... | collective-permute-start | bytes 393224 | tf_op jit(solution)/shard_map/ppermute | solution.py:27
  36.7 9.1 %copy-start.5 = (s32[200]{0:T(256)S(1)}, s32[200]{0:T(256)}, u32[]{:S(2)}) copy-start(s32[200]{0:T(256)} %get-tuple-element.64.refs_1_) | copy-start | bytes 2404
  36.7 9.0 %collective-permute-start.15 = (bf16[512,128]{1,0:T(8,128)(2,1)S(1)}, bf16[512,128]{1,0:T(8,128)(2,1)S(1)}, u32[]{:S(2)}, u32[]{:S(2)}) collective-permute-start(bf16[512,128]{1,0:T(8,128)(2,1)S(1)} %collective-permute-done.5.refs_4_), channel_id=1, source_target_pairs={{0,8},{8,16},{16,24},{24,32},{32,40},{40,48},{48,56},{56,0},{64,72... | collective-permute-start | bytes 393224 | tf_op jit(solution)/shard_map/ppermute | solution.py:27
  36.7 9.1 %collective-permute-start.16 = (bf16[512,128]{1,0:T(8,128)(2,1)S(1)}, bf16[512,128]{1,0:T(8,128)(2,1)S(1)}, u32[]{:S(2)}, u32[]{:S(2)}) collective-permute-start(bf16[512,128]{1,0:T(8,128)(2,1)S(1)} %collective-permute-done.7.refs_5_), channel_id=1, source_target_pairs={{0,56},{8,0},{16,8},{24,16},{32,24},{40,32},{48,40},{56,48},{64,12... | collective-permute-start | bytes 393224 | tf_op jit(solution)/shard_map/ppermute | solution.py:27
  40.4 10.3 %collective-permute-start.13 = (bf16[512,128]{1,0:T(8,128)(2,1)S(1)}, bf16[512,128]{1,0:T(8,128)(2,1)S(1)}, u32[]{:S(2)}, u32[]{:S(2)}) collective-permute-start(bf16[512,128]{1,0:T(8,128)(2,1)S(1)} %get-tuple-element.62), channel_id=1, source_target_pairs={{0,56},{8,0},{16,8},{24,16},{32,24},{40,32},{48,40},{56,48},{64,12... | collective-permute-start | bytes 393224 | tf_op jit(solution)/shard_map/ppermute | solution.py:27
  42.5 12.2 %collective-permute-start.14 = (bf16[512,128]{1,0:T(8,128)(2,1)S(1)}, bf16[512,128]{1,0:T(8,128)(2,1)S(1)}, u32[]{:S(2)}, u32[]{:S(2)}) collective-permute-start(bf16[512,128]{1,0:T(8,128)(2,1)S(1)} %get-tuple-element.63), channel_id=1, source_target_pairs={{0,48},{8,56},{16,0},{24,8},{32,16},{40,24},{48,32},{56,40},{64,11... | collective-permute-start | bytes 393224 | tf_op jit(solution)/shard_map/ppermute | solution.py:27
  42.5 12.6 %collective-permute-start.20 = (bf16[512,128]{1,0:T(8,128)(2,1)S(1)}, bf16[512,128]{1,0:T(8,128)(2,1)S(1)}, u32[]{:S(2)}, u32[]{:S(2)}) collective-permute-start(bf16[512,128]{1,0:T(8,128)(2,1)S(1)} %get-tuple-element.74), channel_id=1, source_target_pairs={{0,16},{8,24},{16,32},{24,40},{32,48},{40,56},{48,0},{56,8},{64,80... | collective-permute-start | bytes 393224 | tf_op jit(solution)/shard_map/ppermute | solution.py:27
  45.8 17.2 %collective-permute-start.21 = (bf16[512,128]{1,0:T(8,128)(2,1)S(1)}, bf16[512,128]{1,0:T(8,128)(2,1)S(1)}, u32[]{:S(2)}, u32[]{:S(2)}) collective-permute-start(bf16[512,128]{1,0:T(8,128)(2,1)S(1)} %get-tuple-element.75), channel_id=1, source_target_pairs={{0,8},{8,16},{16,24},{24,32},{32,40},{40,48},{48,56},{56,0},{64,72... | collective-permute-start | bytes 393224 | tf_op jit(solution)/shard_map/ppermute | solution.py:27
  47.6 15.3 %collective-permute-start.17 = (bf16[512,128]{1,0:T(8,128)(2,1)S(1)}, bf16[512,128]{1,0:T(8,128)(2,1)S(1)}, u32[]{:S(2)}, u32[]{:S(2)}) collective-permute-start(bf16[512,128]{1,0:T(8,128)(2,1)S(1)} %get-tuple-element.71), channel_id=1, source_target_pairs={{0,40},{8,48},{16,56},{24,0},{32,8},{40,16},{48,24},{56,32},{64,10... | collective-permute-start | bytes 393224 | tf_op jit(solution)/shard_map/ppermute | solution.py:27
  50.7 14.3 %collective-permute-start.18 = (bf16[512,128]{1,0:T(8,128)(2,1)S(1)}, bf16[512,128]{1,0:T(8,128)(2,1)S(1)}, u32[]{:S(2)}, u32[]{:S(2)}) collective-permute-start(bf16[512,128]{1,0:T(8,128)(2,1)S(1)} %get-tuple-element.72), channel_id=1, source_target_pairs={{0,32},{8,40},{16,48},{24,56},{32,0},{40,8},{48,16},{56,24},{64,96... | collective-permute-start | bytes 393224 | tf_op jit(solution)/shard_map/ppermute | solution.py:27
  54.7 10.7 %collective-permute-start.19 = (bf16[512,128]{1,0:T(8,128)(2,1)S(1)}, bf16[512,128]{1,0:T(8,128)(2,1)S(1)}, u32[]{:S(2)}, u32[]{:S(2)}) collective-permute-start(bf16[512,128]{1,0:T(8,128)(2,1)S(1)} %get-tuple-element.73), channel_id=1, source_target_pairs={{0,24},{8,32},{16,40},{24,48},{32,56},{40,0},{48,8},{56,16},{64,88... | collective-permute-start | bytes 393224 | tf_op jit(solution)/shard_map/ppermute | solution.py:27
  55.1 11.2 %collective-permute-start.22 = (bf16[1024,128]{1,0:T(8,128)(2,1)S(1)}, bf16[1024,128]{1,0:T(8,128)(2,1)S(1)}, u32[]{:S(2)}, u32[]{:S(2)}) collective-permute-start(bf16[1024,128]{1,0:T(8,128)(2,1)S(1)} %get-tuple-element.77), channel_id=1, source_target_pairs={{0,128},{8,136},{16,144},{24,152},{32,160},{40,168},{48,176},{56,1... | collective-permute-start | bytes 786440 | tf_op jit(solution)/shard_map/ppermute | solution.py:32
  63.0 6.4 %collective-permute-start.23 = (bf16[1024,128]{1,0:T(8,128)(2,1)S(1)}, bf16[1024,128]{1,0:T(8,128)(2,1)S(1)}, u32[]{:S(2)}, u32[]{:S(2)}) collective-permute-start(bf16[1024,128]{1,0:T(8,128)(2,1)S(1)} %get-tuple-element.78), channel_id=1, source_target_pairs={{0,192},{8,200},{16,208},{24,216},{32,224},{40,232},{48,240},{56,2... | collective-permute-start | bytes 786440 | tf_op jit(solution)/shard_map/ppermute | solution.py:32
  63.0 7.6 %collective-permute-start.24 = (bf16[1024,128]{1,0:T(8,128)(2,1)S(1)}, bf16[1024,128]{1,0:T(8,128)(2,1)S(1)}, u32[]{:S(2)}, u32[]{:S(2)}) collective-permute-start(bf16[1024,128]{1,0:T(8,128)(2,1)S(1)} %get-tuple-element.79), channel_id=1, source_target_pairs={{0,64},{8,72},{16,80},{24,88},{32,96},{40,104},{48,112},{56,120},{... | collective-permute-start | bytes 786440 | tf_op jit(solution)/shard_map/ppermute | solution.py:32

commit v4 on v3

--- a/solution.py
+++ b/solution.py
@@ -83,7 +83,7 @@
 
 
 def stack_pairs(a, b, c, d):
-    out = jax.ShapeDtypeStruct((2 * a.shape[0], a.shape[1]), a.dtype)
+    out = pltpu.VMEM((2 * a.shape[0], a.shape[1]), a.dtype)
     return pl.pallas_call(
         stack_kernel,
         out_shape=[out, out],
@@ -94,13 +94,33 @@
     )(a, b, c, d)
 
 
+def pack_kernel(ahead_ref, behind_ref, up_ref, down_ref, ahead_out, behind_out):
+    rows = up_ref.shape[0]
+    ahead_out[pl.ds(0, rows), :] = ahead_ref[pl.ds(0, rows), :]
+    ahead_out[pl.ds(rows, rows), :] = up_ref[...]
+    behind_out[pl.ds(0, rows), :] = behind_ref[pl.ds(rows, rows), :]
+    behind_out[pl.ds(rows, rows), :] = down_ref[...]
+
+
+def pack_last_step(ahead, behind, up, down):
+    vmem = pl.BlockSpec(memory_space=pltpu.VMEM)
+    return pl.pallas_call(
+        pack_kernel,
+        out_shape=[pltpu.VMEM(ahead.shape, ahead.dtype)] * 2,
+        in_specs=[vmem] * 4,
+        out_specs=[vmem] * 2,
+        compiler_params=pltpu.CompilerParams(vmem_limit_bytes=2 * 1024 * 1024),
+        cost_estimate=pl.CostEstimate(flops=0, bytes_accessed=500_000, transcendentals=0),
+    )(ahead, behind, up, down)
+
+
 def make_plan(me, block_order, block_mask):
     smem = pl.BlockSpec(memory_space=pltpu.SMEM)
     vmem = pl.BlockSpec(memory_space=pltpu.VMEM)
     return pl.pallas_call(
         plan_kernel,
         out_shape=[
-            jax.ShapeDtypeStruct((BLK + 8, BLK), f32),
+            pltpu.VMEM((BLK + 8, BLK), f32),
             jax.ShapeDtypeStruct((len(GROUPS),), i32),
         ]
         + [jax.ShapeDtypeStruct((n,), i32) for n in list_sizes()],
@@ -224,7 +244,7 @@
         in_specs=[smem, smem] + [vmem] * (1 + len(row_arrays) + NY + len(acc)),
         out_specs=[vmem] * len(outs),
         scratch_shapes=scratch,
-        compiler_params=pltpu.CompilerParams(vmem_limit_bytes=32 * 1024 * 1024),
+        compiler_params=pltpu.CompilerParams(vmem_limit_bytes=16 * 1024 * 1024),
         cost_estimate=pl.CostEstimate(
             flops=tiles * 10 * BLK**3, bytes_accessed=4_000_000, transcendentals=tiles * BLK * BLK
         ),
@@ -238,28 +258,34 @@
     plan = make_plan(me, block_order, block_mask)
     qg, kv = stack_pairs(queries, out_grad, keys, values)
     ahead, behind = z_shift(qg, 1), z_shift(qg, -1)
-    kvs = [kv, y_shift(kv, 1), None, y_shift(kv, 3)]
-    (ahead, behind), plan, kv = lax.optimization_barrier(((ahead, behind), plan, kv))
-    kvs[2] = y_shift(kv, 2)
+    far_kv = y_shift(kv, 2)
+    (ahead, behind), plan, far_kv, kv = lax.optimization_barrier(
+        ((ahead, behind), plan, far_kv, kv)
+    )
+    kvs = [kv, y_shift(kv, 1), far_kv, y_shift(kv, 3)]
     shards = {0: {"qg": qg}, 1: {"qg": ahead}, NZ - 1: {"qg": behind}}
-    split = lambda a: {"q": a[:rows], "g": a[rows:]}
-    ahead, behind = split(ahead), split(behind)
     for s in range(2, NZ // 2):
-        ahead = {kind: z_shift(a, 1) for kind, a in ahead.items()}
-        behind = {kind: z_shift(a, -1) for kind, a in behind.items()}
-        shards[s], shards[NZ - s] = ahead, behind
+        ahead, behind = z_shift(ahead, 1), z_shift(behind, -1)
+        shards[s], shards[NZ - s] = {"qg": ahead}, {"qg": behind}
+
     back, acc = {}, ()
     for g, group in enumerate(GROUPS):
         out = run_pairs(g, plan, shards, kvs, acc)
         if g == 0:
             ahead, behind, out = lax.optimization_barrier((ahead, behind, out))
-            shards[NZ // 2 - 1], shards[NZ // 2 + 1] = ahead, behind
-            shards[NZ // 2] = {"q": z_shift(ahead["q"], 1), "g": z_shift(behind["g"], -1)}
+            shards[NZ // 2 - 1], shards[NZ // 2 + 1] = {"qg": ahead}, {"qg": behind}
+            up, down = pack_last_step(
+                ahead, behind, out[group.index(NZ - 1)], out[group.index(1)]
+            )
+            up, down = z_shift(up, 1), z_shift(down, -1)
+            shards[NZ // 2] = {"q": up, "g": down}
+            back[NZ - 1], back[1] = up[rows:], down[rows:]
         acc = tuple(out[len(group) :])
         if g == len(GROUPS) - 1:
             kv_back = [y_shift(acc[t + 1], -t) for t in (2, 1, 3)]
         for s, dq in reversed(list(zip(group, out))):
-            back[s] = dq if s == 0 else z_shift(dq, -s)
+            if s not in back:
+                back[s] = dq if s == 0 else z_shift(dq, -s)
     own_k, own_v = acc[0], acc[1]
     query_grad = sum(back[s].astype(f32) for s in range(NZ)) * scale
     key_grad = own_k + sum(p[:rows].astype(f32) for p in kv_back) * scale

time: 71.3 us -> 70.3 us (0.986)
  starting transfers between devices: 38.3 us -> 33 us
  waiting for transfers between devices: 18.6 us -> 22.2 us
  Pallas kernels: 11.3 us -> 12.7 us
  local copies, waits for them, and re-layouts: 0.78 us -> 0.01 us
    ppermute x19 -> x13, starting transfers between devices: 29.7 us -> 24.4 us  [z_shift(): return lax.ppermute(a, 'seq', route)]
    ppermute x19 -> x13, waiting for transfers between devices: 14.3 us -> 18.3 us  [z_shift(): return lax.ppermute(a, 'seq', route)]
    pallas_call x2, Pallas kernels: 4.35 us -> 6.69 us  [run_pairs(): pl.pallas_call(functools.partial(pairs_kernel, g, first, last, row_parts)...]
    pallas_call x1, Pallas kernels: 1.92 us -> 1.13 us  [stack_pairs(): pl.pallas_call(stack_kernel, out_shape=[out, out], in_specs=[pl.BlockSpec...]
    unnamed x12 -> x6, local copies, waits for them, and re-layouts: 0.75 us -> 0.01 us
    pallas_call x1 -> x2, Pallas kernels: 4.99 us -> 4.86 us  [the longest x1 4.82 us: make_plan(): pl.pallas_call(plan_kernel, out_shape=[pltpu.VMEM((BLK + 8, BLK), f32), j...]
  transfers between devices with their start and end apart: 25 -> 19, of which waited for: 10 -> 10; matrix products, arithmetic and copies ran while one was open for 1% -> 1% of each run, Pallas kernels for 13% -> 16%
where the time goes in v4:
time: 70.3 us; the launch traced here: 70.4 us
  starting transfers between devices  33 us (47%)
  waiting for transfers between devices  22.2 us (32%)
  Pallas kernels  12.7 us (18%)
  other arithmetic  1.75 us (2%)
  between operations  0.71 us (1%)
    ppermute x13, starting transfers between devices, z_shift(): return lax.ppermute(a, 'seq', route)  24.4 us
    ppermute x13, waiting for transfers between devices, z_shift(): return lax.ppermute(a, 'seq', route)  18.3 us
    ppermute x6, starting transfers between devices, y_shift(): return lax.ppermute(a, 'seq', route)  8.66 us
    pallas_call x2, Pallas kernels, run_pairs(): pl.pallas_call(functools.partial(pairs_kernel, g, first, last, row_parts)...  6.69 us
    pallas_call x1, Pallas kernels, make_plan(): pl.pallas_call(plan_kernel, out_shape=[pltpu.VMEM((BLK + 8, BLK), f32), j...  4.82 us
    ppermute x6, waiting for transfers between devices, y_shift(): return lax.ppermute(a, 'seq', route)  3.97 us
  transfers between devices with their start and end apart: 19, of which 10 were waited for; matrix products, arithmetic and copies ran while one was open for 1% of the time, Pallas kernels for 16%

profile of v4, /device:TPU:2, one launch (start us, length us, event | category | flops | bytes accessed | tf_op | source)
XLA Modules:
  0.0 70.4 jit_solution(8646984861213393808)
XLA Ops:
  0.6 1.1 %shard_map.85 = (bf16[1024,128]{1,0:T(8,128)(2,1)S(1)}, bf16[1024,128]{1,0:T(8,128)(2,1)S(1)}) custom-call(bf16[512,128]{1,0:T(8,128)(2,1)} %a_ref.1, bf16[512,128]{1,0:T(8,128)(2,1)} %b_ref.1, bf16[512,128]{1,0:T(8,128)(2,1)} %c_ref.1, bf16[512,128]{1,0:T(8,128)(2,1)} %d_ref.1), custom_call_target="tpu_custom_call" | custom-call | bytes 1000000 | tf_op jit(solution)/shard_map/pallas_call | solution.py:87
  1.8 3.3 %collective-permute-start.2 = (bf16[1024,128]{1,0:T(8,128)(2,1)S(1)}, bf16[1024,128]{1,0:T(8,128)(2,1)S(1)}, u32[]{:S(2)}, u32[]{:S(2)}) collective-permute-start(bf16[1024,128]{1,0:T(8,128)(2,1)S(1)} %get-tuple-element.54.refs_8_.refs_7_), channel_id=1, source_target_pairs={{0,128},{8,136},{16,144},{24,152},{32,160},{40,168},{48,176},{56,1... | collective-permute-start | bytes 786440 | tf_op jit(solution)/shard_map/ppermute | solution.py:32
  5.0 5.9 %collective-permute-start.1 = (bf16[1024,128]{1,0:T(8,128)(2,1)S(1)}, bf16[1024,128]{1,0:T(8,128)(2,1)S(1)}, u32[]{:S(2)}, u32[]{:S(2)}) collective-permute-start(bf16[1024,128]{1,0:T(8,128)(2,1)S(1)} %get-tuple-element.43.refs_3_), channel_id=1, source_target_pairs={{0,56},{8,0},{16,8},{24,16},{32,24},{40,32},{48,40},{56,48},{64,12... | collective-permute-start | bytes 786440 | tf_op jit(solution)/shard_map/ppermute | solution.py:27
  10.9 0.0 collective-permute-start
  10.9 4.8 %shard_map.86 = (f32[136,128]{1,0:T(8,128)S(1)}, s32[2]{0:T(128)}, s32[328]{0:T(512)}, s32[200]{0:T(256)}) custom-call(s32[1]{0:T(128)} %bitcast.me_ref, s32[128]{0:T(128)} %order_ref.1, s32[128,128]{1,0:T(8,128)} %vmask_ref.1, s32[128,128]{1,0:T(8,128)} %vmask_ref.1), custom_call_target="tpu_custom_call" | custom-call | flops 10000 | bytes 200000 | tf_op jit(solution)/shard_map/pallas_call | solution.py:120
  15.7 0.0 collective-permute-done.2.refs_10_.refs_9_
  15.8 0.4 collective-permute-done.1.refs_5_
  16.2 3.4 %collective-permute-done.refs_4_ = bf16[1024,128]{1,0:T(8,128)(2,1)S(1)} collective-permute-done((bf16[1024,128]{1,0:T(8,128)(2,1)S(1)}, bf16[1024,128]{1,0:T(8,128)(2,1)S(1)}, u32[]{:S(2)}, u32[]{:S(2)}) %collective-permute-start) | collective-permute-done | bytes 262176 | tf_op jit(solution)/shard_map/ppermute | solution.py:27
  19.6 0.0 copy-start
  19.6 0.0 copy-start.1
  19.6 0.0 collective-permute-start.3
  19.6 3.2 %collective-permute-start.5 = (bf16[1024,128]{1,0:T(8,128)(2,1)S(1)}, bf16[1024,128]{1,0:T(8,128)(2,1)S(1)}, u32[]{:S(2)}, u32[]{:S(2)}) collective-permute-start(bf16[1024,128]{1,0:T(8,128)(2,1)S(1)} %collective-permute-done.1.refs_5_), channel_id=1, source_target_pairs={{0,56},{8,0},{16,8},{24,16},{32,24},{40,32},{48,40},{56,48},{64,12... | collective-permute-start | bytes 786440 | tf_op jit(solution)/shard_map/ppermute | solution.py:27
  22.8 1.1 %collective-permute-start.8 = (bf16[1024,128]{1,0:T(8,128)(2,1)S(1)}, bf16[1024,128]{1,0:T(8,128)(2,1)S(1)}, u32[]{:S(2)}, u32[]{:S(2)}) collective-permute-start(bf16[1024,128]{1,0:T(8,128)(2,1)S(1)} %get-tuple-element.54.refs_8_.refs_7_), channel_id=1, source_target_pairs={{0,192},{8,200},{16,208},{24,216},{32,224},{40,232},{48,240},{56,2... | collective-permute-start | bytes 786440 | tf_op jit(solution)/shard_map/ppermute | solution.py:32
  23.9 1.0 %collective-permute-start.7 = (bf16[1024,128]{1,0:T(8,128)(2,1)S(1)}, bf16[1024,128]{1,0:T(8,128)(2,1)S(1)}, u32[]{:S(2)}, u32[]{:S(2)}) collective-permute-start(bf16[1024,128]{1,0:T(8,128)(2,1)S(1)} %get-tuple-element.54.refs_8_.refs_7_), channel_id=1, source_target_pairs={{0,64},{8,72},{16,80},{24,88},{32,96},{40,104},{48,112},{56,120},{... | collective-permute-start | bytes 786440 | tf_op jit(solution)/shard_map/ppermute | solution.py:32
  24.9 2.5 %collective-permute-done.3.refs_6_ = bf16[1024,128]{1,0:T(8,128)(2,1)S(1)} collective-permute-done((bf16[1024,128]{1,0:T(8,128)(2,1)S(1)}, bf16[1024,128]{1,0:T(8,128)(2,1)S(1)}, u32[]{:S(2)}, u32[]{:S(2)}) %collective-permute-start.3) | collective-permute-done | bytes 262176 | tf_op jit(solution)/shard_map/ppermute | solution.py:27
  27.4 0.0 collective-permute-start.4
  27.4 0.0 collective-permute-done.5.refs_7_
  27.4 3.2 %collective-permute-start.6 = (bf16[1024,128]{1,0:T(8,128)(2,1)S(1)}, bf16[1024,128]{1,0:T(8,128)(2,1)S(1)}, u32[]{:S(2)}, u32[]{:S(2)}) collective-permute-start(bf16[1024,128]{1,0:T(8,128)(2,1)S(1)} %collective-permute-done.5.refs_7_), channel_id=1, source_target_pairs={{0,56},{8,0},{16,8},{24,16},{32,24},{40,32},{48,40},{56,48},{64,12... | collective-permute-start | bytes 786440 | tf_op jit(solution)/shard_map/ppermute | solution.py:27
  30.6 0.0 collective-permute-done.8.refs_11_.refs_10_
  30.6 0.9 %collective-permute-done.7.refs_9_.refs_8_ = bf16[1024,128]{1,0:T(8,128)(2,1)S(1)} collective-permute-done((bf16[1024,128]{1,0:T(8,128)(2,1)S(1)}, bf16[1024,128]{1,0:T(8,128)(2,1)S(1)}, u32[]{:S(2)}, u32[]{:S(2)}) %collective-permute-start.7) | collective-permute-done | bytes 262176 | tf_op jit(solution)/shard_map/ppermute | solution.py:32
  31.5 0.0 copy-done
  31.5 0.0 copy-done.1
  31.5 3.2 %shard_map.87 = (f32[512,128]{1,0:T(8,128)S(1)}, bf16[512,128]{1,0:T(8,128)(2,1)S(1)}, bf16[512,128]{1,0:T(8,128)(2,1)S(1)}, bf16[512,128]{1,0:T(8,128)(2,1)S(1)...) custom-call(s32[2]{0:T(128)S(1)} %copy-done.1, s32[328]{0:T(512)S(1)} %copy-done, ...), custom_call_target="tpu_custom_call" | custom-call | flops 419430400 | bytes 4000000 | tf_op jit(solution)/shard_map/pallas_call | solution.py:241
  34.7 0.2 collective-permute-done.4.ahead_ref.refs_3_
  35.0 0.0 collective-permute-done.6.behind_ref.refs_4_
  35.0 0.0 copy-start.2
  35.0 3.3 %collective-permute-start.9 = (bf16[1024,128]{1,0:T(8,128)(2,1)S(1)}, bf16[1024,128]{1,0:T(8,128)(2,1)S(1)}, u32[]{:S(2)}, u32[]{:S(2)}) collective-permute-start(bf16[1024,128]{1,0:T(8,128)(2,1)S(1)} %get-tuple-element.68), channel_id=1, source_target_pairs={{0,56},{8,0},{16,8},{24,16},{32,24},{40,32},{48,40},{56,48},{64,12... | collective-permute-start | bytes 786440 | tf_op jit(solution)/shard_map/ppermute | solution.py:27
  38.3 0.0 collective-permute-start.11
  38.3 1.5 %collective-permute-start.10 = (bf16[512,128]{1,0:T(8,128)(2,1)S(1)}, bf16[512,128]{1,0:T(8,128)(2,1)S(1)}, u32[]{:S(2)}, u32[]{:S(2)}) collective-permute-start(bf16[512,128]{1,0:T(8,128)(2,1)S(1)} %get-tuple-element.69), channel_id=1, source_target_pairs={{0,48},{8,56},{16,0},{24,8},{32,16},{40,24},{48,32},{56,40},{64,11... | collective-permute-start | bytes 393224 | tf_op jit(solution)/shard_map/ppermute | solution.py:27
  39.9 1.4 %collective-permute-start.15 = (bf16[512,128]{1,0:T(8,128)(2,1)S(1)}, bf16[512,128]{1,0:T(8,128)(2,1)S(1)}, u32[]{:S(2)}, u32[]{:S(2)}) collective-permute-start(bf16[512,128]{1,0:T(8,128)(2,1)S(1)} %get-tuple-element.77), channel_id=1, source_target_pairs={{0,16},{8,24},{16,32},{24,40},{32,48},{40,56},{48,0},{56,8},{64,80... | collective-permute-start | bytes 393224 | tf_op jit(solution)/shard_map/ppermute | solution.py:27
  41.3 5.0 %collective-permute-done.9.refs_6_ = bf16[1024,128]{1,0:T(8,128)(2,1)S(1)} collective-permute-done((bf16[1024,128]{1,0:T(8,128)(2,1)S(1)}, bf16[1024,128]{1,0:T(8,128)(2,1)S(1)}, u32[]{:S(2)}, u32[]{:S(2)}) %collective-permute-start.9) | collective-permute-done | bytes 262176 | tf_op jit(solution)/shard_map/ppermute | solution.py:27
  46.3 0.0 collective-permute-done.11.refs_5_
  46.3 0.0 copy-done.2
  46.3 3.5 %shard_map.89 = (bf16[512,128]{1,0:T(8,128)(2,1)S(1)}, bf16[512,128]{1,0:T(8,128)(2,1)S(1)}, bf16[512,128]{1,0:T(8,128)(2,1)S(1)}, f32[512,128]{1,0:T(8,128)S(1)...) custom-call(s32[2]{0:T(128)S(1)} %copy-done.1, ...), custom_call_target="tpu_custom_call" | custom-call | flops 251658240 | bytes 4000000 | tf_op jit(solution)/shard_map/pallas_call | solution.py:241
  49.8 0.1 collective-permute-start.12
  49.8 3.6 %collective-permute-start.13 = (bf16[512,128]{1,0:T(8,128)(2,1)S(1)}, bf16[512,128]{1,0:T(8,128)(2,1)S(1)}, u32[]{:S(2)}, u32[]{:S(2)}) collective-permute-start(bf16[512,128]{1,0:T(8,128)(2,1)S(1)} %get-tuple-element.75), channel_id=1, source_target_pairs={{0,32},{8,40},{16,48},{24,56},{32,0},{40,8},{48,16},{56,24},{64,96... | collective-permute-start | bytes 393224 | tf_op jit(solution)/shard_map/ppermute | solution.py:27
  53.4 2.2 %collective-permute-start.14 = (bf16[512,128]{1,0:T(8,128)(2,1)S(1)}, bf16[512,128]{1,0:T(8,128)(2,1)S(1)}, u32[]{:S(2)}, u32[]{:S(2)}) collective-permute-start(bf16[512,128]{1,0:T(8,128)(2,1)S(1)} %get-tuple-element.76), channel_id=1, source_target_pairs={{0,24},{8,32},{16,40},{24,48},{32,56},{40,0},{48,8},{56,16},{64,88... | collective-permute-start | bytes 393224 | tf_op jit(solution)/shard_map/ppermute | solution.py:27
  55.6 0.0 collective-permute-done.10
  55.6 1.3 %collective-permute-start.16 = (bf16[1024,128]{1,0:T(8,128)(2,1)S(1)}, bf16[1024,128]{1,0:T(8,128)(2,1)S(1)}, u32[]{:S(2)}, u32[]{:S(2)}) collective-permute-start(bf16[1024,128]{1,0:T(8,128)(2,1)S(1)} %get-tuple-element.79), channel_id=1, source_target_pairs={{0,128},{8,136},{16,144},{24,152},{32,160},{40,168},{48,176},{56,1... | collective-permute-start | bytes 786440 | tf_op jit(solution)/shard_map/ppermute | solution.py:32
  56.8 0.0 collective-permute-done.15
  56.8 2.1 %collective-permute-start.17 = (bf16[1024,128]{1,0:T(8,128)(2,1)S(1)}, bf16[1024,128]{1,0:T(8,128)(2,1)S(1)}, u32[]{:S(2)}, u32[]{:S(2)}) collective-permute-start(bf16[1024,128]{1,0:T(8,128)(2,1)S(1)} %get-tuple-element.80), channel_id=1, source_target_pairs={{0,192},{8,200},{16,208},{24,216},{32,224},{40,232},{48,240},{56,2... | collective-permute-start | bytes 786440 | tf_op jit(solution)/shard_map/ppermute | solution.py:32
  58.9 3.0 %collective-permute-done.12 = bf16[512,128]{1,0:T(8,128)(2,1)S(1)} collective-permute-done((bf16[512,128]{1,0:T(8,128)(2,1)S(1)}, bf16[512,128]{1,0:T(8,128)(2,1)S(1)}, u32[]{:S(2)}, u32[]{:S(2)}) %collective-permute-start.12) | collective-permute-done | bytes 131104 | tf_op jit(solution)/shard_map/ppermute | solution.py:27
  61.9 0.0 collective-permute-start.18
  61.9 0.4 collective-permute-done.13
  62.3 3.3 %collective-permute-done.14 = bf16[512,128]{1,0:T(8,128)(2,1)S(1)} collective-permute-done((bf16[512,128]{1,0:T(8,128)(2,1)S(1)}, bf16[512,128]{1,0:T(8,128)(2,1)S(1)}, u32[]{:S(2)}, u32[]{:S(2)}) %collective-permute-start.14) | collective-permute-done | bytes 131104 | tf_op jit(solution)/shard_map/ppermute | solution.py:27
  65.6 0.8 %add_multiply_fusion = f32[512,128]{1,0:T(8,128)} fusion(bf16[512,128]{1,0:T(8,128)(2,1)S(1)} %collective-permute-done.15, bf16[512,128]{1,0:T(8,128)(2,1)S(1)} %collective-permute-done.14, bf16[512,128]{1,0:T(8,128)(2,1)S(1)} %collective-permute-done.13, bf16[512,128]{1,0:T(8,128)(2,1)S(1)} %collective-permute-done.12, ...), kind=kLoop, calls=%fused_computation.2 | loop fusion | flops 983040 | bytes 1441792 | tf_op jit(solution)/shard_map/mul | solution.py:290
  66.4 0.0 collective-permute-done.16
  66.4 0.0 collective-permute-done.17
  66.4 3.1 %collective-permute-done.18 = bf16[1024,128]{1,0:T(8,128)(2,1)S(1)} collective-permute-done((bf16[1024,128]{1,0:T(8,128)(2,1)S(1)}, bf16[1024,128]{1,0:T(8,128)(2,1)S(1)}, u32[]{:S(2)}, u32[]{:S(2)}) %collective-permute-start.18) | collective-permute-done | bytes 262176 | tf_op jit(solution)/shard_map/ppermute | solution.py:32
  69.5 0.9 %add_add_fusion = (f32[512,128]{1,0:T(8,128)}, f32[512,128]{1,0:T(8,128)}) fusion(f32[512,128]{1,0:T(8,128)S(1)} %get-tuple-element.82, bf16[1024,128]{1,0:T(8,128)(2,1)S(1)} %collective-permute-done.18, bf16[1024,128]{1,0:T(8,128)(2,1)S(1)} %collective-permute-done.17, bf16[1024,128]{1,0:T(8,128)(2,1)S(1)} %collective-permute-done.16, ...), kind=kLoop, calls=%fused_computation | loop fusion | flops 851968 | bytes 1835008 | tf_op jit(solution)/shard_map/add | solution.py:292
  (1 shorter events, 0.0 us)
Async XLA Ops:
  1.8 14.0 %collective-permute-start.2 = (bf16[1024,128]{1,0:T(8,128)(2,1)S(1)}, bf16[1024,128]{1,0:T(8,128)(2,1)S(1)}, u32[]{:S(2)}, u32[]{:S(2)}) collective-permute-start(bf16[1024,128]{1,0:T(8,128)(2,1)S(1)} %get-tuple-element.54.refs_8_.refs_7_), channel_id=1, source_target_pairs={{0,128},{8,136},{16,144},{24,152},{32,160},{40,168},{48,176},{56,1... | collective-permute-start | bytes 786440 | tf_op jit(solution)/shard_map/ppermute | solution.py:32
  5.0 11.1 %collective-permute-start.1 = (bf16[1024,128]{1,0:T(8,128)(2,1)S(1)}, bf16[1024,128]{1,0:T(8,128)(2,1)S(1)}, u32[]{:S(2)}, u32[]{:S(2)}) collective-permute-start(bf16[1024,128]{1,0:T(8,128)(2,1)S(1)} %get-tuple-element.43.refs_3_), channel_id=1, source_target_pairs={{0,56},{8,0},{16,8},{24,16},{32,24},{40,32},{48,40},{56,48},{64,12... | collective-permute-start | bytes 786440 | tf_op jit(solution)/shard_map/ppermute | solution.py:27
  10.9 8.7 %collective-permute-start = (bf16[1024,128]{1,0:T(8,128)(2,1)S(1)}, bf16[1024,128]{1,0:T(8,128)(2,1)S(1)}, u32[]{:S(2)}, u32[]{:S(2)}) collective-permute-start(bf16[1024,128]{1,0:T(8,128)(2,1)S(1)} %get-tuple-element.43.refs_3_), channel_id=1, source_target_pairs={{0,8},{8,16},{16,24},{24,32},{32,40},{40,48},{48,56},{56,0},{64,72... | collective-permute-start | bytes 786440 | tf_op jit(solution)/shard_map/ppermute | solution.py:27
  19.6 11.9 %copy-start = (s32[328]{0:T(512)S(1)}, s32[328]{0:T(512)}, u32[]{:S(2)}) copy-start(s32[328]{0:T(512)} %get-tuple-element.52.refs_1_) | copy-start | bytes 3940
  19.6 11.9 %copy-start.1 = (s32[2]{0:T(128)S(1)}, s32[2]{0:T(128)}, u32[]{:S(2)}) copy-start(s32[2]{0:T(128)} %get-tuple-element.51.refs_0_) | copy-start | bytes 28
  19.6 7.8 %collective-permute-start.3 = (bf16[1024,128]{1,0:T(8,128)(2,1)S(1)}, bf16[1024,128]{1,0:T(8,128)(2,1)S(1)}, u32[]{:S(2)}, u32[]{:S(2)}) collective-permute-start(bf16[1024,128]{1,0:T(8,128)(2,1)S(1)} %collective-permute-done.refs_4_), channel_id=1, source_target_pairs={{0,8},{8,16},{16,24},{24,32},{32,40},{40,48},{48,56},{56,0},{64,72... | collective-permute-start | bytes 786440 | tf_op jit(solution)/shard_map/ppermute | solution.py:27
  19.6 7.8 %collective-permute-start.5 = (bf16[1024,128]{1,0:T(8,128)(2,1)S(1)}, bf16[1024,128]{1,0:T(8,128)(2,1)S(1)}, u32[]{:S(2)}, u32[]{:S(2)}) collective-permute-start(bf16[1024,128]{1,0:T(8,128)(2,1)S(1)} %collective-permute-done.1.refs_5_), channel_id=1, source_target_pairs={{0,56},{8,0},{16,8},{24,16},{32,24},{40,32},{48,40},{56,48},{64,12... | collective-permute-start | bytes 786440 | tf_op jit(solution)/shard_map/ppermute | solution.py:27
  22.8 7.8 %collective-permute-start.8 = (bf16[1024,128]{1,0:T(8,128)(2,1)S(1)}, bf16[1024,128]{1,0:T(8,128)(2,1)S(1)}, u32[]{:S(2)}, u32[]{:S(2)}) collective-permute-start(bf16[1024,128]{1,0:T(8,128)(2,1)S(1)} %get-tuple-element.54.refs_8_.refs_7_), channel_id=1, source_target_pairs={{0,192},{8,200},{16,208},{24,216},{32,224},{40,232},{48,240},{56,2... | collective-permute-start | bytes 786440 | tf_op jit(solution)/shard_map/ppermute | solution.py:32
  23.9 7.6 %collective-permute-start.7 = (bf16[1024,128]{1,0:T(8,128)(2,1)S(1)}, bf16[1024,128]{1,0:T(8,128)(2,1)S(1)}, u32[]{:S(2)}, u32[]{:S(2)}) collective-permute-start(bf16[1024,128]{1,0:T(8,128)(2,1)S(1)} %get-tuple-element.54.refs_8_.refs_7_), channel_id=1, source_target_pairs={{0,64},{8,72},{16,80},{24,88},{32,96},{40,104},{48,112},{56,120},{... | collective-permute-start | bytes 786440 | tf_op jit(solution)/shard_map/ppermute | solution.py:32
  27.4 7.6 %collective-permute-start.4 = (bf16[1024,128]{1,0:T(8,128)(2,1)S(1)}, bf16[1024,128]{1,0:T(8,128)(2,1)S(1)}, u32[]{:S(2)}, u32[]{:S(2)}) collective-permute-start(bf16[1024,128]{1,0:T(8,128)(2,1)S(1)} %collective-permute-done.3.refs_6_), channel_id=1, source_target_pairs={{0,8},{8,16},{16,24},{24,32},{32,40},{40,48},{48,56},{56,0},{64,72... | collective-permute-start | bytes 786440 | tf_op jit(solution)/shard_map/ppermute | solution.py:27
  27.4 7.6 %collective-permute-start.6 = (bf16[1024,128]{1,0:T(8,128)(2,1)S(1)}, bf16[1024,128]{1,0:T(8,128)(2,1)S(1)}, u32[]{:S(2)}, u32[]{:S(2)}) collective-permute-start(bf16[1024,128]{1,0:T(8,128)(2,1)S(1)} %collective-permute-done.5.refs_7_), channel_id=1, source_target_pairs={{0,56},{8,0},{16,8},{24,16},{32,24},{40,32},{48,40},{56,48},{64,12... | collective-permute-start | bytes 786440 | tf_op jit(solution)/shard_map/ppermute | solution.py:27
  35.0 11.3 %copy-start.2 = (s32[200]{0:T(256)S(1)}, s32[200]{0:T(256)}, u32[]{:S(2)}) copy-start(s32[200]{0:T(256)} %get-tuple-element.70.refs_1_) | copy-start | bytes 2404
  35.0 11.3 %collective-permute-start.9 = (bf16[1024,128]{1,0:T(8,128)(2,1)S(1)}, bf16[1024,128]{1,0:T(8,128)(2,1)S(1)}, u32[]{:S(2)}, u32[]{:S(2)}) collective-permute-start(bf16[1024,128]{1,0:T(8,128)(2,1)S(1)} %get-tuple-element.68), channel_id=1, source_target_pairs={{0,56},{8,0},{16,8},{24,16},{32,24},{40,32},{48,40},{56,48},{64,12... | collective-permute-start | bytes 786440 | tf_op jit(solution)/shard_map/ppermute | solution.py:27
  38.3 8.0 %collective-permute-start.11 = (bf16[1024,128]{1,0:T(8,128)(2,1)S(1)}, bf16[1024,128]{1,0:T(8,128)(2,1)S(1)}, u32[]{:S(2)}, u32[]{:S(2)}) collective-permute-start(bf16[1024,128]{1,0:T(8,128)(2,1)S(1)} %get-tuple-element.71), channel_id=1, source_target_pairs={{0,8},{8,16},{16,24},{24,32},{32,40},{40,48},{48,56},{56,0},{64,72... | collective-permute-start | bytes 786440 | tf_op jit(solution)/shard_map/ppermute | solution.py:27
  38.3 17.2 %collective-permute-start.10 = (bf16[512,128]{1,0:T(8,128)(2,1)S(1)}, bf16[512,128]{1,0:T(8,128)(2,1)S(1)}, u32[]{:S(2)}, u32[]{:S(2)}) collective-permute-start(bf16[512,128]{1,0:T(8,128)(2,1)S(1)} %get-tuple-element.69), channel_id=1, source_target_pairs={{0,48},{8,56},{16,0},{24,8},{32,16},{40,24},{48,32},{56,40},{64,11... | collective-permute-start | bytes 393224 | tf_op jit(solution)/shard_map/ppermute | solution.py:27
  39.9 17.0 %collective-permute-start.15 = (bf16[512,128]{1,0:T(8,128)(2,1)S(1)}, bf16[512,128]{1,0:T(8,128)(2,1)S(1)}, u32[]{:S(2)}, u32[]{:S(2)}) collective-permute-start(bf16[512,128]{1,0:T(8,128)(2,1)S(1)} %get-tuple-element.77), channel_id=1, source_target_pairs={{0,16},{8,24},{16,32},{24,40},{32,48},{40,56},{48,0},{56,8},{64,80... | collective-permute-start | bytes 393224 | tf_op jit(solution)/shard_map/ppermute | solution.py:27
  49.8 12.2 %collective-permute-start.12 = (bf16[512,128]{1,0:T(8,128)(2,1)S(1)}, bf16[512,128]{1,0:T(8,128)(2,1)S(1)}, u32[]{:S(2)}, u32[]{:S(2)}) collective-permute-start(bf16[512,128]{1,0:T(8,128)(2,1)S(1)} %get-tuple-element.74), channel_id=1, source_target_pairs={{0,40},{8,48},{16,56},{24,0},{32,8},{40,16},{48,24},{56,32},{64,10... | collective-permute-start | bytes 393224 | tf_op jit(solution)/shard_map/ppermute | solution.py:27
  49.8 12.5 %collective-permute-start.13 = (bf16[512,128]{1,0:T(8,128)(2,1)S(1)}, bf16[512,128]{1,0:T(8,128)(2,1)S(1)}, u32[]{:S(2)}, u32[]{:S(2)}) collective-permute-start(bf16[512,128]{1,0:T(8,128)(2,1)S(1)} %get-tuple-element.75), channel_id=1, source_target_pairs={{0,32},{8,40},{16,48},{24,56},{32,0},{40,8},{48,16},{56,24},{64,96... | collective-permute-start | bytes 393224 | tf_op jit(solution)/shard_map/ppermute | solution.py:27
  53.4 12.2 %collective-permute-start.14 = (bf16[512,128]{1,0:T(8,128)(2,1)S(1)}, bf16[512,128]{1,0:T(8,128)(2,1)S(1)}, u32[]{:S(2)}, u32[]{:S(2)}) collective-permute-start(bf16[512,128]{1,0:T(8,128)(2,1)S(1)} %get-tuple-element.76), channel_id=1, source_target_pairs={{0,24},{8,32},{16,40},{24,48},{32,56},{40,0},{48,8},{56,16},{64,88... | collective-permute-start | bytes 393224 | tf_op jit(solution)/shard_map/ppermute | solution.py:27
  55.6 10.8 %collective-permute-start.16 = (bf16[1024,128]{1,0:T(8,128)(2,1)S(1)}, bf16[1024,128]{1,0:T(8,128)(2,1)S(1)}, u32[]{:S(2)}, u32[]{:S(2)}) collective-permute-start(bf16[1024,128]{1,0:T(8,128)(2,1)S(1)} %get-tuple-element.79), channel_id=1, source_target_pairs={{0,128},{8,136},{16,144},{24,152},{32,160},{40,168},{48,176},{56,1... | collective-permute-start | bytes 786440 | tf_op jit(solution)/shard_map/ppermute | solution.py:32
  56.8 9.6 %collective-permute-start.17 = (bf16[1024,128]{1,0:T(8,128)(2,1)S(1)}, bf16[1024,128]{1,0:T(8,128)(2,1)S(1)}, u32[]{:S(2)}, u32[]{:S(2)}) collective-permute-start(bf16[1024,128]{1,0:T(8,128)(2,1)S(1)} %get-tuple-element.80), channel_id=1, source_target_pairs={{0,192},{8,200},{16,208},{24,216},{32,224},{40,232},{48,240},{56,2... | collective-permute-start | bytes 786440 | tf_op jit(solution)/shard_map/ppermute | solution.py:32
  61.9 7.6 %collective-permute-start.18 = (bf16[1024,128]{1,0:T(8,128)(2,1)S(1)}, bf16[1024,128]{1,0:T(8,128)(2,1)S(1)}, u32[]{:S(2)}, u32[]{:S(2)}) collective-permute-start(bf16[1024,128]{1,0:T(8,128)(2,1)S(1)} %get-tuple-element.81), channel_id=1, source_target_pairs={{0,64},{8,72},{16,80},{24,88},{32,96},{40,104},{48,112},{56,120},{... | collective-permute-start | bytes 786440 | tf_op jit(solution)/shard_map/ppermute | solution.py:32

commit v5 on v4

--- a/solution.py
+++ b/solution.py
@@ -288,8 +288,13 @@
                 back[s] = dq if s == 0 else z_shift(dq, -s)
     own_k, own_v = acc[0], acc[1]
     query_grad = sum(back[s].astype(f32) for s in range(NZ)) * scale
-    key_grad = own_k + sum(p[:rows].astype(f32) for p in kv_back) * scale
-    value_grad = own_v + sum(p[rows:].astype(f32) for p in kv_back)
+    early = (
+        own_k + sum(p[:rows].astype(f32) for p in kv_back[:-1]) * scale,
+        own_v + sum(p[rows:].astype(f32) for p in kv_back[:-1]),
+    )
+    early_k, early_v = lax.optimization_barrier(early)
+    key_grad = early_k + kv_back[-1][:rows].astype(f32) * scale
+    value_grad = early_v + kv_back[-1][rows:].astype(f32)
     return query_grad, key_grad, value_grad
 
 

time: 70.3 us -> 69.8 us (level)
  starting transfers between devices: 33 us -> 34.4 us
  waiting for transfers between devices: 22.2 us -> 21 us
    ppermute x13, starting transfers between devices: 24.4 us -> 25.8 us  [z_shift(): return lax.ppermute(a, 'seq', route)]
    ppermute x13, waiting for transfers between devices: 18.3 us -> 17.5 us  [z_shift(): return lax.ppermute(a, 'seq', route)]
    pallas_call x2, Pallas kernels: 6.69 us -> 5.96 us  [run_pairs(): pl.pallas_call(functools.partial(pairs_kernel, g, first, last, row_parts)...]
  transfers between devices with their start and end apart: 19 -> 19, of which waited for: 10 -> 9; matrix products, arithmetic and copies ran while one was open for 1% -> 1% of each run, Pallas kernels for 16% -> 15%
where the time goes in v5:
time: 69.8 us; the launch traced here: 69.7 us
  starting transfers between devices  34.4 us (49%)
  waiting for transfers between devices  21 us (30%)
  Pallas kernels  12 us (17%)
  other arithmetic  1.75 us (3%)
  between operations  0.71 us (1%)
    ppermute x13, starting transfers between devices, z_shift(): return lax.ppermute(a, 'seq', route)  25.8 us
    ppermute x13, waiting for transfers between devices, z_shift(): return lax.ppermute(a, 'seq', route)  17.5 us
    ppermute x6, starting transfers between devices, y_shift(): return lax.ppermute(a, 'seq', route)  8.52 us
    pallas_call x2, Pallas kernels, run_pairs(): pl.pallas_call(functools.partial(pairs_kernel, g, first, last, row_parts)...  5.96 us
    pallas_call x1, Pallas kernels, make_plan(): pl.pallas_call(plan_kernel, out_shape=[pltpu.VMEM((BLK + 8, BLK), f32), j...  4.82 us
    ppermute x6, waiting for transfers between devices, y_shift(): return lax.ppermute(a, 'seq', route)  3.47 us
  transfers between devices with their start and end apart: 19, of which 9 were waited for; matrix products, arithmetic and copies ran while one was open for 1% of the time, Pallas kernels for 15%

profile of v5, /device:TPU:2, one launch (start us, length us, event | category | flops | bytes accessed | tf_op | source)
XLA Modules:
  0.0 69.7 jit_solution(5838023723962370446)
XLA Ops:
  0.6 1.1 %shard_map.85 = (bf16[1024,128]{1,0:T(8,128)(2,1)S(1)}, bf16[1024,128]{1,0:T(8,128)(2,1)S(1)}) custom-call(bf16[512,128]{1,0:T(8,128)(2,1)} %a_ref.1, bf16[512,128]{1,0:T(8,128)(2,1)} %b_ref.1, bf16[512,128]{1,0:T(8,128)(2,1)} %c_ref.1, bf16[512,128]{1,0:T(8,128)(2,1)} %d_ref.1), custom_call_target="tpu_custom_call" | custom-call | bytes 1000000 | tf_op jit(solution)/shard_map/pallas_call | solution.py:87
  1.8 3.3 %collective-permute-start.2 = (bf16[1024,128]{1,0:T(8,128)(2,1)S(1)}, bf16[1024,128]{1,0:T(8,128)(2,1)S(1)}, u32[]{:S(2)}, u32[]{:S(2)}) collective-permute-start(bf16[1024,128]{1,0:T(8,128)(2,1)S(1)} %get-tuple-element.56.refs_8_.refs_7_), channel_id=1, source_target_pairs={{0,128},{8,136},{16,144},{24,152},{32,160},{40,168},{48,176},{56,1... | collective-permute-start | bytes 786440 | tf_op jit(solution)/shard_map/ppermute | solution.py:32
  5.0 5.9 %collective-permute-start.1 = (bf16[1024,128]{1,0:T(8,128)(2,1)S(1)}, bf16[1024,128]{1,0:T(8,128)(2,1)S(1)}, u32[]{:S(2)}, u32[]{:S(2)}) collective-permute-start(bf16[1024,128]{1,0:T(8,128)(2,1)S(1)} %get-tuple-element.45.refs_3_), channel_id=1, source_target_pairs={{0,56},{8,0},{16,8},{24,16},{32,24},{40,32},{48,40},{56,48},{64,12... | collective-permute-start | bytes 786440 | tf_op jit(solution)/shard_map/ppermute | solution.py:27
  10.9 0.0 collective-permute-start
  10.9 4.8 %shard_map.86 = (f32[136,128]{1,0:T(8,128)S(1)}, s32[2]{0:T(128)}, s32[328]{0:T(512)}, s32[200]{0:T(256)}) custom-call(s32[1]{0:T(128)} %bitcast.me_ref, s32[128]{0:T(128)} %order_ref.1, s32[128,128]{1,0:T(8,128)} %vmask_ref.1, s32[128,128]{1,0:T(8,128)} %vmask_ref.1), custom_call_target="tpu_custom_call" | custom-call | flops 10000 | bytes 200000 | tf_op jit(solution)/shard_map/pallas_call | solution.py:120
  15.7 0.0 collective-permute-done.2.refs_10_.refs_9_
  15.8 0.4 collective-permute-done.1.refs_5_
  16.2 3.4 %collective-permute-done.refs_4_ = bf16[1024,128]{1,0:T(8,128)(2,1)S(1)} collective-permute-done((bf16[1024,128]{1,0:T(8,128)(2,1)S(1)}, bf16[1024,128]{1,0:T(8,128)(2,1)S(1)}, u32[]{:S(2)}, u32[]{:S(2)}) %collective-permute-start) | collective-permute-done | bytes 262176 | tf_op jit(solution)/shard_map/ppermute | solution.py:27
  19.6 0.0 copy-start
  19.6 0.0 copy-start.1
  19.6 0.0 collective-permute-start.3
  19.6 3.2 %collective-permute-start.5 = (bf16[1024,128]{1,0:T(8,128)(2,1)S(1)}, bf16[1024,128]{1,0:T(8,128)(2,1)S(1)}, u32[]{:S(2)}, u32[]{:S(2)}) collective-permute-start(bf16[1024,128]{1,0:T(8,128)(2,1)S(1)} %collective-permute-done.1.refs_5_), channel_id=1, source_target_pairs={{0,56},{8,0},{16,8},{24,16},{32,24},{40,32},{48,40},{56,48},{64,12... | collective-permute-start | bytes 786440 | tf_op jit(solution)/shard_map/ppermute | solution.py:27
  22.8 1.1 %collective-permute-start.8 = (bf16[1024,128]{1,0:T(8,128)(2,1)S(1)}, bf16[1024,128]{1,0:T(8,128)(2,1)S(1)}, u32[]{:S(2)}, u32[]{:S(2)}) collective-permute-start(bf16[1024,128]{1,0:T(8,128)(2,1)S(1)} %get-tuple-element.56.refs_8_.refs_7_), channel_id=1, source_target_pairs={{0,192},{8,200},{16,208},{24,216},{32,224},{40,232},{48,240},{56,2... | collective-permute-start | bytes 786440 | tf_op jit(solution)/shard_map/ppermute | solution.py:32
  23.9 1.0 %collective-permute-start.7 = (bf16[1024,128]{1,0:T(8,128)(2,1)S(1)}, bf16[1024,128]{1,0:T(8,128)(2,1)S(1)}, u32[]{:S(2)}, u32[]{:S(2)}) collective-permute-start(bf16[1024,128]{1,0:T(8,128)(2,1)S(1)} %get-tuple-element.56.refs_8_.refs_7_), channel_id=1, source_target_pairs={{0,64},{8,72},{16,80},{24,88},{32,96},{40,104},{48,112},{56,120},{... | collective-permute-start | bytes 786440 | tf_op jit(solution)/shard_map/ppermute | solution.py:32
  24.9 2.5 %collective-permute-done.3.refs_6_ = bf16[1024,128]{1,0:T(8,128)(2,1)S(1)} collective-permute-done((bf16[1024,128]{1,0:T(8,128)(2,1)S(1)}, bf16[1024,128]{1,0:T(8,128)(2,1)S(1)}, u32[]{:S(2)}, u32[]{:S(2)}) %collective-permute-start.3) | collective-permute-done | bytes 262176 | tf_op jit(solution)/shard_map/ppermute | solution.py:27
  27.4 0.0 collective-permute-start.4
  27.4 0.0 collective-permute-done.5.refs_7_
  27.4 3.2 %collective-permute-start.6 = (bf16[1024,128]{1,0:T(8,128)(2,1)S(1)}, bf16[1024,128]{1,0:T(8,128)(2,1)S(1)}, u32[]{:S(2)}, u32[]{:S(2)}) collective-permute-start(bf16[1024,128]{1,0:T(8,128)(2,1)S(1)} %collective-permute-done.5.refs_7_), channel_id=1, source_target_pairs={{0,56},{8,0},{16,8},{24,16},{32,24},{40,32},{48,40},{56,48},{64,12... | collective-permute-start | bytes 786440 | tf_op jit(solution)/shard_map/ppermute | solution.py:27
  30.6 0.0 collective-permute-done.8.refs_11_.refs_10_
  30.6 0.9 %collective-permute-done.7.refs_9_.refs_8_ = bf16[1024,128]{1,0:T(8,128)(2,1)S(1)} collective-permute-done((bf16[1024,128]{1,0:T(8,128)(2,1)S(1)}, bf16[1024,128]{1,0:T(8,128)(2,1)S(1)}, u32[]{:S(2)}, u32[]{:S(2)}) %collective-permute-start.7) | collective-permute-done | bytes 262176 | tf_op jit(solution)/shard_map/ppermute | solution.py:32
  31.5 0.0 copy-done
  31.5 0.0 copy-done.1
  31.5 3.2 %shard_map.87 = (f32[512,128]{1,0:T(8,128)S(1)}, bf16[512,128]{1,0:T(8,128)(2,1)S(1)}, bf16[512,128]{1,0:T(8,128)(2,1)S(1)}, bf16[512,128]{1,0:T(8,128)(2,1)S(1)...) custom-call(s32[2]{0:T(128)S(1)} %copy-done.1, s32[328]{0:T(512)S(1)} %copy-done, ...), custom_call_target="tpu_custom_call" | custom-call | flops 419430400 | bytes 4000000 | tf_op jit(solution)/shard_map/pallas_call | solution.py:241
  34.7 0.2 collective-permute-done.4.ahead_ref.refs_3_
  35.0 0.0 collective-permute-done.6.behind_ref.refs_4_
  35.0 0.0 copy-start.2
  35.0 3.3 %collective-permute-start.9 = (bf16[1024,128]{1,0:T(8,128)(2,1)S(1)}, bf16[1024,128]{1,0:T(8,128)(2,1)S(1)}, u32[]{:S(2)}, u32[]{:S(2)}) collective-permute-start(bf16[1024,128]{1,0:T(8,128)(2,1)S(1)} %get-tuple-element.70), channel_id=1, source_target_pairs={{0,56},{8,0},{16,8},{24,16},{32,24},{40,32},{48,40},{56,48},{64,12... | collective-permute-start | bytes 786440 | tf_op jit(solution)/shard_map/ppermute | solution.py:27
  38.3 0.0 collective-permute-start.11
  38.3 1.5 %collective-permute-start.10 = (bf16[512,128]{1,0:T(8,128)(2,1)S(1)}, bf16[512,128]{1,0:T(8,128)(2,1)S(1)}, u32[]{:S(2)}, u32[]{:S(2)}) collective-permute-start(bf16[512,128]{1,0:T(8,128)(2,1)S(1)} %get-tuple-element.71), channel_id=1, source_target_pairs={{0,48},{8,56},{16,0},{24,8},{32,16},{40,24},{48,32},{56,40},{64,11... | collective-permute-start | bytes 393224 | tf_op jit(solution)/shard_map/ppermute | solution.py:27
  39.9 1.4 %collective-permute-start.15 = (bf16[512,128]{1,0:T(8,128)(2,1)S(1)}, bf16[512,128]{1,0:T(8,128)(2,1)S(1)}, u32[]{:S(2)}, u32[]{:S(2)}) collective-permute-start(bf16[512,128]{1,0:T(8,128)(2,1)S(1)} %get-tuple-element.79), channel_id=1, source_target_pairs={{0,16},{8,24},{16,32},{24,40},{32,48},{40,56},{48,0},{56,8},{64,80... | collective-permute-start | bytes 393224 | tf_op jit(solution)/shard_map/ppermute | solution.py:27
  41.3 5.0 %collective-permute-done.9.refs_6_ = bf16[1024,128]{1,0:T(8,128)(2,1)S(1)} collective-permute-done((bf16[1024,128]{1,0:T(8,128)(2,1)S(1)}, bf16[1024,128]{1,0:T(8,128)(2,1)S(1)}, u32[]{:S(2)}, u32[]{:S(2)}) %collective-permute-start.9) | collective-permute-done | bytes 262176 | tf_op jit(solution)/shard_map/ppermute | solution.py:27
  46.3 0.0 collective-permute-done.11.refs_5_
  46.3 0.0 copy-done.2
  46.3 2.7 %shard_map.89 = (bf16[512,128]{1,0:T(8,128)(2,1)S(1)}, bf16[512,128]{1,0:T(8,128)(2,1)S(1)}, bf16[512,128]{1,0:T(8,128)(2,1)S(1)}, f32[512,128]{1,0:T(8,128)S(1)...) custom-call(s32[2]{0:T(128)S(1)} %copy-done.1, ...), custom_call_target="tpu_custom_call" | custom-call | flops 251658240 | bytes 4000000 | tf_op jit(solution)/shard_map/pallas_call | solution.py:241
  49.0 0.2 collective-permute-start.12
  49.3 3.4 %collective-permute-start.13 = (bf16[512,128]{1,0:T(8,128)(2,1)S(1)}, bf16[512,128]{1,0:T(8,128)(2,1)S(1)}, u32[]{:S(2)}, u32[]{:S(2)}) collective-permute-start(bf16[512,128]{1,0:T(8,128)(2,1)S(1)} %get-tuple-element.77), channel_id=1, source_target_pairs={{0,32},{8,40},{16,48},{24,56},{32,0},{40,8},{48,16},{56,24},{64,96... | collective-permute-start | bytes 393224 | tf_op jit(solution)/shard_map/ppermute | solution.py:27
  52.7 3.6 %collective-permute-start.14 = (bf16[512,128]{1,0:T(8,128)(2,1)S(1)}, bf16[512,128]{1,0:T(8,128)(2,1)S(1)}, u32[]{:S(2)}, u32[]{:S(2)}) collective-permute-start(bf16[512,128]{1,0:T(8,128)(2,1)S(1)} %get-tuple-element.78), channel_id=1, source_target_pairs={{0,24},{8,32},{16,40},{24,48},{32,56},{40,0},{48,8},{56,16},{64,88... | collective-permute-start | bytes 393224 | tf_op jit(solution)/shard_map/ppermute | solution.py:27
  56.3 0.0 collective-permute-done.10
  56.3 0.0 collective-permute-start.16
  56.3 0.0 collective-permute-done.15
  56.3 2.6 %collective-permute-start.17 = (bf16[1024,128]{1,0:T(8,128)(2,1)S(1)}, bf16[1024,128]{1,0:T(8,128)(2,1)S(1)}, u32[]{:S(2)}, u32[]{:S(2)}) collective-permute-start(bf16[1024,128]{1,0:T(8,128)(2,1)S(1)} %get-tuple-element.82), channel_id=1, source_target_pairs={{0,192},{8,200},{16,208},{24,216},{32,224},{40,232},{48,240},{56,2... | collective-permute-start | bytes 786440 | tf_op jit(solution)/shard_map/ppermute | solution.py:32
  58.9 2.4 %collective-permute-done.12 = bf16[512,128]{1,0:T(8,128)(2,1)S(1)} collective-permute-done((bf16[512,128]{1,0:T(8,128)(2,1)S(1)}, bf16[512,128]{1,0:T(8,128)(2,1)S(1)}, u32[]{:S(2)}, u32[]{:S(2)}) %collective-permute-start.12) | collective-permute-done | bytes 131104 | tf_op jit(solution)/shard_map/ppermute | solution.py:27
  61.3 0.6 collective-permute-start.18
  61.9 0.0 collective-permute-done.13
  61.9 3.5 %collective-permute-done.14 = bf16[512,128]{1,0:T(8,128)(2,1)S(1)} collective-permute-done((bf16[512,128]{1,0:T(8,128)(2,1)S(1)}, bf16[512,128]{1,0:T(8,128)(2,1)S(1)}, u32[]{:S(2)}, u32[]{:S(2)}) %collective-permute-start.14) | collective-permute-done | bytes 131104 | tf_op jit(solution)/shard_map/ppermute | solution.py:27
  65.4 0.8 %add_multiply_fusion = f32[512,128]{1,0:T(8,128)} fusion(bf16[512,128]{1,0:T(8,128)(2,1)S(1)} %collective-permute-done.15, bf16[512,128]{1,0:T(8,128)(2,1)S(1)} %collective-permute-done.14, bf16[512,128]{1,0:T(8,128)(2,1)S(1)} %collective-permute-done.13, bf16[512,128]{1,0:T(8,128)(2,1)S(1)} %collective-permute-done.12, ...), kind=kLoop, calls=%fused_computation.4 | loop fusion | flops 983040 | bytes 1441792 | tf_op jit(solution)/shard_map/mul | solution.py:290
  66.2 0.0 collective-permute-done.16
  66.2 0.0 collective-permute-done.17
  66.2 0.1 add_add_fusion
  66.3 2.6 %collective-permute-done.18 = bf16[1024,128]{1,0:T(8,128)(2,1)S(1)} collective-permute-done((bf16[1024,128]{1,0:T(8,128)(2,1)S(1)}, bf16[1024,128]{1,0:T(8,128)(2,1)S(1)}, u32[]{:S(2)}, u32[]{:S(2)}) %collective-permute-start.18) | collective-permute-done | bytes 262176 | tf_op jit(solution)/shard_map/ppermute | solution.py:32
  68.9 0.8 %convert_add_fusion = (f32[512,128]{1,0:T(8,128)}, f32[512,128]{1,0:T(8,128)}) fusion(f32[512,128]{1,0:T(8,128)S(1)} %get-tuple-element.86, bf16[1024,128]{1,0:T(8,128)(2,1)S(1)} %collective-permute-done.18, f32[512,128]{1,0:T(8,128)S(1)} %get-tuple-element.84), kind=kLoop, calls=%fused_computation | loop fusion | flops 327680 | bytes 1310720 | tf_op jit(solution)/shard_map/add | solution.py:297
  (1 shorter events, 0.0 us)
Async XLA Ops:
  1.8 14.0 %collective-permute-start.2 = (bf16[1024,128]{1,0:T(8,128)(2,1)S(1)}, bf16[1024,128]{1,0:T(8,128)(2,1)S(1)}, u32[]{:S(2)}, u32[]{:S(2)}) collective-permute-start(bf16[1024,128]{1,0:T(8,128)(2,1)S(1)} %get-tuple-element.56.refs_8_.refs_7_), channel_id=1, source_target_pairs={{0,128},{8,136},{16,144},{24,152},{32,160},{40,168},{48,176},{56,1... | collective-permute-start | bytes 786440 | tf_op jit(solution)/shard_map/ppermute | solution.py:32
  5.0 11.1 %collective-permute-start.1 = (bf16[1024,128]{1,0:T(8,128)(2,1)S(1)}, bf16[1024,128]{1,0:T(8,128)(2,1)S(1)}, u32[]{:S(2)}, u32[]{:S(2)}) collective-permute-start(bf16[1024,128]{1,0:T(8,128)(2,1)S(1)} %get-tuple-element.45.refs_3_), channel_id=1, source_target_pairs={{0,56},{8,0},{16,8},{24,16},{32,24},{40,32},{48,40},{56,48},{64,12... | collective-permute-start | bytes 786440 | tf_op jit(solution)/shard_map/ppermute | solution.py:27
  10.9 8.7 %collective-permute-start = (bf16[1024,128]{1,0:T(8,128)(2,1)S(1)}, bf16[1024,128]{1,0:T(8,128)(2,1)S(1)}, u32[]{:S(2)}, u32[]{:S(2)}) collective-permute-start(bf16[1024,128]{1,0:T(8,128)(2,1)S(1)} %get-tuple-element.45.refs_3_), channel_id=1, source_target_pairs={{0,8},{8,16},{16,24},{24,32},{32,40},{40,48},{48,56},{56,0},{64,72... | collective-permute-start | bytes 786440 | tf_op jit(solution)/shard_map/ppermute | solution.py:27
  19.6 11.9 %copy-start = (s32[328]{0:T(512)S(1)}, s32[328]{0:T(512)}, u32[]{:S(2)}) copy-start(s32[328]{0:T(512)} %get-tuple-element.54.refs_1_) | copy-start | bytes 3940
  19.6 11.9 %copy-start.1 = (s32[2]{0:T(128)S(1)}, s32[2]{0:T(128)}, u32[]{:S(2)}) copy-start(s32[2]{0:T(128)} %get-tuple-element.53.refs_0_) | copy-start | bytes 28
  19.6 7.8 %collective-permute-start.3 = (bf16[1024,128]{1,0:T(8,128)(2,1)S(1)}, bf16[1024,128]{1,0:T(8,128)(2,1)S(1)}, u32[]{:S(2)}, u32[]{:S(2)}) collective-permute-start(bf16[1024,128]{1,0:T(8,128)(2,1)S(1)} %collective-permute-done.refs_4_), channel_id=1, source_target_pairs={{0,8},{8,16},{16,24},{24,32},{32,40},{40,48},{48,56},{56,0},{64,72... | collective-permute-start | bytes 786440 | tf_op jit(solution)/shard_map/ppermute | solution.py:27
  19.6 7.8 %collective-permute-start.5 = (bf16[1024,128]{1,0:T(8,128)(2,1)S(1)}, bf16[1024,128]{1,0:T(8,128)(2,1)S(1)}, u32[]{:S(2)}, u32[]{:S(2)}) collective-permute-start(bf16[1024,128]{1,0:T(8,128)(2,1)S(1)} %collective-permute-done.1.refs_5_), channel_id=1, source_target_pairs={{0,56},{8,0},{16,8},{24,16},{32,24},{40,32},{48,40},{56,48},{64,12... | collective-permute-start | bytes 786440 | tf_op jit(solution)/shard_map/ppermute | solution.py:27
  22.8 7.8 %collective-permute-start.8 = (bf16[1024,128]{1,0:T(8,128)(2,1)S(1)}, bf16[1024,128]{1,0:T(8,128)(2,1)S(1)}, u32[]{:S(2)}, u32[]{:S(2)}) collective-permute-start(bf16[1024,128]{1,0:T(8,128)(2,1)S(1)} %get-tuple-element.56.refs_8_.refs_7_), channel_id=1, source_target_pairs={{0,192},{8,200},{16,208},{24,216},{32,224},{40,232},{48,240},{56,2... | collective-permute-start | bytes 786440 | tf_op jit(solution)/shard_map/ppermute | solution.py:32
  23.9 7.6 %collective-permute-start.7 = (bf16[1024,128]{1,0:T(8,128)(2,1)S(1)}, bf16[1024,128]{1,0:T(8,128)(2,1)S(1)}, u32[]{:S(2)}, u32[]{:S(2)}) collective-permute-start(bf16[1024,128]{1,0:T(8,128)(2,1)S(1)} %get-tuple-element.56.refs_8_.refs_7_), channel_id=1, source_target_pairs={{0,64},{8,72},{16,80},{24,88},{32,96},{40,104},{48,112},{56,120},{... | collective-permute-start | bytes 786440 | tf_op jit(solution)/shard_map/ppermute | solution.py:32
  27.4 7.6 %collective-permute-start.4 = (bf16[1024,128]{1,0:T(8,128)(2,1)S(1)}, bf16[1024,128]{1,0:T(8,128)(2,1)S(1)}, u32[]{:S(2)}, u32[]{:S(2)}) collective-permute-start(bf16[1024,128]{1,0:T(8,128)(2,1)S(1)} %collective-permute-done.3.refs_6_), channel_id=1, source_target_pairs={{0,8},{8,16},{16,24},{24,32},{32,40},{40,48},{48,56},{56,0},{64,72... | collective-permute-start | bytes 786440 | tf_op jit(solution)/shard_map/ppermute | solution.py:27
  27.4 7.6 %collective-permute-start.6 = (bf16[1024,128]{1,0:T(8,128)(2,1)S(1)}, bf16[1024,128]{1,0:T(8,128)(2,1)S(1)}, u32[]{:S(2)}, u32[]{:S(2)}) collective-permute-start(bf16[1024,128]{1,0:T(8,128)(2,1)S(1)} %collective-permute-done.5.refs_7_), channel_id=1, source_target_pairs={{0,56},{8,0},{16,8},{24,16},{32,24},{40,32},{48,40},{56,48},{64,12... | collective-permute-start | bytes 786440 | tf_op jit(solution)/shard_map/ppermute | solution.py:27
  35.0 11.3 %copy-start.2 = (s32[200]{0:T(256)S(1)}, s32[200]{0:T(256)}, u32[]{:S(2)}) copy-start(s32[200]{0:T(256)} %get-tuple-element.72.refs_1_) | copy-start | bytes 2404
  35.0 11.3 %collective-permute-start.9 = (bf16[1024,128]{1,0:T(8,128)(2,1)S(1)}, bf16[1024,128]{1,0:T(8,128)(2,1)S(1)}, u32[]{:S(2)}, u32[]{:S(2)}) collective-permute-start(bf16[1024,128]{1,0:T(8,128)(2,1)S(1)} %get-tuple-element.70), channel_id=1, source_target_pairs={{0,56},{8,0},{16,8},{24,16},{32,24},{40,32},{48,40},{56,48},{64,12... | collective-permute-start | bytes 786440 | tf_op jit(solution)/shard_map/ppermute | solution.py:27
  38.3 8.0 %collective-permute-start.11 = (bf16[1024,128]{1,0:T(8,128)(2,1)S(1)}, bf16[1024,128]{1,0:T(8,128)(2,1)S(1)}, u32[]{:S(2)}, u32[]{:S(2)}) collective-permute-start(bf16[1024,128]{1,0:T(8,128)(2,1)S(1)} %get-tuple-element.73), channel_id=1, source_target_pairs={{0,8},{8,16},{16,24},{24,32},{32,40},{40,48},{48,56},{56,0},{64,72... | collective-permute-start | bytes 786440 | tf_op jit(solution)/shard_map/ppermute | solution.py:27
  38.3 18.0 %collective-permute-start.10 = (bf16[512,128]{1,0:T(8,128)(2,1)S(1)}, bf16[512,128]{1,0:T(8,128)(2,1)S(1)}, u32[]{:S(2)}, u32[]{:S(2)}) collective-permute-start(bf16[512,128]{1,0:T(8,128)(2,1)S(1)} %get-tuple-element.71), channel_id=1, source_target_pairs={{0,48},{8,56},{16,0},{24,8},{32,16},{40,24},{48,32},{56,40},{64,11... | collective-permute-start | bytes 393224 | tf_op jit(solution)/shard_map/ppermute | solution.py:27
  39.9 16.4 %collective-permute-start.15 = (bf16[512,128]{1,0:T(8,128)(2,1)S(1)}, bf16[512,128]{1,0:T(8,128)(2,1)S(1)}, u32[]{:S(2)}, u32[]{:S(2)}) collective-permute-start(bf16[512,128]{1,0:T(8,128)(2,1)S(1)} %get-tuple-element.79), channel_id=1, source_target_pairs={{0,16},{8,24},{16,32},{24,40},{32,48},{40,56},{48,0},{56,8},{64,80... | collective-permute-start | bytes 393224 | tf_op jit(solution)/shard_map/ppermute | solution.py:27
  49.0 12.3 %collective-permute-start.12 = (bf16[512,128]{1,0:T(8,128)(2,1)S(1)}, bf16[512,128]{1,0:T(8,128)(2,1)S(1)}, u32[]{:S(2)}, u32[]{:S(2)}) collective-permute-start(bf16[512,128]{1,0:T(8,128)(2,1)S(1)} %get-tuple-element.76), channel_id=1, source_target_pairs={{0,40},{8,48},{16,56},{24,0},{32,8},{40,16},{48,24},{56,32},{64,10... | collective-permute-start | bytes 393224 | tf_op jit(solution)/shard_map/ppermute | solution.py:27
  49.3 12.7 %collective-permute-start.13 = (bf16[512,128]{1,0:T(8,128)(2,1)S(1)}, bf16[512,128]{1,0:T(8,128)(2,1)S(1)}, u32[]{:S(2)}, u32[]{:S(2)}) collective-permute-start(bf16[512,128]{1,0:T(8,128)(2,1)S(1)} %get-tuple-element.77), channel_id=1, source_target_pairs={{0,32},{8,40},{16,48},{24,56},{32,0},{40,8},{48,16},{56,24},{64,96... | collective-permute-start | bytes 393224 | tf_op jit(solution)/shard_map/ppermute | solution.py:27
  52.7 12.7 %collective-permute-start.14 = (bf16[512,128]{1,0:T(8,128)(2,1)S(1)}, bf16[512,128]{1,0:T(8,128)(2,1)S(1)}, u32[]{:S(2)}, u32[]{:S(2)}) collective-permute-start(bf16[512,128]{1,0:T(8,128)(2,1)S(1)} %get-tuple-element.78), channel_id=1, source_target_pairs={{0,24},{8,32},{16,40},{24,48},{32,56},{40,0},{48,8},{56,16},{64,88... | collective-permute-start | bytes 393224 | tf_op jit(solution)/shard_map/ppermute | solution.py:27
  56.3 9.9 %collective-permute-start.16 = (bf16[1024,128]{1,0:T(8,128)(2,1)S(1)}, bf16[1024,128]{1,0:T(8,128)(2,1)S(1)}, u32[]{:S(2)}, u32[]{:S(2)}) collective-permute-start(bf16[1024,128]{1,0:T(8,128)(2,1)S(1)} %get-tuple-element.81), channel_id=1, source_target_pairs={{0,128},{8,136},{16,144},{24,152},{32,160},{40,168},{48,176},{56,1... | collective-permute-start | bytes 786440 | tf_op jit(solution)/shard_map/ppermute | solution.py:32
  56.3 9.9 %collective-permute-start.17 = (bf16[1024,128]{1,0:T(8,128)(2,1)S(1)}, bf16[1024,128]{1,0:T(8,128)(2,1)S(1)}, u32[]{:S(2)}, u32[]{:S(2)}) collective-permute-start(bf16[1024,128]{1,0:T(8,128)(2,1)S(1)} %get-tuple-element.82), channel_id=1, source_target_pairs={{0,192},{8,200},{16,208},{24,216},{32,224},{40,232},{48,240},{56,2... | collective-permute-start | bytes 786440 | tf_op jit(solution)/shard_map/ppermute | solution.py:32
  61.3 7.6 %collective-permute-start.18 = (bf16[1024,128]{1,0:T(8,128)(2,1)S(1)}, bf16[1024,128]{1,0:T(8,128)(2,1)S(1)}, u32[]{:S(2)}, u32[]{:S(2)}) collective-permute-start(bf16[1024,128]{1,0:T(8,128)(2,1)S(1)} %get-tuple-element.85), channel_id=1, source_target_pairs={{0,64},{8,72},{16,80},{24,88},{32,96},{40,104},{48,112},{56,120},{... | collective-permute-start | bytes 786440 | tf_op jit(solution)/shard_map/ppermute | solution.py:32
